TPU v7x, 512 devices: a whole 4x8x8 slice. The times are simulated.
512 devices in a mesh: inst: 16 (over z, core), sp: 32 (over x, y).
Axes of the slice: x: 4, y: 8, z: 8, core: 2. Of those that a mesh axis runs over, the one named last changes fastest.
Arguments:
- prompt_queries: bfloat16 [16, 768, 4096], P('inst', None, 'sp')
- prompt_keys: bfloat16 [16, 768, 512], P('inst', 'sp')
- prompt_values: bfloat16 [16, 768, 512], P('inst', 'sp'), may hold values from -6 to 6
- span_of: int32 [16], replicated, may hold values from 0 to 15, each once
- short_queries: bfloat16 [16, 512, 4096], P('inst', None, 'sp')
- short_keys: bfloat16 [16, 512, 512], P('inst', 'sp')
- short_values: bfloat16 [16, 512, 512], P('inst', 'sp'), may hold values from -6 to 6
- short_lengths: int32 [16, 8], replicated, may hold values from 1 to 128, 512 in all within a row
- pair_partner: int32 [16], replicated, may hold values from 0 to 15, as said below
Outputs:
- prompt_out: bfloat16 [16, 768, 4096], P('inst', None, 'sp')
- short_out: bfloat16 [16, 512, 4096], P('inst', None, 'sp')
Inputs may be any that keep to these rules, and one draw needn't show every extreme that they name: pair_partner is a permutation of the groups. `short_lengths`: each group's lengths sum to 512.
All inputs are finite; a program needn't handle non-finite values.
Results may differ from a plain program's by a relative error of at most 0.006.
Values may be sent and summed in bfloat16 or wider, within the bound.
No kernel may reach another device: no remote copies, remote signals or barrier semaphores. Data moves between devices by JAX's collectives and lax.ppermute only.
A program may use at most 64 MiB of HBM per device.

v0:
```python
import jax
import jax.numpy as jnp
from jax import lax
from jax.sharding import PartitionSpec as P

DH = 128
QH = 32
KVH = 4


def passed_along(block, axis, distance):
    devices = range(lax.axis_size(axis))
    route = [((i - distance) % len(devices), i) for i in devices]
    return lax.ppermute(block, axis, route)


def absorb(state, q_rows, key_block, value_block, visible):
    running_max, running_sum, accumulated = state
    scores = jnp.einsum(
        "rhd,kd->hrk", q_rows, key_block, preferred_element_type=jnp.float32
    ) * DH ** (-0.5)
    scores = jnp.where(visible[None], scores, -jnp.inf)
    new_max = jnp.maximum(running_max, jnp.max(scores, axis=2))
    weights = jnp.exp(scores - new_max[:, :, None])
    factor = jnp.exp(running_max - new_max)
    running_sum = running_sum * factor + jnp.sum(weights, axis=2)
    accumulated = accumulated * factor[:, :, None] + jnp.einsum(
        "hrk,kd->hrd", weights.astype(jnp.bfloat16), value_block, preferred_element_type=jnp.float32
    )
    return (new_max, running_sum, accumulated)


def empty_state(local_heads, row_count):
    return (
        jnp.full((local_heads, row_count), -jnp.inf, jnp.float32),
        jnp.zeros((local_heads, row_count), jnp.float32),
        jnp.zeros((local_heads, row_count, DH), jnp.float32),
    )


def finish(state, row_count, local_heads):
    running_max, running_sum, accumulated = state
    result = accumulated / running_sum[:, :, None]
    return result.transpose(1, 0, 2).reshape(1, row_count, local_heads * DH).astype(jnp.bfloat16)


def body(
    prompt_queries,
    prompt_keys,
    prompt_values,
    span_of,
    short_queries,
    short_keys,
    short_values,
    short_lengths,
    pair_partner,
):
    inst_count = lax.axis_size("inst")
    inst_index = lax.axis_index("inst")
    local_heads = prompt_queries.shape[2] // DH
    kv_head = lax.axis_index("sp") * local_heads // (QH // KVH)
    span_rows = prompt_queries.shape[1]
    queries = prompt_queries[0].reshape(span_rows, local_heads, DH)
    keys_group, values_group = (
        lax.all_gather(prompt_keys, "sp", axis=1, tiled=True),
        lax.all_gather(prompt_values, "sp", axis=1, tiled=True),
    )
    own_keys = lax.dynamic_slice_in_dim(keys_group[0], kv_head * DH, DH, 1)
    own_values = lax.dynamic_slice_in_dim(values_group[0], kv_head * DH, DH, 1)
    my_span = span_of[inst_index]
    row_ids = jnp.arange(span_rows, dtype=jnp.int32)

    def visible_for(key_span):
        return key_span * span_rows + row_ids[None, :] <= my_span * span_rows + row_ids[:, None]

    start_state = empty_state(local_heads, span_rows)
    first_state = absorb(start_state, queries, own_keys, own_values, visible_for(my_span))

    def cycle_turn(offset, carry):
        held_state, key_block, value_block = carry
        key_block, value_block = passed_along((key_block, value_block), "inst", 1)
        key_span = span_of[(inst_index - offset) % inst_count]
        held_state = lax.cond(
            key_span < my_span,
            lambda inner: absorb(inner, queries, key_block, value_block, visible_for(key_span)),
            lambda inner: inner,
            held_state,
        )
        return (held_state, key_block, value_block)

    prompt_state = lax.fori_loop(1, inst_count, cycle_turn, (first_state, own_keys, own_values))[0]
    prompt_out = finish(prompt_state, span_rows, local_heads)
    partner_now = pair_partner[inst_index]
    receivers = jnp.sum(
        (pair_partner == inst_index).astype(jnp.int32) * jnp.arange(inst_count, dtype=jnp.int32)
    )
    slot_mask = (jnp.arange(inst_count, dtype=jnp.int32) == receivers).astype(jnp.bfloat16)[
        :, None, None
    ]
    got_queries, got_keys, got_values = (
        lax.all_to_all(slot_mask * short_queries, "inst", split_axis=0, concat_axis=0, tiled=True),
        lax.all_to_all(slot_mask * short_keys, "inst", split_axis=0, concat_axis=0, tiled=True),
        lax.all_to_all(slot_mask * short_values, "inst", split_axis=0, concat_axis=0, tiled=True),
    )
    arrived = (
        lax.dynamic_slice_in_dim(got_queries, partner_now, 1, 0),
        lax.dynamic_slice_in_dim(got_keys, partner_now, 1, 0),
        lax.dynamic_slice_in_dim(got_values, partner_now, 1, 0),
    )
    moved_queries, moved_keys, moved_values = arrived
    short_rows = moved_queries.shape[1]
    keys_served, values_served = (
        lax.all_gather(moved_keys, "sp", axis=1, tiled=True),
        lax.all_gather(moved_values, "sp", axis=1, tiled=True),
    )
    served_keys = lax.dynamic_slice_in_dim(keys_served[0], kv_head * DH, DH, 1)
    served_values = lax.dynamic_slice_in_dim(values_served[0], kv_head * DH, DH, 1)
    short_ids = jnp.arange(short_rows, dtype=jnp.int32)
    seg_ends = jnp.cumsum(short_lengths[partner_now])
    seg_ids = jnp.sum((short_ids[:, None] >= seg_ends[None, :]).astype(jnp.int32), axis=1)
    short_visible = (seg_ids[:, None] == seg_ids[None, :]) & (
        short_ids[None, :] <= short_ids[:, None]
    )
    short_state = absorb(
        empty_state(local_heads, short_rows),
        moved_queries[0].reshape(short_rows, local_heads, DH),
        served_keys,
        served_values,
        short_visible,
    )
    short_out = finish(short_state, short_rows, local_heads)
    return (prompt_out, short_out)


def solution(mesh):
    placed = (
        P("inst", None, "sp"),
        P("inst", "sp", None),
        P("inst", "sp", None),
        P(),
        P("inst", None, "sp"),
        P("inst", "sp", None),
        P("inst", "sp", None),
        P(),
        P(),
    )
    return jax.shard_map(
        body,
        mesh=mesh,
        in_specs=placed,
        out_specs=(P("inst", None, "sp"), P("inst", None, "sp")),
        check_vma=False,
    )
```

profile of v0, /device:TPU:448, one launch (start us, length us, event | category | flops | bytes accessed | tf_op | source)
XLA Modules:
  0.0 411.2 jit_solution(11195329392213965728)
XLA Ops:
  4.2 12.5 %all_to_all.15 = bf16[16,16,512]{2,1,0:T(8,128)(2,1)S(1)} all-to-all(bf16[16,16,512]{2,1,0:T(8,128)(2,1)S(1)} %get-tuple-element.410), channel_id=1, replica_groups=mesh['inst'=16,'sp'=32] {'inst'}, dimensions={0} | all-to-all | bytes 524288 | tf_op jit(solution)/shard_map/all_to_all | solution.py:102
  16.6 6.5 %all-to-all-start.2 = ((bf16[16,16,512]{2,1,0:T(8,128)(2,1)}), bf16[16,16,512]{2,1,0:T(8,128)(2,1)S(1)}, u32[]{:S(2)}, u32[]{:S(2)}) async-start(bf16[16,16,512]{2,1,0:T(8,128)(2,1)} %get-tuple-element.409), calls=%async_computation.2 | async-start | bytes 524288 | tf_op jit(solution)/shard_map/all_to_all | solution.py:103
  25.6 5.7 %all-to-all-done.2 = bf16[16,16,512]{2,1,0:T(8,128)(2,1)S(1)} async-done(((bf16[16,16,512]{2,1,0:T(8,128)(2,1)}), bf16[16,16,512]{2,1,0:T(8,128)(2,1)S(1)}, u32[]{:S(2)}, u32[]{:S(2)}) %all-to-all-start.2) | async-done | bytes 262176 | tf_op jit(solution)/shard_map/all_to_all | solution.py:103
  31.3 7.5 %all-to-all-start.1 = ((bf16[16,512,128]{2,1,0:T(8,128)(2,1)}), bf16[16,512,128]{2,1,0:T(8,128)(2,1)}, u32[]{:S(2)}, u32[]{:S(2)}) async-start(bf16[16,512,128]{2,1,0:T(8,128)(2,1)} %broadcast_multiply_fusion), calls=%async_computation.1 | async-start | bytes 4194304 | tf_op jit(solution)/shard_map/all_to_all | solution.py:101
  42.2 50.9 %all_gather.12 = bf16[1,768,512]{2,1,0:T(8,128)(2,1)S(1)} all-gather(bf16[1,24,512]{2,1,0:T(8,128)(2,1)S(1)} %copy-done.2), channel_id=1, replica_groups=mesh['inst'=16,'sp'=32] {'sp'}, dimensions={1}, use_global_device_ids=true | all-gather | bytes 811008 | tf_op jit(solution)/shard_map/all_gather | solution.py:65
  96.7 48.6 %all_gather.13 = bf16[1,768,512]{2,1,0:T(8,128)(2,1)S(1)} all-gather(bf16[1,24,512]{2,1,0:T(8,128)(2,1)S(1)} %copy-done.3), channel_id=1, replica_groups=mesh['inst'=16,'sp'=32] {'sp'}, dimensions={1}, use_global_device_ids=true | all-gather | bytes 811008 | tf_op jit(solution)/shard_map/all_gather | solution.py:66
  145.9 165.7 %while.25 = (s32[]{:T(128)}, f32[1,768]{1,0:T(1,128)S(1)}, f32[1,768]{1,0:T(1,128)S(1)}, f32[1,768,128]{2,1,0:T(8,128)S(1)}, bf16[768,128]{1,0:T(8,128)(2,1)}, /...) while((s32[]{:T(128)}, f32[1,768]{1,0:T(1,128)S(1)}, ...), condition=%wide.region_7.8_spmd.clone.clone, body=%wide.region_2.7_spmd.clone.clone.sunk | while | flops 306908960 | bytes 10887730 | solution.py:91
  147.9 3.3 collective-permute-done
  158.9 3.3 collective-permute-done
  170.0 3.3 collective-permute-done
  175.4 2.9 conditional.4
  181.0 3.3 collective-permute-done
  186.4 2.9 conditional.4
  192.1 3.3 collective-permute-done
  197.5 2.9 conditional.4
  203.1 3.3 collective-permute-done
  214.2 3.3 collective-permute-done
  219.6 2.9 conditional.4
  225.2 3.3 collective-permute-done
  236.3 3.3 collective-permute-done
  241.7 2.9 conditional.4
  247.3 3.3 collective-permute-done
  258.4 3.3 collective-permute-done
  263.8 2.9 conditional.4
  269.4 3.3 collective-permute-done
  280.5 3.3 collective-permute-done
  285.9 2.9 conditional.4
  291.5 3.3 collective-permute-done
  302.6 3.3 collective-permute-done
  308.0 2.9 conditional.4
  313.3 47.2 %all_gather.14 = bf16[1,512,512]{2,1,0:T(8,128)(2,1)S(1)} all-gather(bf16[1,16,512]{2,1,0:T(8,128)(2,1)S(1)} %constant_dynamic-slice_fusion.1), channel_id=1, replica_groups=mesh['inst'=16,'sp'=32] {'sp'}, dimensions={1}, use_global_device_ids=true | all-gather | bytes 540672 | tf_op jit(solution)/shard_map/all_gather | solution.py:113
  360.4 48.3 %all_gather.15 = bf16[1,512,512]{2,1,0:T(8,128)(2,1)S(1)} all-gather(bf16[1,16,512]{2,1,0:T(8,128)(2,1)S(1)} %constant_dynamic-slice_fusion), channel_id=1, replica_groups=mesh['inst'=16,'sp'=32] {'sp'}, dimensions={1}, use_global_device_ids=true | all-gather | bytes 540672 | tf_op jit(solution)/shard_map/all_gather | solution.py:114
  (258 shorter events, 110.2 us)
Async XLA Ops:
  16.6 14.7 %all-to-all-start.2 = ((bf16[16,16,512]{2,1,0:T(8,128)(2,1)}), bf16[16,16,512]{2,1,0:T(8,128)(2,1)S(1)}, u32[]{:S(2)}, u32[]{:S(2)}) async-start(bf16[16,16,512]{2,1,0:T(8,128)(2,1)} %get-tuple-element.409), calls=%async_computation.2 | async-start | bytes 524288 | tf_op jit(solution)/shard_map/all_to_all | solution.py:103
  31.3 377.4 %all-to-all-start.1 = ((bf16[16,512,128]{2,1,0:T(8,128)(2,1)}), bf16[16,512,128]{2,1,0:T(8,128)(2,1)}, u32[]{:S(2)}, u32[]{:S(2)}) async-start(bf16[16,512,128]{2,1,0:T(8,128)(2,1)} %broadcast_multiply_fusion), calls=%async_computation.1 | async-start | bytes 4194304 | tf_op jit(solution)/shard_map/all_to_all | solution.py:101
  145.9 5.3 %collective-permute-start = (bf16[768,128]{1,0:T(8,128)(2,1)}, bf16[768,128]{1,0:T(8,128)(2,1)S(1)}, u32[]{:S(2)}, u32[]{:S(2)}) collective-permute-start(bf16[768,128]{1,0:T(8,128)(2,1)} %get-tuple-element.506), channel_id=1, source_target_pairs={{480,0},{0,32},{32,64},{64,96},{96,128},{128,160},{160,192},{192,2... | collective-permute-start | bytes 589832 | tf_op jit(solution)/shard_map/while/body/eval_jaxpr/ppermute | solution.py:14
  145.9 7.4 %collective-permute-start.1 = (bf16[768,128]{1,0:T(8,128)(2,1)S(1)}, bf16[768,128]{1,0:T(8,128)(2,1)S(1)}, u32[]{:S(2)}, u32[]{:S(2)}) collective-permute-start(bf16[768,128]{1,0:T(8,128)(2,1)S(1)} %get-tuple-element.507), channel_id=1, source_target_pairs={{480,0},{0,32},{32,64},{64,96},{96,128},{128,160},{160,192},{192,2... | collective-permute-start | bytes 589832 | tf_op jit(solution)/shard_map/while/body/eval_jaxpr/ppermute | solution.py:14
  156.9 5.3 %collective-permute-start = (bf16[768,128]{1,0:T(8,128)(2,1)}, bf16[768,128]{1,0:T(8,128)(2,1)S(1)}, u32[]{:S(2)}, u32[]{:S(2)}) collective-permute-start(bf16[768,128]{1,0:T(8,128)(2,1)} %get-tuple-element.506), channel_id=1, source_target_pairs={{480,0},{0,32},{32,64},{64,96},{96,128},{128,160},{160,192},{192,2... | collective-permute-start | bytes 589832 | tf_op jit(solution)/shard_map/while/body/eval_jaxpr/ppermute | solution.py:14
  156.9 7.4 %collective-permute-start.1 = (bf16[768,128]{1,0:T(8,128)(2,1)S(1)}, bf16[768,128]{1,0:T(8,128)(2,1)S(1)}, u32[]{:S(2)}, u32[]{:S(2)}) collective-permute-start(bf16[768,128]{1,0:T(8,128)(2,1)S(1)} %get-tuple-element.507), channel_id=1, source_target_pairs={{480,0},{0,32},{32,64},{64,96},{96,128},{128,160},{160,192},{192,2... | collective-permute-start | bytes 589832 | tf_op jit(solution)/shard_map/while/body/eval_jaxpr/ppermute | solution.py:14
  167.9 5.3 %collective-permute-start = (bf16[768,128]{1,0:T(8,128)(2,1)}, bf16[768,128]{1,0:T(8,128)(2,1)S(1)}, u32[]{:S(2)}, u32[]{:S(2)}) collective-permute-start(bf16[768,128]{1,0:T(8,128)(2,1)} %get-tuple-element.506), channel_id=1, source_target_pairs={{480,0},{0,32},{32,64},{64,96},{96,128},{128,160},{160,192},{192,2... | collective-permute-start | bytes 589832 | tf_op jit(solution)/shard_map/while/body/eval_jaxpr/ppermute | solution.py:14
  168.0 7.4 %collective-permute-start.1 = (bf16[768,128]{1,0:T(8,128)(2,1)S(1)}, bf16[768,128]{1,0:T(8,128)(2,1)S(1)}, u32[]{:S(2)}, u32[]{:S(2)}) collective-permute-start(bf16[768,128]{1,0:T(8,128)(2,1)S(1)} %get-tuple-element.507), channel_id=1, source_target_pairs={{480,0},{0,32},{32,64},{64,96},{96,128},{128,160},{160,192},{192,2... | collective-permute-start | bytes 589832 | tf_op jit(solution)/shard_map/while/body/eval_jaxpr/ppermute | solution.py:14
  179.0 5.3 %collective-permute-start = (bf16[768,128]{1,0:T(8,128)(2,1)}, bf16[768,128]{1,0:T(8,128)(2,1)S(1)}, u32[]{:S(2)}, u32[]{:S(2)}) collective-permute-start(bf16[768,128]{1,0:T(8,128)(2,1)} %get-tuple-element.506), channel_id=1, source_target_pairs={{480,0},{0,32},{32,64},{64,96},{96,128},{128,160},{160,192},{192,2... | collective-permute-start | bytes 589832 | tf_op jit(solution)/shard_map/while/body/eval_jaxpr/ppermute | solution.py:14
  179.0 7.4 %collective-permute-start.1 = (bf16[768,128]{1,0:T(8,128)(2,1)S(1)}, bf16[768,128]{1,0:T(8,128)(2,1)S(1)}, u32[]{:S(2)}, u32[]{:S(2)}) collective-permute-start(bf16[768,128]{1,0:T(8,128)(2,1)S(1)} %get-tuple-element.507), channel_id=1, source_target_pairs={{480,0},{0,32},{32,64},{64,96},{96,128},{128,160},{160,192},{192,2... | collective-permute-start | bytes 589832 | tf_op jit(solution)/shard_map/while/body/eval_jaxpr/ppermute | solution.py:14
  190.0 5.3 %collective-permute-start = (bf16[768,128]{1,0:T(8,128)(2,1)}, bf16[768,128]{1,0:T(8,128)(2,1)S(1)}, u32[]{:S(2)}, u32[]{:S(2)}) collective-permute-start(bf16[768,128]{1,0:T(8,128)(2,1)} %get-tuple-element.506), channel_id=1, source_target_pairs={{480,0},{0,32},{32,64},{64,96},{96,128},{128,160},{160,192},{192,2... | collective-permute-start | bytes 589832 | tf_op jit(solution)/shard_map/while/body/eval_jaxpr/ppermute | solution.py:14
  190.1 7.4 %collective-permute-start.1 = (bf16[768,128]{1,0:T(8,128)(2,1)S(1)}, bf16[768,128]{1,0:T(8,128)(2,1)S(1)}, u32[]{:S(2)}, u32[]{:S(2)}) collective-permute-start(bf16[768,128]{1,0:T(8,128)(2,1)S(1)} %get-tuple-element.507), channel_id=1, source_target_pairs={{480,0},{0,32},{32,64},{64,96},{96,128},{128,160},{160,192},{192,2... | collective-permute-start | bytes 589832 | tf_op jit(solution)/shard_map/while/body/eval_jaxpr/ppermute | solution.py:14
  201.1 5.3 %collective-permute-start = (bf16[768,128]{1,0:T(8,128)(2,1)}, bf16[768,128]{1,0:T(8,128)(2,1)S(1)}, u32[]{:S(2)}, u32[]{:S(2)}) collective-permute-start(bf16[768,128]{1,0:T(8,128)(2,1)} %get-tuple-element.506), channel_id=1, source_target_pairs={{480,0},{0,32},{32,64},{64,96},{96,128},{128,160},{160,192},{192,2... | collective-permute-start | bytes 589832 | tf_op jit(solution)/shard_map/while/body/eval_jaxpr/ppermute | solution.py:14
  201.1 7.4 %collective-permute-start.1 = (bf16[768,128]{1,0:T(8,128)(2,1)S(1)}, bf16[768,128]{1,0:T(8,128)(2,1)S(1)}, u32[]{:S(2)}, u32[]{:S(2)}) collective-permute-start(bf16[768,128]{1,0:T(8,128)(2,1)S(1)} %get-tuple-element.507), channel_id=1, source_target_pairs={{480,0},{0,32},{32,64},{64,96},{96,128},{128,160},{160,192},{192,2... | collective-permute-start | bytes 589832 | tf_op jit(solution)/shard_map/while/body/eval_jaxpr/ppermute | solution.py:14
  212.1 5.3 %collective-permute-start = (bf16[768,128]{1,0:T(8,128)(2,1)}, bf16[768,128]{1,0:T(8,128)(2,1)S(1)}, u32[]{:S(2)}, u32[]{:S(2)}) collective-permute-start(bf16[768,128]{1,0:T(8,128)(2,1)} %get-tuple-element.506), channel_id=1, source_target_pairs={{480,0},{0,32},{32,64},{64,96},{96,128},{128,160},{160,192},{192,2... | collective-permute-start | bytes 589832 | tf_op jit(solution)/shard_map/while/body/eval_jaxpr/ppermute | solution.py:14
  212.2 7.4 %collective-permute-start.1 = (bf16[768,128]{1,0:T(8,128)(2,1)S(1)}, bf16[768,128]{1,0:T(8,128)(2,1)S(1)}, u32[]{:S(2)}, u32[]{:S(2)}) collective-permute-start(bf16[768,128]{1,0:T(8,128)(2,1)S(1)} %get-tuple-element.507), channel_id=1, source_target_pairs={{480,0},{0,32},{32,64},{64,96},{96,128},{128,160},{160,192},{192,2... | collective-permute-start | bytes 589832 | tf_op jit(solution)/shard_map/while/body/eval_jaxpr/ppermute | solution.py:14
  223.2 5.3 %collective-permute-start = (bf16[768,128]{1,0:T(8,128)(2,1)}, bf16[768,128]{1,0:T(8,128)(2,1)S(1)}, u32[]{:S(2)}, u32[]{:S(2)}) collective-permute-start(bf16[768,128]{1,0:T(8,128)(2,1)} %get-tuple-element.506), channel_id=1, source_target_pairs={{480,0},{0,32},{32,64},{64,96},{96,128},{128,160},{160,192},{192,2... | collective-permute-start | bytes 589832 | tf_op jit(solution)/shard_map/while/body/eval_jaxpr/ppermute | solution.py:14
  223.2 7.4 %collective-permute-start.1 = (bf16[768,128]{1,0:T(8,128)(2,1)S(1)}, bf16[768,128]{1,0:T(8,128)(2,1)S(1)}, u32[]{:S(2)}, u32[]{:S(2)}) collective-permute-start(bf16[768,128]{1,0:T(8,128)(2,1)S(1)} %get-tuple-element.507), channel_id=1, source_target_pairs={{480,0},{0,32},{32,64},{64,96},{96,128},{128,160},{160,192},{192,2... | collective-permute-start | bytes 589832 | tf_op jit(solution)/shard_map/while/body/eval_jaxpr/ppermute | solution.py:14
  234.2 5.3 %collective-permute-start = (bf16[768,128]{1,0:T(8,128)(2,1)}, bf16[768,128]{1,0:T(8,128)(2,1)S(1)}, u32[]{:S(2)}, u32[]{:S(2)}) collective-permute-start(bf16[768,128]{1,0:T(8,128)(2,1)} %get-tuple-element.506), channel_id=1, source_target_pairs={{480,0},{0,32},{32,64},{64,96},{96,128},{128,160},{160,192},{192,2... | collective-permute-start | bytes 589832 | tf_op jit(solution)/shard_map/while/body/eval_jaxpr/ppermute | solution.py:14
  234.3 7.4 %collective-permute-start.1 = (bf16[768,128]{1,0:T(8,128)(2,1)S(1)}, bf16[768,128]{1,0:T(8,128)(2,1)S(1)}, u32[]{:S(2)}, u32[]{:S(2)}) collective-permute-start(bf16[768,128]{1,0:T(8,128)(2,1)S(1)} %get-tuple-element.507), channel_id=1, source_target_pairs={{480,0},{0,32},{32,64},{64,96},{96,128},{128,160},{160,192},{192,2... | collective-permute-start | bytes 589832 | tf_op jit(solution)/shard_map/while/body/eval_jaxpr/ppermute | solution.py:14
  245.3 5.3 %collective-permute-start = (bf16[768,128]{1,0:T(8,128)(2,1)}, bf16[768,128]{1,0:T(8,128)(2,1)S(1)}, u32[]{:S(2)}, u32[]{:S(2)}) collective-permute-start(bf16[768,128]{1,0:T(8,128)(2,1)} %get-tuple-element.506), channel_id=1, source_target_pairs={{480,0},{0,32},{32,64},{64,96},{96,128},{128,160},{160,192},{192,2... | collective-permute-start | bytes 589832 | tf_op jit(solution)/shard_map/while/body/eval_jaxpr/ppermute | solution.py:14
  245.3 7.4 %collective-permute-start.1 = (bf16[768,128]{1,0:T(8,128)(2,1)S(1)}, bf16[768,128]{1,0:T(8,128)(2,1)S(1)}, u32[]{:S(2)}, u32[]{:S(2)}) collective-permute-start(bf16[768,128]{1,0:T(8,128)(2,1)S(1)} %get-tuple-element.507), channel_id=1, source_target_pairs={{480,0},{0,32},{32,64},{64,96},{96,128},{128,160},{160,192},{192,2... | collective-permute-start | bytes 589832 | tf_op jit(solution)/shard_map/while/body/eval_jaxpr/ppermute | solution.py:14
  256.3 5.3 %collective-permute-start = (bf16[768,128]{1,0:T(8,128)(2,1)}, bf16[768,128]{1,0:T(8,128)(2,1)S(1)}, u32[]{:S(2)}, u32[]{:S(2)}) collective-permute-start(bf16[768,128]{1,0:T(8,128)(2,1)} %get-tuple-element.506), channel_id=1, source_target_pairs={{480,0},{0,32},{32,64},{64,96},{96,128},{128,160},{160,192},{192,2... | collective-permute-start | bytes 589832 | tf_op jit(solution)/shard_map/while/body/eval_jaxpr/ppermute | solution.py:14
  256.4 7.4 %collective-permute-start.1 = (bf16[768,128]{1,0:T(8,128)(2,1)S(1)}, bf16[768,128]{1,0:T(8,128)(2,1)S(1)}, u32[]{:S(2)}, u32[]{:S(2)}) collective-permute-start(bf16[768,128]{1,0:T(8,128)(2,1)S(1)} %get-tuple-element.507), channel_id=1, source_target_pairs={{480,0},{0,32},{32,64},{64,96},{96,128},{128,160},{160,192},{192,2... | collective-permute-start | bytes 589832 | tf_op jit(solution)/shard_map/while/body/eval_jaxpr/ppermute | solution.py:14
  267.4 5.3 %collective-permute-start = (bf16[768,128]{1,0:T(8,128)(2,1)}, bf16[768,128]{1,0:T(8,128)(2,1)S(1)}, u32[]{:S(2)}, u32[]{:S(2)}) collective-permute-start(bf16[768,128]{1,0:T(8,128)(2,1)} %get-tuple-element.506), channel_id=1, source_target_pairs={{480,0},{0,32},{32,64},{64,96},{96,128},{128,160},{160,192},{192,2... | collective-permute-start | bytes 589832 | tf_op jit(solution)/shard_map/while/body/eval_jaxpr/ppermute | solution.py:14
  267.4 7.4 %collective-permute-start.1 = (bf16[768,128]{1,0:T(8,128)(2,1)S(1)}, bf16[768,128]{1,0:T(8,128)(2,1)S(1)}, u32[]{:S(2)}, u32[]{:S(2)}) collective-permute-start(bf16[768,128]{1,0:T(8,128)(2,1)S(1)} %get-tuple-element.507), channel_id=1, source_target_pairs={{480,0},{0,32},{32,64},{64,96},{96,128},{128,160},{160,192},{192,2... | collective-permute-start | bytes 589832 | tf_op jit(solution)/shard_map/while/body/eval_jaxpr/ppermute | solution.py:14
  278.4 5.3 %collective-permute-start = (bf16[768,128]{1,0:T(8,128)(2,1)}, bf16[768,128]{1,0:T(8,128)(2,1)S(1)}, u32[]{:S(2)}, u32[]{:S(2)}) collective-permute-start(bf16[768,128]{1,0:T(8,128)(2,1)} %get-tuple-element.506), channel_id=1, source_target_pairs={{480,0},{0,32},{32,64},{64,96},{96,128},{128,160},{160,192},{192,2... | collective-permute-start | bytes 589832 | tf_op jit(solution)/shard_map/while/body/eval_jaxpr/ppermute | solution.py:14
  278.5 7.4 %collective-permute-start.1 = (bf16[768,128]{1,0:T(8,128)(2,1)S(1)}, bf16[768,128]{1,0:T(8,128)(2,1)S(1)}, u32[]{:S(2)}, u32[]{:S(2)}) collective-permute-start(bf16[768,128]{1,0:T(8,128)(2,1)S(1)} %get-tuple-element.507), channel_id=1, source_target_pairs={{480,0},{0,32},{32,64},{64,96},{96,128},{128,160},{160,192},{192,2... | collective-permute-start | bytes 589832 | tf_op jit(solution)/shard_map/while/body/eval_jaxpr/ppermute | solution.py:14
  289.5 5.3 %collective-permute-start = (bf16[768,128]{1,0:T(8,128)(2,1)}, bf16[768,128]{1,0:T(8,128)(2,1)S(1)}, u32[]{:S(2)}, u32[]{:S(2)}) collective-permute-start(bf16[768,128]{1,0:T(8,128)(2,1)} %get-tuple-element.506), channel_id=1, source_target_pairs={{480,0},{0,32},{32,64},{64,96},{96,128},{128,160},{160,192},{192,2... | collective-permute-start | bytes 589832 | tf_op jit(solution)/shard_map/while/body/eval_jaxpr/ppermute | solution.py:14
  289.5 7.4 %collective-permute-start.1 = (bf16[768,128]{1,0:T(8,128)(2,1)S(1)}, bf16[768,128]{1,0:T(8,128)(2,1)S(1)}, u32[]{:S(2)}, u32[]{:S(2)}) collective-permute-start(bf16[768,128]{1,0:T(8,128)(2,1)S(1)} %get-tuple-element.507), channel_id=1, source_target_pairs={{480,0},{0,32},{32,64},{64,96},{96,128},{128,160},{160,192},{192,2... | collective-permute-start | bytes 589832 | tf_op jit(solution)/shard_map/while/body/eval_jaxpr/ppermute | solution.py:14
  300.5 5.3 %collective-permute-start = (bf16[768,128]{1,0:T(8,128)(2,1)}, bf16[768,128]{1,0:T(8,128)(2,1)S(1)}, u32[]{:S(2)}, u32[]{:S(2)}) collective-permute-start(bf16[768,128]{1,0:T(8,128)(2,1)} %get-tuple-element.506), channel_id=1, source_target_pairs={{480,0},{0,32},{32,64},{64,96},{96,128},{128,160},{160,192},{192,2... | collective-permute-start | bytes 589832 | tf_op jit(solution)/shard_map/while/body/eval_jaxpr/ppermute | solution.py:14
  300.6 7.4 %collective-permute-start.1 = (bf16[768,128]{1,0:T(8,128)(2,1)S(1)}, bf16[768,128]{1,0:T(8,128)(2,1)S(1)}, u32[]{:S(2)}, u32[]{:S(2)}) collective-permute-start(bf16[768,128]{1,0:T(8,128)(2,1)S(1)} %get-tuple-element.507), channel_id=1, source_target_pairs={{480,0},{0,32},{32,64},{64,96},{96,128},{128,160},{160,192},{192,2... | collective-permute-start | bytes 589832 | tf_op jit(solution)/shard_map/while/body/eval_jaxpr/ppermute | solution.py:14
  (7 other events, 273.0 us)
where the time goes:
time: 414 us; the launch traced here: 411 us
  blocking collectives  207 us (50%)
  waiting for transfers between devices  86.8 us (21%)
  loops' own time  41.3 us (10%)
  local copies, waits for them, and re-layouts  22.7 us (5%)
  matrix products  21.1 us (5%)
  starting transfers between devices  14.6 us (4%)
  other arithmetic  14 us (3%)
    ppermute x30, waiting for transfers between devices, passed_along(): return lax.ppermute(block, axis, route)  81.1 us
    all_gather x1, blocking collectives, body(): lax.all_gather(prompt_keys, 'sp', axis=1, tiled=True)  50.9 us
    all_gather x1, blocking collectives, body(): lax.all_gather(prompt_values, 'sp', axis=1, tiled=True)  48.6 us
    all_gather x1, blocking collectives, body(): lax.all_gather(moved_values, 'sp', axis=1, tiled=True)  48.3 us
    all_gather x1, blocking collectives, body(): lax.all_gather(moved_keys, 'sp', axis=1, tiled=True)  47.2 us
    another operation x1, loops' own time, body(): lax.fori_loop(1, inst_count, cycle_turn, (first_state, own_keys, own_valu...  20.9 us
    another operation x15, loops' own time, cycle_turn(): lax.cond(key_span < my_span, lambda inner: absorb(inner, queries, key_blo...  20.4 us
    all_to_all x1, blocking collectives, body(): lax.all_to_all(slot_mask * short_keys, 'inst', split_axis=0, concat_axis=...  12.5 us
  transfers between devices with their start and end apart: 32, of which 31 were waited for; matrix products, arithmetic and copies ran while one was open for 13% of the time, Pallas kernels for 0%

commit v1 on v0

v1 whole, which is shorter than its diff:
```python
import functools

import jax
import jax.numpy as jnp
from jax import lax
from jax.experimental import pallas as pl
from jax.experimental.pallas import tpu as pltpu
from jax.sharding import PartitionSpec as P

DH = 128
QH = 32
KVH = 4
TILE = 256
LOG2E = 1.4426950408889634
GAIN = DH ** (-0.5) * LOG2E
VMEM = 48 * 1024 * 1024


def with_ones(values):
    return jnp.concatenate([values, jnp.ones_like(values)], axis=1)


def scores_of(q, keys):
    return lax.dot_general(q, keys, (((1,), (1,)), ((), ())), preferred_element_type=jnp.float32)


def weigh(weights, values):
    return jnp.dot(
        weights.astype(jnp.bfloat16), with_ones(values), preferred_element_type=jnp.float32
    )


def diagonal_kernel(q_ref, kv_ref, acc_ref, max_ref):
    for start in range(0, q_ref.shape[0], TILE):
        rows = pl.ds(start, TILE)
        seen = start + TILE
        scores = scores_of(q_ref[rows, :], kv_ref[:seen, :DH])
        row = start + lax.broadcasted_iota(jnp.int32, scores.shape, 0)
        col = lax.broadcasted_iota(jnp.int32, scores.shape, 1)
        scores = jnp.where(col <= row, scores, -jnp.inf)
        top = jnp.max(scores, axis=1, keepdims=True)
        weights = jnp.exp2((scores - top) * GAIN)
        acc_ref[rows, :] = weigh(weights, kv_ref[:seen, DH:])
        max_ref[rows, :] = jnp.broadcast_to(top, (TILE, DH))


def short_kernel(lengths_ref, q_ref, kv_ref, out_ref):
    ends = []
    total = 0
    for k in range(lengths_ref.shape[0]):
        total = total + lengths_ref[k]
        ends.append(total)
    for start in range(0, q_ref.shape[0], TILE):
        rows = pl.ds(start, TILE)
        seen = start + TILE
        scores = scores_of(q_ref[rows, :], kv_ref[:seen, :DH])
        row = start + lax.broadcasted_iota(jnp.int32, (TILE, 1), 0)
        first = jnp.zeros((TILE, 1), jnp.int32)
        for end in ends:
            first = jnp.where(row >= end, end, first)
        col = lax.broadcasted_iota(jnp.int32, scores.shape, 1)
        scores = jnp.where((col <= row) & (col >= first), scores, -jnp.inf)
        top = jnp.max(scores, axis=1, keepdims=True)
        weights = jnp.exp2((scores - top) * GAIN)
        acc = weigh(weights, kv_ref[:seen, DH:])
        out_ref[rows, :] = (acc[:, :DH] / acc[:, DH:]).astype(jnp.bfloat16)


def earlier_kernel(order_ref, count_ref, q_ref, kv_ref, acc0_ref, max0_ref, out_ref, acc, top):
    step = pl.program_id(0)

    @pl.when(step == 0)
    def _():
        acc[...] = acc0_ref[...]
        top[...] = max0_ref[:, :1]

    @pl.when(step < count_ref[0])
    def _():
        for start in range(0, q_ref.shape[0], TILE):
            rows = pl.ds(start, TILE)
            scores = scores_of(q_ref[rows, :], kv_ref[0, :, :DH])
            old = top[rows, :]
            new = jnp.maximum(old, jnp.max(scores, axis=1, keepdims=True))
            weights = jnp.exp2((scores - new) * GAIN)
            factor = jnp.exp2((old - new) * GAIN)
            acc[rows, :] = acc[rows, :] * factor + weigh(weights, kv_ref[0, :, DH:])
            top[rows, :] = new

    @pl.when(step == pl.num_programs(0) - 1)
    def _():
        out_ref[...] = (acc[:, :DH] / acc[:, DH:]).astype(jnp.bfloat16)


def diagonal(q, kv):
    rows = q.shape[0]
    return pl.pallas_call(
        diagonal_kernel,
        out_shape=(
            jax.ShapeDtypeStruct((rows, 2 * DH), jnp.float32),
            jax.ShapeDtypeStruct((rows, DH), jnp.float32),
        ),
        compiler_params=pltpu.CompilerParams(vmem_limit_bytes=VMEM),
        cost_estimate=pl.CostEstimate(flops=2 * rows * rows * DH, bytes_accessed=4 * rows * 1024, transcendentals=rows * rows // 2),
        name="diagonal",
    )(q, kv)


def shorts(lengths, q, kv):
    rows = q.shape[0]
    return pl.pallas_call(
        short_kernel,
        out_shape=jax.ShapeDtypeStruct((rows, DH), jnp.bfloat16),
        in_specs=[
            pl.BlockSpec(memory_space=pltpu.SMEM),
            pl.BlockSpec(memory_space=pltpu.VMEM),
            pl.BlockSpec(memory_space=pltpu.VMEM),
        ],
        compiler_params=pltpu.CompilerParams(vmem_limit_bytes=VMEM),
        cost_estimate=pl.CostEstimate(flops=2 * rows * rows * DH, bytes_accessed=rows * 1024, transcendentals=rows * rows // 2),
        name="shorts",
    )(lengths, q, kv)


def earlier(order, count, q, kv_all, acc, top):
    groups, rows, width = kv_all.shape
    whole = lambda j, order, count: (0, 0)
    return pl.pallas_call(
        earlier_kernel,
        out_shape=jax.ShapeDtypeStruct((rows, DH), jnp.bfloat16),
        grid_spec=pltpu.PrefetchScalarGridSpec(
            num_scalar_prefetch=2,
            grid=(groups,),
            in_specs=[
                pl.BlockSpec((rows, DH), whole),
                pl.BlockSpec((1, rows, width), lambda j, order, count: (order[j], 0, 0)),
                pl.BlockSpec((rows, 2 * DH), whole),
                pl.BlockSpec((rows, DH), whole),
            ],
            out_specs=pl.BlockSpec((rows, DH), whole),
            scratch_shapes=[
                pltpu.VMEM((rows, 2 * DH), jnp.float32),
                pltpu.VMEM((rows, 1), jnp.float32),
            ],
        ),
        compiler_params=pltpu.CompilerParams(vmem_limit_bytes=VMEM),
        cost_estimate=pl.CostEstimate(
            flops=2 * 8 * 2 * rows * rows * DH, bytes_accessed=groups * rows * width * 2, transcendentals=8 * rows * rows
        ),
        name="earlier",
    )(order, count, q, kv_all, acc, top)


def reorder_kernel(index_ref, blocks_ref, out_ref):
    for slot in range(out_ref.shape[0]):
        out_ref[slot] = blocks_ref[index_ref[slot]]


def reorder(index, blocks):
    return pl.pallas_call(
        reorder_kernel,
        out_shape=jax.ShapeDtypeStruct(blocks.shape, blocks.dtype),
        in_specs=[
            pl.BlockSpec(memory_space=pltpu.SMEM),
            pl.BlockSpec(memory_space=pltpu.VMEM),
        ],
        name="reorder",
    )(index, blocks)


def by_head(keys, values, copies):
    rows = keys.shape[0]
    both = jnp.concatenate(
        [keys.reshape(rows, KVH, DH), values.reshape(rows, KVH, DH)], axis=2
    ).transpose(1, 0, 2)
    return jnp.broadcast_to(both[:, None], (KVH, copies, rows, 2 * DH)).reshape(
        KVH * copies, rows, 2 * DH
    )


def swapped(blocks, axis):
    return lax.all_to_all(blocks, axis, split_axis=0, concat_axis=0, tiled=True)


def body(
    prompt_queries,
    prompt_keys,
    prompt_values,
    span_of,
    short_queries,
    short_keys,
    short_values,
    short_lengths,
    pair_partner,
):
    groups = lax.axis_size("inst")
    me = lax.axis_index("inst")
    copies = lax.axis_size("sp") // KVH
    span_rows = prompt_queries.shape[1]
    short_rows = short_queries.shape[1]

    own = swapped(by_head(prompt_keys[0], prompt_values[0], copies), "sp")
    own = own.reshape(span_rows, 2 * DH)
    everyone = lax.all_gather(own, "inst", axis=0, tiled=False)

    short_keys, short_values, own = lax.optimization_barrier((short_keys, short_values, own))
    acc, top = diagonal(prompt_queries[0], own)

    short_own = swapped(by_head(short_keys[0], short_values[0], copies), "sp")
    short_own = short_own.reshape(short_rows, 2 * DH)
    served = shorts(short_lengths[me], short_queries[0], short_own)
    pieces = swapped(served.reshape(groups, short_rows // groups, DH), "inst")
    pieces = swapped(reorder(pair_partner, pieces), "inst")
    short_out = pieces.reshape(1, short_rows, DH)

    my_span = span_of[me]
    ids = jnp.arange(groups, dtype=jnp.int32)
    holder = jnp.sum(jnp.where(span_of[None, :] == ids[:, None], ids[None, :], 0), axis=1)
    last = jnp.maximum(my_span - 1, 0)
    order = jnp.where(ids <= last, holder, jnp.sum(jnp.where(ids == last, holder, 0)))
    prompt_out = earlier(order, my_span[None], prompt_queries[0], everyone, acc, top)
    return (prompt_out[None], short_out)


def solution(mesh):
    placed = (
        P("inst", None, "sp"),
        P("inst", "sp", None),
        P("inst", "sp", None),
        P(),
        P("inst", None, "sp"),
        P("inst", "sp", None),
        P("inst", "sp", None),
        P(),
        P(),
    )
    return jax.shard_map(
        body,
        mesh=mesh,
        in_specs=placed,
        out_specs=(P("inst", None, "sp"), P("inst", None, "sp")),
        check_vma=False,
    )
```

time: 414 us -> 122 us (0.29)
  the two profiles are of different devices: /device:TPU:448 before, /device:TPU:1 now
where the time goes in v1:
time: 122 us
  Pallas kernels  25.4 us (21%)
  starting transfers between devices  25 us (20%)
  blocking collectives  22.1 us (18%)
  waiting for transfers between devices  22.1 us (18%)
  between operations  14.8 us (12%)
  local copies, waits for them, and re-layouts  10.3 us (8%)
  other arithmetic  2.1 us (2%)
    all_to_all x3, starting transfers between devices, swapped(): return lax.all_to_all(blocks, axis, split_axis=0, concat_axis=0, tiled=True)  25 us
    all_to_all x1, blocking collectives, swapped(): return lax.all_to_all(blocks, axis, split_axis=0, concat_axis=0, tiled=True)  22.1 us
    all_to_all x3, waiting for transfers between devices, swapped(): return lax.all_to_all(blocks, axis, split_axis=0, concat_axis=0, tiled=True)  22 us
    pallas_call x1, Pallas kernels, earlier(): pl.pallas_call(earlier_kernel, out_shape=jax.ShapeDtypeStruct((rows, DH),...  20.5 us
    unnamed x13, local copies, waits for them, and re-layouts  5.07 us
  transfers between devices with their start and end apart: 4, of which 3 were waited for; matrix products, arithmetic and copies ran while one was open for 5% of the time, Pallas kernels for 4%

profile of v1, /device:TPU:1, one launch (start us, length us, event | category | flops | bytes accessed | tf_op | source)
XLA Modules:
  0.0 121.7 jit_solution(144427596884880063)
XLA Ops:
  7.2 0.0 copy-start
  7.2 0.0 all-gather.2.cloned.1.call-start
  7.2 0.8 reshape_squeeze.13
  8.0 0.8 reshape_squeeze.12
  8.8 22.1 %all_to_all.20 = bf16[32,24,256]{2,1,0:T(8,128)(2,1)} all-to-all(bf16[32,24,256]{2,1,0:T(8,128)(2,1)S(1)} %bitcast.21), channel_id=1, replica_groups=mesh['inst'=16,'sp'=32] {'sp'}, dimensions={0} | all-to-all | bytes 786432 | tf_op jit(solution)/shard_map/all_to_all | solution.py:181
  30.9 0.0 all-gather.2.cloned.1.call-update
  30.9 0.7 reshape_squeeze.15
  31.6 0.7 reshape_squeeze.14
  32.4 0.7 broadcast_in_dim.44
  33.1 7.5 %all-to-all-start.1 = ((bf16[32,16,256]{2,1,0:T(8,128)(2,1)}), bf16[32,16,256]{2,1,0:T(8,128)(2,1)S(1)}, u32[]{:S(2)}, u32[]{:S(2)}) async-start(bf16[32,16,256]{2,1,0:T(8,128)(2,1)} %bitcast.9), calls=%async_computation.1 | async-start | bytes 524288 | tf_op jit(solution)/shard_map/all_to_all | solution.py:181
  40.6 0.0 copy-done
  40.6 0.2 dynamic-slice_reduce_fusion.lengths_ref
  40.8 9.5 %all-to-all-done.1 = bf16[32,16,256]{2,1,0:T(8,128)(2,1)S(1)} async-done(((bf16[32,16,256]{2,1,0:T(8,128)(2,1)}), bf16[32,16,256]{2,1,0:T(8,128)(2,1)S(1)}, u32[]{:S(2)}, u32[]{:S(2)}) %all-to-all-start.1) | async-done | bytes 262176 | tf_op jit(solution)/shard_map/all_to_all | solution.py:181
  50.3 0.9 copy-done.4
  51.2 2.0 %shorts.1 = bf16[512,128]{1,0:T(8,128)(2,1)} custom-call(s32[8]{0:T(128)S(1)} %dynamic-slice_reduce_fusion.lengths_ref, bf16[512,128]{1,0:T(8,128)(2,1)S(1)} %bitcast.20, bf16[512,256]{1,0:T(8,128)(2,1)S(1)} %bitcast.17), custom_call_target="tpu_custom_call" | custom-call | flops 67108864 | bytes 524288 | tf_op jit(solution)/shard_map/shorts/pallas_call | solution.py:110
  53.2 14.0 %all-to-all-start.2 = ((bf16[16,32,128]{2,1,0:T(8,128)(2,1)}), bf16[16,32,128]{2,1,0:T(8,128)(2,1)S(1)}, u32[]{:S(2)}, u32[]{:S(2)}) async-start(bf16[16,32,128]{2,1,0:T(8,128)(2,1)} %bitcast.11), calls=%async_computation.2 | async-start | bytes 262144 | tf_op jit(solution)/shard_map/all_to_all | solution.py:181
  67.1 1.3 %dynamic_slice.6.count_ref = s32[1]{0:T(128)} dynamic-slice(s32[16]{0:T(128)} %param.12, s32[]{:T(128)S(6)} %select_n.16), dynamic_slice_sizes={1} | dynamic-slice | bytes 12 | tf_op jit(solution)/shard_map/dynamic_slice | solution.py:215
  69.1 0.8 select_reduce_fusion
  69.9 7.8 %all-to-all-done.2.blocks_ref = bf16[16,32,128]{2,1,0:T(8,128)(2,1)S(1)} async-done(((bf16[16,32,128]{2,1,0:T(8,128)(2,1)}), bf16[16,32,128]{2,1,0:T(8,128)(2,1)S(1)}, u32[]{:S(2)}, u32[]{:S(2)}) %all-to-all-start.2) | async-done | bytes 131104 | tf_op jit(solution)/shard_map/all_to_all | solution.py:181
  77.7 0.7 copy-done.5
  78.4 1.6 %reorder.1 = bf16[16,32,128]{2,1,0:T(8,128)(2,1)} custom-call(s32[16]{0:T(128)} %index_ref.1, bf16[16,32,128]{2,1,0:T(8,128)(2,1)} %copy-done.5), custom_call_target="tpu_custom_call" | custom-call | tf_op jit(solution)/shard_map/reorder/pallas_call | solution.py:159
  80.0 3.6 %all-to-all-start.3 = ((bf16[16,32,128]{2,1,0:T(8,128)(2,1)}), bf16[16,32,128]{2,1,0:T(8,128)(2,1)S(1)}, u32[]{:S(2)}, u32[]{:S(2)}) async-start(bf16[16,32,128]{2,1,0:T(8,128)(2,1)} %reorder.1), calls=%async_computation.3 | async-start | bytes 262144 | tf_op jit(solution)/shard_map/all_to_all | solution.py:181
  83.5 0.6 fusion
  84.2 0.6 compare_select_fusion.1.order_ref
  84.8 0.0 copy-start.1
  84.8 1.0 copy-done.1
  85.8 0.9 copy-done.2
  86.7 1.2 %diagonal.1 = (f32[768,256]{1,0:T(8,128)S(1)}, f32[768,128]{1,0:T(8,128)S(1)}) custom-call(bf16[768,128]{1,0:T(8,128)(2,1)S(1)} %bitcast.18, bf16[768,256]{1,0:T(8,128)(2,1)S(1)} %bitcast.16), custom_call_target="tpu_custom_call" | custom-call | flops 150994944 | bytes 3145728 | tf_op jit(solution)/shard_map/diagonal/pallas_call | solution.py:96
  88.0 4.8 %all-to-all-done.3 = bf16[16,32,128]{2,1,0:T(8,128)(2,1)S(1)} async-done(((bf16[16,32,128]{2,1,0:T(8,128)(2,1)}), bf16[16,32,128]{2,1,0:T(8,128)(2,1)S(1)}, u32[]{:S(2)}, u32[]{:S(2)}) %all-to-all-start.3) | async-done | bytes 131104 | tf_op jit(solution)/shard_map/all_to_all | solution.py:181
  92.7 0.9 copy-done.3
  93.7 20.5 %earlier.1 = bf16[768,128]{1,0:T(8,128)(2,1)} custom-call(s32[16]{0:T(128)S(1)} %compare_select_fusion.1.order_ref, s32[1]{0:T(128)} %dynamic_slice.6.count_ref, bf16[768,128]{1,0:T(8,128)(2,1)S(1)} %bitcast.19, bf16[16,768,256]{2,1,0:T(8,128)(2,1)} %all-gather.2.cloned.1.call-done.kv_ref, f32[768,256]{1,0:T(8,128)S(1)} %get-tuple-element.8.acc0_ref, ...), custom_call_target="tpu_custom_call" | custom-call | flops 2415919104 | bytes 6291456 | tf_op jit(solution)/shard_map/earlier/pallas_call | solution.py:127
  114.2 0.7 copy.18
  (10 shorter events, 0.1 us)
Async XLA Ops:
  7.2 33.4 %copy-start = (s32[16,8]{0,1:T(8,128)S(1)}, s32[16,8]{0,1:T(8,128)}, u32[]{:S(2)}) copy-start(s32[16,8]{0,1:T(8,128)} %param.16) | copy-start | bytes 1540
  7.2 85.6 %all-gather.2.cloned.1.call-start = ((), (), s32[]{:S(2)}) async-start(), calls=%async_computation.4 | async-start | bytes 6684672 | tf_op jit(solution)/shard_map/all_gather | solution.py:203
  33.1 17.1 %all-to-all-start.1 = ((bf16[32,16,256]{2,1,0:T(8,128)(2,1)}), bf16[32,16,256]{2,1,0:T(8,128)(2,1)S(1)}, u32[]{:S(2)}, u32[]{:S(2)}) async-start(bf16[32,16,256]{2,1,0:T(8,128)(2,1)} %bitcast.9), calls=%async_computation.1 | async-start | bytes 524288 | tf_op jit(solution)/shard_map/all_to_all | solution.py:181
  50.3 0.9 copy-start.4
  53.2 24.6 %all-to-all-start.2 = ((bf16[16,32,128]{2,1,0:T(8,128)(2,1)}), bf16[16,32,128]{2,1,0:T(8,128)(2,1)S(1)}, u32[]{:S(2)}, u32[]{:S(2)}) async-start(bf16[16,32,128]{2,1,0:T(8,128)(2,1)} %bitcast.11), calls=%async_computation.2 | async-start | bytes 262144 | tf_op jit(solution)/shard_map/all_to_all | solution.py:181
  77.7 0.7 copy-start.5
  80.0 12.8 %all-to-all-start.3 = ((bf16[16,32,128]{2,1,0:T(8,128)(2,1)}), bf16[16,32,128]{2,1,0:T(8,128)(2,1)S(1)}, u32[]{:S(2)}, u32[]{:S(2)}) async-start(bf16[16,32,128]{2,1,0:T(8,128)(2,1)} %reorder.1), calls=%async_computation.3 | async-start | bytes 262144 | tf_op jit(solution)/shard_map/all_to_all | solution.py:181
  84.8 1.0 copy-start.1
  85.8 0.9 copy-start.2
  92.7 0.9 copy-start.3
Sparse Core Ops, SparseCore 0:
  31.0 55.6 all-gather.1

commit v2 on v1

v2 whole, which is shorter than its diff:
```python
import functools

import jax
import jax.numpy as jnp
from jax import lax
from jax.experimental import pallas as pl
from jax.experimental.pallas import tpu as pltpu
from jax.sharding import PartitionSpec as P

DH = 128
QH = 32
KVH = 4
CORES = 2
TILE = 128
SHORT_TILE = 256
LOG2E = 1.4426950408889634
GAIN = DH ** (-0.5) * LOG2E
VMEM = 48 * 1024 * 1024
SMEM_SPEC = pl.BlockSpec(memory_space=pltpu.SMEM)
VMEM_SPEC = pl.BlockSpec(memory_space=pltpu.VMEM)


def with_ones(values):
    return jnp.concatenate([values, jnp.ones_like(values)], axis=1)


def scores_of(q, keys):
    return lax.dot_general(q, keys, (((1,), (1,)), ((), ())), preferred_element_type=jnp.float32)


def weigh(weights, values):
    return jnp.dot(
        weights.astype(jnp.bfloat16), with_ones(values), preferred_element_type=jnp.float32
    )


def add_block(q_ref, keys_t, values, state):
    tiles = [pl.ds(start, TILE) for start in range(0, q_ref.shape[0], TILE)]
    values = with_ones(values)
    scores = [jnp.dot(q_ref[rows, :], keys_t, preferred_element_type=jnp.float32) for rows in tiles]
    olds = [state[rows, 2 * DH : 2 * DH + 1] for rows in tiles]
    parts = []
    for score, old in zip(scores, olds):
        new = jnp.maximum(old, jnp.max(score, axis=1, keepdims=True))
        weights = jnp.exp2((score - new) * GAIN).astype(jnp.bfloat16)
        parts.append((new, jnp.exp2((old - new) * GAIN), weights))
    for rows, (new, factor, weights) in zip(tiles, parts):
        added = jnp.dot(weights, values, preferred_element_type=jnp.float32)
        state[rows, : 2 * DH] = state[rows, : 2 * DH] * factor + added
        state[rows, 2 * DH :] = jnp.broadcast_to(new, (TILE, DH))


def diagonal(q_ref, keys_t, kv_ref, state):
    for start in range(0, q_ref.shape[0], TILE):
        rows = pl.ds(start, TILE)
        seen = start + TILE
        scores = jnp.dot(q_ref[rows, :], keys_t[:, :seen], preferred_element_type=jnp.float32)
        row = start + lax.broadcasted_iota(jnp.int32, scores.shape, 0)
        col = lax.broadcasted_iota(jnp.int32, scores.shape, 1)
        scores = jnp.where(col <= row, scores, -jnp.inf)
        top = jnp.max(scores, axis=1, keepdims=True)
        weights = jnp.exp2((scores - top) * GAIN)
        state[rows, : 2 * DH] = weigh(weights, kv_ref[:seen, DH:])
        state[rows, 2 * DH :] = jnp.broadcast_to(top, (TILE, DH))


def own_kernel(seen_ref, q_ref, other_q_ref, kv_ref, state, other, keys_t):
    keys_t[...] = kv_ref[: q_ref.shape[0], :DH].T
    diagonal(q_ref, keys_t, kv_ref, state)
    other[:, : 2 * DH] = jnp.zeros((other.shape[0], 2 * DH), jnp.float32)
    other[:, 2 * DH :] = jnp.full((other.shape[0], DH), -jnp.inf, jnp.float32)

    @pl.when(seen_ref[1, 0] > 0)
    def _():
        add_block(other_q_ref, keys_t[...], kv_ref[: q_ref.shape[0], DH:], other)


def ring_kernel(seen_ref, q_ref, other_q_ref, *refs, indices):
    kv_refs, (before, other_before, state, other, keys_t) = refs[:-5], refs[-5:]
    state[...] = before[...]
    other[...] = other_before[...]
    for index, kv_ref in zip(indices, kv_refs):

        @pl.when((seen_ref[0, index] > 0) | (seen_ref[1, index] > 0))
        def _():
            keys_t[...] = kv_ref[: q_ref.shape[0], :DH].T

        @pl.when(seen_ref[0, index] > 0)
        def _():
            add_block(q_ref, keys_t[...], kv_ref[: q_ref.shape[0], DH:], state)

        @pl.when(seen_ref[1, index] > 0)
        def _():
            add_block(other_q_ref, keys_t[...], kv_ref[: q_ref.shape[0], DH:], other)


def fetch(slot, riders, target, sem):
    for k, ref in enumerate(riders):

        @pl.when(slot == k)
        def _():
            load = pltpu.make_async_copy(ref.at[pl.ds(ref.shape[0] - target.shape[0], target.shape[0]), :], target, sem)
            load.start()
            load.wait()


def end_kernel(seen_ref, slot_ref, q_ref, kv_ref, before, *refs, which, index):
    riders, (packed, state, keys_t, rider, sem) = refs[:-5], refs[-5:]
    rows = q_ref.shape[0]
    state[...] = before[...]

    @pl.when(seen_ref[which, index] > 0)
    def _():
        keys_t[...] = kv_ref[:rows, :DH].T
        add_block(q_ref, keys_t[...], kv_ref[:rows, DH:], state)

    packed[:rows, :DH] = state[:, :DH]
    lane = lax.broadcasted_iota(jnp.int32, (rows, DH), 1)
    packed[:rows, DH:] = jnp.where(lane < DH // 2, state[:, DH : 2 * DH], state[:, 2 * DH :])
    if riders:
        rider[...] = jnp.zeros(rider.shape, rider.dtype)
        fetch(slot_ref[which], riders, rider, sem)
        packed[rows:, :] = rider[...].astype(jnp.float32)


def merge_kernel(slot_ref, mine_ref, other_ref, *refs):
    riders, (out, short_out, rider, sem) = refs[:-4], refs[-4:]
    total = out.shape[0]
    rider[...] = other_ref[total:, :].astype(jnp.bfloat16)
    fetch(slot_ref[0], riders, rider, sem)
    half = rider.shape[0]
    short_out[:half, :] = rider[:, :DH]
    short_out[half:, :] = rider[:, DH:]
    for start in range(0, total, TILE):
        rows = pl.ds(start, TILE)
        mine = mine_ref[rows, 2 * DH - 1 :]
        other = other_ref[rows, 2 * DH - 1 :]
        top = jnp.maximum(mine, other)
        mine = jnp.exp2((mine - top) * GAIN)
        other = jnp.exp2((other - top) * GAIN)
        sums = mine_ref[rows, :DH] * mine + other_ref[rows, :DH] * other
        weight = mine_ref[rows, DH : DH + 1] * mine + other_ref[rows, DH : DH + 1] * other
        out[rows, :] = (sums / weight).astype(jnp.bfloat16)


def load_kernel(lengths_ref, q_ref, kv_ref, own_ref, out_ref):
    out_ref[: own_ref.shape[0], :] = own_ref[...]
    half = q_ref.shape[0] // 2
    ends = []
    total = 0
    for k in range(lengths_ref.shape[0]):
        total = total + lengths_ref[k]
        ends.append(total)
    for start in range(0, q_ref.shape[0], SHORT_TILE):
        rows = pl.ds(start, SHORT_TILE)
        seen = start + SHORT_TILE
        scores = scores_of(q_ref[rows, :], kv_ref[:seen, :DH])
        row = start + lax.broadcasted_iota(jnp.int32, (SHORT_TILE, 1), 0)
        first = jnp.zeros((SHORT_TILE, 1), jnp.int32)
        for end in ends:
            first = jnp.where(row >= end, end, first)
        col = lax.broadcasted_iota(jnp.int32, scores.shape, 1)
        scores = jnp.where((col <= row) & (col >= first), scores, -jnp.inf)
        top = jnp.max(scores, axis=1, keepdims=True)
        weights = jnp.exp2((scores - top) * GAIN)
        acc = weigh(weights, kv_ref[:seen, DH:])
        columns = slice(0, DH) if start < half else slice(DH, 2 * DH)
        place = pl.ds(own_ref.shape[0] + start % half, SHORT_TILE)
        out_ref[place, columns] = (acc[:, :DH] / acc[:, DH:]).astype(jnp.bfloat16)


def call(kernel, out_shape, operands, name, scratch=(), left=0):
    specs = [SMEM_SPEC if x.dtype == jnp.int32 else VMEM_SPEC for x in operands]
    return pl.pallas_call(
        kernel,
        out_shape=out_shape,
        in_specs=specs[: len(specs) - left] + [pl.BlockSpec(memory_space=pl.ANY)] * left,
        out_specs=jax.tree.map(lambda _: VMEM_SPEC, out_shape),
        scratch_shapes=scratch,
        compiler_params=pltpu.CompilerParams(vmem_limit_bytes=VMEM),
        cost_estimate=pl.CostEstimate(flops=1, bytes_accessed=1, transcendentals=0),
        name=name,
    )(*operands)


def state_of(rows, width=3 * DH):
    return jax.ShapeDtypeStruct((rows, width), jnp.float32)


def heads_kernel(short_keys, short_values, keys, values, out):
    cut = short_keys.shape[0]
    copies = out.shape[0] // KVH
    for head in range(KVH):
        columns = slice(head * DH, (head + 1) * DH)
        block = jnp.concatenate(
            [
                jnp.concatenate([short_keys[:, columns], short_values[:, columns]], axis=1),
                jnp.concatenate([keys[:, columns], values[:, columns]], axis=1),
            ],
            axis=0,
        )
        for copy in range(copies):
            out[head * copies + copy] = block


def swapped(blocks, axis):
    return lax.all_to_all(blocks, axis, split_axis=0, concat_axis=0, tiled=True)


def across(block):
    return lax.ppermute(block, "inst", [(i, i ^ 1) for i in range(lax.axis_size("inst"))])


def ahead(block):
    size = lax.axis_size("inst")
    step = lambda i: CORES if i % CORES == 0 else -CORES
    return lax.ppermute(block, "inst", [(i, (i + step(i)) % size) for i in range(size)])


def body(
    prompt_queries,
    prompt_keys,
    prompt_values,
    span_of,
    short_queries,
    short_keys,
    short_values,
    short_lengths,
    pair_partner,
):
    groups = lax.axis_size("inst")
    chips = groups // CORES
    me = lax.axis_index("inst")
    rows = prompt_queries.shape[1]
    short_rows = short_queries.shape[1]
    queries = prompt_queries[0]

    cut = short_keys.shape[1]
    heads = pl.pallas_call(
        heads_kernel,
        out_shape=jax.ShapeDtypeStruct(
            (lax.axis_size("sp"), cut + prompt_keys.shape[1], 2 * DH), jnp.bfloat16
        ),
        name="heads",
    )(short_keys[0], short_values[0], prompt_keys[0], prompt_values[0])
    got = swapped(heads, "sp")
    short_own = got[:, :cut].reshape(short_rows, 2 * DH)
    own = got[:, cut:].reshape(rows, 2 * DH)
    own, short_own, other_queries = lax.optimization_barrier((own, short_own, across(queries)))
    load = call(
        load_kernel,
        jax.ShapeDtypeStruct((rows + short_rows // 2, 2 * DH), jnp.bfloat16),
        (short_lengths[me], short_queries[0], short_own, own),
        "load",
    )
    ring = [(load, across(load))]
    for step in range(1, chips // 2):
        ring.append(tuple(ahead(block) for block in ring[-1]))
    end = ahead(ring[-1][0])
    core = me % CORES
    chip = me // CORES + jnp.asarray(range(chips // 2 + 1), jnp.int32) * (2 * core - 1)
    held = (chip % chips * CORES)[:, None] + jnp.stack([core, 1 - core])[None, :]
    held = held.reshape(-1)
    ids = jnp.arange(groups, dtype=jnp.int32)
    spans = jnp.sum(jnp.where(held[:, None] == ids[None, :], span_of[None, :], 0), axis=1)
    mine = jnp.stack([span_of[me], span_of[me ^ 1]])
    seen = (spans[None, :] < mine[:, None]).astype(jnp.int32)

    riders = [block for pair in ring for block in pair] + [end]
    wanted = jnp.stack([pair_partner[me], pair_partner[me ^ 1]])
    found = held[None, : len(riders)] == wanted[:, None]
    slots = jnp.arange(len(riders), dtype=jnp.int32)
    slot = jnp.min(jnp.where(found, slots[None, :], len(riders)), axis=1)

    keys_t = pltpu.VMEM((DH, rows), jnp.bfloat16)
    both = (state_of(rows), state_of(rows))

    def ring_step(step, state, other):
        return call(
            functools.partial(ring_kernel, indices=(2 * step, 2 * step + 1)),
            both,
            (seen, queries, other_queries, *ring[step], state, other),
            "ring",
            [keys_t],
        )

    state, other = call(own_kernel, both, (seen, queries, other_queries, load), "own", [keys_t])
    for step in range(1, chips // 2):
        state, other = ring_step(step, state, other)

    rider_space = [pltpu.VMEM((short_rows // 2, 2 * DH), jnp.bfloat16), pltpu.SemaphoreType.DMA]
    end_space = [pltpu.VMEM((rows, 3 * DH), jnp.float32), keys_t] + rider_space

    def ending(which, q, before, riders):
        return call(
            functools.partial(end_kernel, which=which, index=chips),
            state_of(rows + (short_rows // 2 if riders else 0), 2 * DH),
            (seen, slot, q, end, before, *riders),
            "end",
            end_space,
            len(riders),
        )

    other = across(ending(1, other_queries, other, riders))
    state = ending(0, queries, state, [])
    prompt_out, short_out = call(
        merge_kernel,
        (jax.ShapeDtypeStruct((rows, DH), jnp.bfloat16), jax.ShapeDtypeStruct((short_rows, DH), jnp.bfloat16)),
        (slot, state, other, *riders),
        "merge",
        rider_space,
        len(riders),
    )
    return (prompt_out[None], short_out[None])


def solution(mesh):
    placed = (
        P("inst", None, "sp"),
        P("inst", "sp", None),
        P("inst", "sp", None),
        P(),
        P("inst", None, "sp"),
        P("inst", "sp", None),
        P("inst", "sp", None),
        P(),
        P(),
    )
    return jax.shard_map(
        body,
        mesh=mesh,
        in_specs=placed,
        out_specs=(P("inst", None, "sp"), P("inst", None, "sp")),
        check_vma=False,
    )
```

time: 122 us -> 112 us (0.918); the launches traced: 122 us -> 110 us
  starting transfers between devices: 25 us -> 60.4 us
  blocking collectives: 22.1 us -> 0 us
  between operations: 14.8 us -> 1.08 us
  local copies, waits for them, and re-layouts: 10.3 us -> 4.36 us
  Pallas kernels: 25.4 us -> 21 us
  waiting for transfers between devices: 22.1 us -> 18.6 us
  other arithmetic: 2.1 us -> 4.64 us
    ppermute x0 -> x10, starting transfers between devices: none -> 49.8 us  [the longest x7 35.7 us: ahead(): lax.ppermute(block, 'inst', [(i, (i + step(i)) % size) for i in range(siz...]
    all_to_all x1 -> x0, blocking collectives: 22.1 us -> none  [swapped(): return lax.all_to_all(blocks, axis, split_axis=0, concat_axis=0, tiled=True)]
    all_to_all x3 -> x1, starting transfers between devices: 25 us -> 10.6 us  [swapped(): return lax.all_to_all(blocks, axis, split_axis=0, concat_axis=0, tiled=True)]
    all_to_all x3 -> x1, waiting for transfers between devices: 22 us -> 13.3 us  [swapped(): return lax.all_to_all(blocks, axis, split_axis=0, concat_axis=0, tiled=True)]
    ppermute x0 -> x10, waiting for transfers between devices: none -> 5.28 us  [the longest x7 4.86 us: ahead(): lax.ppermute(block, 'inst', [(i, (i + step(i)) % size) for i in range(siz...]
    pallas_call x4 -> x9, Pallas kernels: 25.4 us -> 21 us  [the longest x8 19.3 us: call(): pl.pallas_call(kernel, out_shape=out_shape, in_specs=specs[:len(specs) -...]
    another operation x4 -> x0, local copies, waits for them, and re-layouts: 2.96 us -> none  [the longest x2 1.48 us: by_head(): values.reshape(rows, KVH, DH)]
    another operation x0 -> x3, other arithmetic: none -> 2.81 us  [the longest x1 1.41 us: body(): mine = jnp.stack([span_of[me], span_of[me ^ 1]])]
  transfers between devices with their start and end apart: 4 -> 11, of which waited for: 3 -> 6; matrix products, arithmetic and copies ran while one was open for 5% -> 6% of each run, Pallas kernels for 4% -> 11%
where the time goes in v2:
time: 112 us; the launch traced here: 110 us
  starting transfers between devices  60.4 us (54%)
  Pallas kernels  21 us (19%)
  waiting for transfers between devices  18.6 us (17%)
  other arithmetic  4.64 us (4%)
  local copies, waits for them, and re-layouts  4.36 us (4%)
    ppermute x7, starting transfers between devices, ahead(): lax.ppermute(block, 'inst', [(i, (i + step(i)) % size) for i in range(siz...  35.7 us
    pallas_call x8, Pallas kernels, call(): pl.pallas_call(kernel, out_shape=out_shape, in_specs=specs[:len(specs) -...  19.3 us
    ppermute x3, starting transfers between devices, across(): lax.ppermute(block, 'inst', [(i, i ^ 1) for i in range(lax.axis_size('ins...  14.1 us
    all_to_all x1, waiting for transfers between devices, swapped(): return lax.all_to_all(blocks, axis, split_axis=0, concat_axis=0, tiled=True)  13.3 us
    all_to_all x1, starting transfers between devices, swapped(): return lax.all_to_all(blocks, axis, split_axis=0, concat_axis=0, tiled=True)  10.6 us
    ppermute x7, waiting for transfers between devices, ahead(): lax.ppermute(block, 'inst', [(i, (i + step(i)) % size) for i in range(siz...  4.86 us
    unnamed x18, local copies, waits for them, and re-layouts  2.87 us
  transfers between devices with their start and end apart: 11, of which 6 were waited for; matrix products, arithmetic and copies ran while one was open for 6% of the time, Pallas kernels for 11%

profile of v2, /device:TPU:1, one launch (start us, length us, event | category | flops | bytes accessed | tf_op | source)
XLA Modules:
  0.0 110.1 jit_solution(16079446701081170948)
XLA Ops:
  0.7 1.7 %heads.1 = bf16[32,40,256]{2,1,0:T(8,128)(2,1)} custom-call(bf16[16,512]{1,0:T(8,128)(2,1)} %bitcast.24, bf16[16,512]{1,0:T(8,128)(2,1)} %bitcast.25, bf16[24,512]{1,0:T(8,128)(2,1)} %bitcast.22, bf16[24,512]{1,0:T(8,128)(2,1)} %bitcast.23), custom_call_target="tpu_custom_call" | custom-call | tf_op jit(solution)/shard_map/heads/pallas_call | solution.py:239
  2.4 10.6 %all-to-all-start = ((bf16[32,40,256]{2,1,0:T(8,128)(2,1)}), bf16[32,40,256]{2,1,0:T(8,128)(2,1)S(1)}, u32[]{:S(2)}, u32[]{:S(2)}) async-start(bf16[32,40,256]{2,1,0:T(8,128)(2,1)} %heads.1), calls=%async_computation | async-start | bytes 1310720 | tf_op jit(solution)/shard_map/all_to_all | solution.py:207
  13.0 2.9 %collective-permute-start = (bf16[768,128]{1,0:T(8,128)(2,1)S(1)}, bf16[768,128]{1,0:T(8,128)(2,1)S(1)}, u32[]{:S(2)}, u32[]{:S(2)}) collective-permute-start(bf16[768,128]{1,0:T(8,128)(2,1)S(1)} %bitcast.13), channel_id=1, source_target_pairs={{0,32},{32,0},{64,96},{96,64},{128,160},{160,128},{192,224},{224,1... | collective-permute-start | bytes 589832 | tf_op jit(solution)/shard_map/ppermute | solution.py:211
  16.1 13.3 %all-to-all-done = bf16[32,40,256]{2,1,0:T(8,128)(2,1)S(1)} async-done(((bf16[32,40,256]{2,1,0:T(8,128)(2,1)}), bf16[32,40,256]{2,1,0:T(8,128)(2,1)S(1)}, u32[]{:S(2)}, u32[]{:S(2)}) %all-to-all-start) | async-done | bytes 655392 | tf_op jit(solution)/shard_map/all_to_all | solution.py:207
  29.5 1.4 %load.1.kv_ref.refs_0_ = bf16[1024,256]{1,0:T(8,128)(2,1)S(1)} custom-call(s32[8]{0:T(128)S(1)} %dynamic-slice_reduce_fusion.lengths_ref, bf16[512,128]{1,0:T(8,128)(2,1)S(1)} %bitcast.21, bf16[512,256]{1,0:T(8,128)(2,1)S(1)} %bitcast.20, bf16[768,256]{1,0:T(8,128)(2,1)S(1)} %bitcast.19), custom_call_target="tpu_custom_call" | custom-call | flops 1 | bytes 1 | tf_op jit(solution)/shard_map/load/pallas_call | solution.py:174
  30.9 6.9 %collective-permute-start.5 = (bf16[1024,256]{1,0:T(8,128)(2,1)S(1)}, bf16[1024,256]{1,0:T(8,128)(2,1)S(1)}, u32[]{:S(2)}, u32[]{:S(2)}) collective-permute-start(bf16[1024,256]{1,0:T(8,128)(2,1)S(1)} %load.1.kv_ref.refs_0_), channel_id=1, source_target_pairs={{0,32},{32,0},{64,96},{96,64},{128,160},{160,128},{192,224},{224,1... | collective-permute-start | bytes 1572872 | tf_op jit(solution)/shard_map/ppermute | solution.py:211
  37.8 10.7 %collective-permute-start.1 = (bf16[1024,256]{1,0:T(8,128)(2,1)S(1)}, bf16[1024,256]{1,0:T(8,128)(2,1)S(1)}, u32[]{:S(2)}, u32[]{:S(2)}) collective-permute-start(bf16[1024,256]{1,0:T(8,128)(2,1)S(1)} %load.1.kv_ref.refs_0_), channel_id=1, source_target_pairs={{0,64},{32,480},{64,128},{96,32},{128,192},{160,96},{192,256},{224... | collective-permute-start | bytes 1572872 | tf_op jit(solution)/shard_map/ppermute | solution.py:217
  48.5 2.2 %collective-permute-start.6 = (bf16[1024,256]{1,0:T(8,128)(2,1)S(1)}, bf16[1024,256]{1,0:T(8,128)(2,1)S(1)}, u32[]{:S(2)}, u32[]{:S(2)}) collective-permute-start(bf16[1024,256]{1,0:T(8,128)(2,1)S(1)} %collective-permute-done.5.refs_1_), channel_id=1, source_target_pairs={{0,64},{32,480},{64,128},{96,32},{128,192},{160,96},{192,256},{224... | collective-permute-start | bytes 1572872 | tf_op jit(solution)/shard_map/ppermute | solution.py:217
  50.7 0.8 copy-done.2
  51.5 3.1 %collective-permute-done.1.refs_0_.refs_2_ = bf16[1024,256]{1,0:T(8,128)(2,1)S(1)} collective-permute-done((bf16[1024,256]{1,0:T(8,128)(2,1)S(1)}, bf16[1024,256]{1,0:T(8,128)(2,1)S(1)}, u32[]{:S(2)}, u32[]{:S(2)}) %collective-permute-start.1) | collective-permute-done | bytes 524320 | tf_op jit(solution)/shard_map/ppermute | solution.py:217
  54.6 5.0 %collective-permute-start.2 = (bf16[1024,256]{1,0:T(8,128)(2,1)S(1)}, bf16[1024,256]{1,0:T(8,128)(2,1)S(1)}, u32[]{:S(2)}, u32[]{:S(2)}) collective-permute-start(bf16[1024,256]{1,0:T(8,128)(2,1)S(1)} %collective-permute-done.1.refs_0_.refs_2_), channel_id=1, source_target_pairs={{0,64},{32,480},{64,128},{96,32},{128,192},{160,96},{192,256},{224... | collective-permute-start | bytes 1572872 | tf_op jit(solution)/shard_map/ppermute | solution.py:217
  60.2 5.0 %collective-permute-start.7 = (bf16[1024,256]{1,0:T(8,128)(2,1)S(1)}, bf16[1024,256]{1,0:T(8,128)(2,1)S(1)}, u32[]{:S(2)}, u32[]{:S(2)}) collective-permute-start(bf16[1024,256]{1,0:T(8,128)(2,1)S(1)} %collective-permute-done.6.refs_1_.refs_3_), channel_id=1, source_target_pairs={{0,64},{32,480},{64,128},{96,32},{128,192},{160,96},{192,256},{224... | collective-permute-start | bytes 1572872 | tf_op jit(solution)/shard_map/ppermute | solution.py:217
  65.2 0.6 collective-permute-done.2.refs_0_.refs_4_
  65.8 5.0 %collective-permute-start.3 = (bf16[1024,256]{1,0:T(8,128)(2,1)S(1)}, bf16[1024,256]{1,0:T(8,128)(2,1)S(1)}, u32[]{:S(2)}, u32[]{:S(2)}) collective-permute-start(bf16[1024,256]{1,0:T(8,128)(2,1)S(1)} %collective-permute-done.2.refs_0_.refs_4_), channel_id=1, source_target_pairs={{0,64},{32,480},{64,128},{96,32},{128,192},{160,96},{192,256},{224... | collective-permute-start | bytes 1572872 | tf_op jit(solution)/shard_map/ppermute | solution.py:217
  71.6 0.7 fusion.3
  72.3 1.4 %pad_add_fusion.2 = s32[2]{0:T(128)S(1)} fusion(s32[1]{0:T(128)} %get-tuple-element.29, s32[1]{0:T(128)} %get-tuple-element.28), kind=kLoop, calls=%fused_computation.14 | loop fusion | flops 2 | bytes 16 | tf_op jit(solution)/shard_map/stack | solution.py:266
  73.7 2.8 %collective-permute-start.8 = (bf16[1024,256]{1,0:T(8,128)(2,1)S(1)}, bf16[1024,256]{1,0:T(8,128)(2,1)S(1)}, u32[]{:S(2)}, u32[]{:S(2)}) collective-permute-start(bf16[1024,256]{1,0:T(8,128)(2,1)S(1)} %collective-permute-done.7.refs_1_.refs_5_), channel_id=1, source_target_pairs={{0,64},{32,480},{64,128},{96,32},{128,192},{160,96},{192,256},{224... | collective-permute-start | bytes 1572872 | tf_op jit(solution)/shard_map/ppermute | solution.py:217
  76.4 0.6 collective-permute-done.3.refs_0_.refs_6_
  77.0 5.0 %collective-permute-start.4 = (bf16[1024,256]{1,0:T(8,128)(2,1)S(1)}, bf16[1024,256]{1,0:T(8,128)(2,1)S(1)}, u32[]{:S(2)}, u32[]{:S(2)}) collective-permute-start(bf16[1024,256]{1,0:T(8,128)(2,1)S(1)} %collective-permute-done.3.refs_0_.refs_6_), channel_id=1, source_target_pairs={{0,64},{32,480},{64,128},{96,32},{128,192},{160,96},{192,256},{224... | collective-permute-start | bytes 1572872 | tf_op jit(solution)/shard_map/ppermute | solution.py:217
  82.1 1.3 %pad_add_fusion.1 = s32[2]{0:T(128)S(1)} fusion(s32[1]{0:T(128)} %get-tuple-element.32, s32[1]{0:T(128)} %get-tuple-element.33), kind=kLoop, calls=%fused_computation.13 | loop fusion | flops 2 | bytes 16 | tf_op jit(solution)/shard_map/stack | solution.py:270
  83.4 0.8 select_reduce_fusion
  84.2 0.8 fusion.slot_ref
  85.1 1.8 %own.1 = (f32[768,384]{1,0:T(8,128)S(1)}, f32[768,384]{1,0:T(8,128)S(1)}) custom-call(s32[2,10]{1,0:T(2,128)S(1)} %compare_convert_fusion.seen_ref, bf16[768,128]{1,0:T(8,128)(2,1)S(1)} %bitcast.14, bf16[768,128]{1,0:T(8,128)(2,1)S(1)} %collective-permute-done.other_q_ref.q_ref, bf16[1024,256]{1,0:T(8,128)(2,1)S(1)} %load.1.kv_ref.refs_0_), custom_call_target="tpu_custom_call" | custom-call | flops 1 | bytes 1 | tf_op jit(solution)/shard_map/own/pallas_call | solution.py:174
  87.0 3.1 %ring.3 = (f32[768,384]{1,0:T(8,128)S(1)}, f32[768,384]{1,0:T(8,128)S(1)}) custom-call(s32[2,10]{1,0:T(2,128)S(1)} %compare_convert_fusion.seen_ref, bf16[768,128]{1,0:T(8,128)(2,1)S(1)} %bitcast.15, bf16[768,128]{1,0:T(8,128)(2,1)S(1)} %collective-permute-done.other_q_ref.q_ref, bf16[1024,256]{1,0:T(8,128)(2,1)S(1)} %collective-permute-done.1.refs_0_.refs_2_, ...), custom_call_target="tpu_custom_call" | custom-call | flops 1 | bytes 1 | tf_op jit(solution)/shard_map/ring/pallas_call | solution.py:174
  90.1 3.3 %ring.4 = (f32[768,384]{1,0:T(8,128)S(1)}, f32[768,384]{1,0:T(8,128)S(1)}) custom-call(s32[2,10]{1,0:T(2,128)S(1)} %compare_convert_fusion.seen_ref, bf16[768,128]{1,0:T(8,128)(2,1)S(1)} %bitcast.16, bf16[768,128]{1,0:T(8,128)(2,1)S(1)} %collective-permute-done.other_q_ref.q_ref, bf16[1024,256]{1,0:T(8,128)(2,1)S(1)} %collective-permute-done.2.refs_0_.refs_4_, ...), custom_call_target="tpu_custom_call" | custom-call | flops 1 | bytes 1 | tf_op jit(solution)/shard_map/ring/pallas_call | solution.py:174
  93.4 1.9 %ring.5 = (f32[768,384]{1,0:T(8,128)S(1)}, f32[768,384]{1,0:T(8,128)S(1)}) custom-call(s32[2,10]{1,0:T(2,128)S(1)} %compare_convert_fusion.seen_ref, bf16[768,128]{1,0:T(8,128)(2,1)S(1)} %bitcast.17, bf16[768,128]{1,0:T(8,128)(2,1)S(1)} %collective-permute-done.other_q_ref.q_ref, bf16[1024,256]{1,0:T(8,128)(2,1)S(1)} %collective-permute-done.3.refs_0_.refs_6_, ...), custom_call_target="tpu_custom_call" | custom-call | flops 1 | bytes 1 | tf_op jit(solution)/shard_map/ring/pallas_call | solution.py:174
  95.4 1.0 copy-done.4
  96.4 2.6 %end.3 = f32[1024,256]{1,0:T(8,128)S(1)} custom-call(s32[2,10]{1,0:T(2,128)S(1)} %compare_convert_fusion.seen_ref, s32[2]{0:T(128)S(1)} %fusion.slot_ref, bf16[768,128]{1,0:T(8,128)(2,1)S(1)} %collective-permute-done.other_q_ref.q_ref, bf16[1024,256]{1,0:T(8,128)(2,1)S(1)} %collective-permute-done.4.kv_ref.refs_8_, f32[768,384]{1,0:T(8,128)} %copy-done.4, ...), custom_call_target="tpu_custom_call" | custom-call | flops 1 | bytes 1 | tf_op jit(solution)/shard_map/end/pallas_call | solution.py:174
  99.1 4.3 %collective-permute-start.9 = (f32[1024,256]{1,0:T(8,128)S(1)}, f32[1024,256]{1,0:T(8,128)S(1)}, u32[]{:S(2)}, u32[]{:S(2)}) collective-permute-start(f32[1024,256]{1,0:T(8,128)S(1)} %end.3), channel_id=1, source_target_pairs={{0,32},{32,0},{64,96},{96,64},{128,160},{160,128},{192,224},{224,1... | collective-permute-start | bytes 3145736 | tf_op jit(solution)/shard_map/ppermute | solution.py:211
  103.4 1.8 %end.2.mine_ref = f32[768,256]{1,0:T(8,128)S(1)} custom-call(s32[2,10]{1,0:T(2,128)S(1)} %compare_convert_fusion.seen_ref, s32[2]{0:T(128)S(1)} %fusion.slot_ref, bf16[768,128]{1,0:T(8,128)(2,1)S(1)} %bitcast.18, bf16[1024,256]{1,0:T(8,128)(2,1)S(1)} %collective-permute-done.4.kv_ref.refs_8_, f32[768,384]{1,0:T(8,128)S(1)} %get-tuple-element.24.before), custom_call_target="tpu_custom_call" | custom-call | flops 1 | bytes 1 | tf_op jit(solution)/shard_map/end/pallas_call | solution.py:174
  105.7 1.0 copy-done.6
  106.7 3.3 %merge.1 = (bf16[768,128]{1,0:T(8,128)(2,1)}, bf16[512,128]{1,0:T(8,128)(2,1)}) custom-call(s32[2]{0:T(128)S(1)} %fusion.slot_ref, f32[768,256]{1,0:T(8,128)S(1)} %end.2.mine_ref, f32[1024,256]{1,0:T(8,128)} %copy-done.6, bf16[1024,256]{1,0:T(8,128)(2,1)S(1)} %load.1.kv_ref.refs_0_, bf16[1024,256]{1,0:T(8,128)(2,1)S(1)} %copy-done.3, ...), custom_call_target="tpu_custom_call" | custom-call | flops 1 | bytes 1 | tf_op jit(solution)/shard_map/merge/pallas_call | solution.py:174
  (30 shorter events, 2.1 us)
Async XLA Ops:
  0.6 15.3 %copy-start = (s32[16,8]{0,1:T(8,128)S(1)}, s32[16,8]{0,1:T(8,128)}, u32[]{:S(2)}) copy-start(s32[16,8]{0,1:T(8,128)} %param.17) | copy-start | bytes 1540
  0.6 12.4 %copy-start.1 = (bf16[1,768,128]{2,1,0:T(8,128)(2,1)S(1)}, bf16[1,768,128]{2,1,0:T(8,128)(2,1)}, u32[]{:S(2)}) copy-start(bf16[1,768,128]{2,1,0:T(8,128)(2,1)} %param.10) | copy-start | bytes 589828
  2.4 27.1 %copy-start.5 = (bf16[1,512,128]{2,1,0:T(8,128)(2,1)S(1)}, bf16[1,512,128]{2,1,0:T(8,128)(2,1)}, u32[]{:S(2)}) copy-start(bf16[1,512,128]{2,1,0:T(8,128)(2,1)} %param.14) | copy-start | bytes 393220
  2.4 27.0 %all-to-all-start = ((bf16[32,40,256]{2,1,0:T(8,128)(2,1)}), bf16[32,40,256]{2,1,0:T(8,128)(2,1)S(1)}, u32[]{:S(2)}, u32[]{:S(2)}) async-start(bf16[32,40,256]{2,1,0:T(8,128)(2,1)} %heads.1), calls=%async_computation | async-start | bytes 1310720 | tf_op jit(solution)/shard_map/all_to_all | solution.py:207
  13.0 16.4 %collective-permute-start = (bf16[768,128]{1,0:T(8,128)(2,1)S(1)}, bf16[768,128]{1,0:T(8,128)(2,1)S(1)}, u32[]{:S(2)}, u32[]{:S(2)}) collective-permute-start(bf16[768,128]{1,0:T(8,128)(2,1)S(1)} %bitcast.13), channel_id=1, source_target_pairs={{0,32},{32,0},{64,96},{96,64},{128,160},{160,128},{192,224},{224,1... | collective-permute-start | bytes 589832 | tf_op jit(solution)/shard_map/ppermute | solution.py:211
  16.1 55.5 %copy-start.7 = (s32[16]{0:T(128)S(1)}, s32[16]{0:T(128)}, u32[]{:S(2)}) copy-start(s32[16]{0:T(128)} %param.18) | copy-start | bytes 196
  16.1 55.5 %copy-start.8 = (s32[16]{0:T(128)S(1)}, s32[16]{0:T(128)}, u32[]{:S(2)}) copy-start(s32[16]{0:T(128)} %param.13) | copy-start | bytes 196
  30.9 17.6 %collective-permute-start.5 = (bf16[1024,256]{1,0:T(8,128)(2,1)S(1)}, bf16[1024,256]{1,0:T(8,128)(2,1)S(1)}, u32[]{:S(2)}, u32[]{:S(2)}) collective-permute-start(bf16[1024,256]{1,0:T(8,128)(2,1)S(1)} %load.1.kv_ref.refs_0_), channel_id=1, source_target_pairs={{0,32},{32,0},{64,96},{96,64},{128,160},{160,128},{192,224},{224,1... | collective-permute-start | bytes 1572872 | tf_op jit(solution)/shard_map/ppermute | solution.py:211
  37.8 16.8 %collective-permute-start.1 = (bf16[1024,256]{1,0:T(8,128)(2,1)S(1)}, bf16[1024,256]{1,0:T(8,128)(2,1)S(1)}, u32[]{:S(2)}, u32[]{:S(2)}) collective-permute-start(bf16[1024,256]{1,0:T(8,128)(2,1)S(1)} %load.1.kv_ref.refs_0_), channel_id=1, source_target_pairs={{0,64},{32,480},{64,128},{96,32},{128,192},{160,96},{192,256},{224... | collective-permute-start | bytes 1572872 | tf_op jit(solution)/shard_map/ppermute | solution.py:217
  48.5 11.7 %collective-permute-start.6 = (bf16[1024,256]{1,0:T(8,128)(2,1)S(1)}, bf16[1024,256]{1,0:T(8,128)(2,1)S(1)}, u32[]{:S(2)}, u32[]{:S(2)}) collective-permute-start(bf16[1024,256]{1,0:T(8,128)(2,1)S(1)} %collective-permute-done.5.refs_1_), channel_id=1, source_target_pairs={{0,64},{32,480},{64,128},{96,32},{128,192},{160,96},{192,256},{224... | collective-permute-start | bytes 1572872 | tf_op jit(solution)/shard_map/ppermute | solution.py:217
  50.7 0.8 copy-start.2
  54.6 11.2 %collective-permute-start.2 = (bf16[1024,256]{1,0:T(8,128)(2,1)S(1)}, bf16[1024,256]{1,0:T(8,128)(2,1)S(1)}, u32[]{:S(2)}, u32[]{:S(2)}) collective-permute-start(bf16[1024,256]{1,0:T(8,128)(2,1)S(1)} %collective-permute-done.1.refs_0_.refs_2_), channel_id=1, source_target_pairs={{0,64},{32,480},{64,128},{96,32},{128,192},{160,96},{192,256},{224... | collective-permute-start | bytes 1572872 | tf_op jit(solution)/shard_map/ppermute | solution.py:217
  60.2 13.5 %collective-permute-start.7 = (bf16[1024,256]{1,0:T(8,128)(2,1)S(1)}, bf16[1024,256]{1,0:T(8,128)(2,1)S(1)}, u32[]{:S(2)}, u32[]{:S(2)}) collective-permute-start(bf16[1024,256]{1,0:T(8,128)(2,1)S(1)} %collective-permute-done.6.refs_1_.refs_3_), channel_id=1, source_target_pairs={{0,64},{32,480},{64,128},{96,32},{128,192},{160,96},{192,256},{224... | collective-permute-start | bytes 1572872 | tf_op jit(solution)/shard_map/ppermute | solution.py:217
  65.8 11.2 %collective-permute-start.3 = (bf16[1024,256]{1,0:T(8,128)(2,1)S(1)}, bf16[1024,256]{1,0:T(8,128)(2,1)S(1)}, u32[]{:S(2)}, u32[]{:S(2)}) collective-permute-start(bf16[1024,256]{1,0:T(8,128)(2,1)S(1)} %collective-permute-done.2.refs_0_.refs_4_), channel_id=1, source_target_pairs={{0,64},{32,480},{64,128},{96,32},{128,192},{160,96},{192,256},{224... | collective-permute-start | bytes 1572872 | tf_op jit(solution)/shard_map/ppermute | solution.py:217
  73.7 19.7 %collective-permute-start.8 = (bf16[1024,256]{1,0:T(8,128)(2,1)S(1)}, bf16[1024,256]{1,0:T(8,128)(2,1)S(1)}, u32[]{:S(2)}, u32[]{:S(2)}) collective-permute-start(bf16[1024,256]{1,0:T(8,128)(2,1)S(1)} %collective-permute-done.7.refs_1_.refs_5_), channel_id=1, source_target_pairs={{0,64},{32,480},{64,128},{96,32},{128,192},{160,96},{192,256},{224... | collective-permute-start | bytes 1572872 | tf_op jit(solution)/shard_map/ppermute | solution.py:217
  77.0 19.4 %collective-permute-start.4 = (bf16[1024,256]{1,0:T(8,128)(2,1)S(1)}, bf16[1024,256]{1,0:T(8,128)(2,1)S(1)}, u32[]{:S(2)}, u32[]{:S(2)}) collective-permute-start(bf16[1024,256]{1,0:T(8,128)(2,1)S(1)} %collective-permute-done.3.refs_0_.refs_6_), channel_id=1, source_target_pairs={{0,64},{32,480},{64,128},{96,32},{128,192},{160,96},{192,256},{224... | collective-permute-start | bytes 1572872 | tf_op jit(solution)/shard_map/ppermute | solution.py:217
  93.4 3.0 %copy-start.3 = (bf16[1024,256]{1,0:T(8,128)(2,1)S(1)}, bf16[1024,256]{1,0:T(8,128)(2,1)}, u32[]{:S(2)}) copy-start(bf16[1024,256]{1,0:T(8,128)(2,1)} %copy-done.2) | copy-start | bytes 1572868
  95.4 1.1 copy-start.4
  99.1 6.6 %collective-permute-start.9 = (f32[1024,256]{1,0:T(8,128)S(1)}, f32[1024,256]{1,0:T(8,128)S(1)}, u32[]{:S(2)}, u32[]{:S(2)}) collective-permute-start(f32[1024,256]{1,0:T(8,128)S(1)} %end.3), channel_id=1, source_target_pairs={{0,32},{32,0},{64,96},{96,64},{128,160},{160,128},{192,224},{224,1... | collective-permute-start | bytes 3145736 | tf_op jit(solution)/shard_map/ppermute | solution.py:211
  105.7 1.0 copy-start.6

commit v3 on v2

--- a/solution.py
+++ b/solution.py
@@ -15,7 +15,8 @@
 SHORT_TILE = 256
 LOG2E = 1.4426950408889634
 GAIN = DH ** (-0.5) * LOG2E
-VMEM = 48 * 1024 * 1024
+VMEM = 24 * 1024 * 1024
+COST = {"load": 10**9, "own": 2 * 10**9, "ring": 4 * 10**9, "end": 10**9, "merge": 10**9}
 SMEM_SPEC = pl.BlockSpec(memory_space=pltpu.SMEM)
 VMEM_SPEC = pl.BlockSpec(memory_space=pltpu.VMEM)
 
@@ -143,22 +144,17 @@
         out[rows, :] = (sums / weight).astype(jnp.bfloat16)
 
 
-def load_kernel(lengths_ref, q_ref, kv_ref, own_ref, out_ref):
+def load_kernel(ends_ref, q_ref, kv_ref, own_ref, out_ref):
     out_ref[: own_ref.shape[0], :] = own_ref[...]
     half = q_ref.shape[0] // 2
-    ends = []
-    total = 0
-    for k in range(lengths_ref.shape[0]):
-        total = total + lengths_ref[k]
-        ends.append(total)
     for start in range(0, q_ref.shape[0], SHORT_TILE):
         rows = pl.ds(start, SHORT_TILE)
         seen = start + SHORT_TILE
         scores = scores_of(q_ref[rows, :], kv_ref[:seen, :DH])
         row = start + lax.broadcasted_iota(jnp.int32, (SHORT_TILE, 1), 0)
         first = jnp.zeros((SHORT_TILE, 1), jnp.int32)
-        for end in ends:
-            first = jnp.where(row >= end, end, first)
+        for k in range(ends_ref.shape[0]):
+            first = jnp.where(row >= ends_ref[k], ends_ref[k], first)
         col = lax.broadcasted_iota(jnp.int32, scores.shape, 1)
         scores = jnp.where((col <= row) & (col >= first), scores, -jnp.inf)
         top = jnp.max(scores, axis=1, keepdims=True)
@@ -178,9 +174,31 @@
         out_specs=jax.tree.map(lambda _: VMEM_SPEC, out_shape),
         scratch_shapes=scratch,
         compiler_params=pltpu.CompilerParams(vmem_limit_bytes=VMEM),
-        cost_estimate=pl.CostEstimate(flops=1, bytes_accessed=1, transcendentals=0),
+        cost_estimate=pl.CostEstimate(flops=COST[name], bytes_accessed=1, transcendentals=0),
         name=name,
     )(*operands)
+
+
+def plan_kernel(me_ref, span_ref, partner_ref, lengths_ref, seen_ref, slot_ref, ends_ref):
+    groups = span_ref.shape[0]
+    chips = groups // CORES
+    me = me_ref[0]
+    core = lax.rem(me, CORES)
+    for which in range(CORES):
+        rows = me if which == 0 else me + 1 - 2 * core
+        wanted = partner_ref[rows]
+        slot = jnp.int32(chips)
+        for k in range(chips + 1):
+            chip = lax.rem(me // CORES + (k // 2) * (2 * core - 1) + chips, chips)
+            held = chip * CORES + (core if k % 2 == 0 else 1 - core)
+            seen_ref[which, k] = (span_ref[held] < span_ref[rows]).astype(jnp.int32)
+            if k != 1:
+                slot = jnp.where(held == wanted, max(k - 1, 0), slot)
+        slot_ref[which] = slot
+    total = jnp.int32(0)
+    for k in range(lengths_ref.shape[1]):
+        total = total + lengths_ref[me, k]
+        ends_ref[k] = total
 
 
 def state_of(rows, width=3 * DH):
@@ -211,10 +229,10 @@
     return lax.ppermute(block, "inst", [(i, i ^ 1) for i in range(lax.axis_size("inst"))])
 
 
-def ahead(block):
+def ahead(block, crossing=False):
     size = lax.axis_size("inst")
-    step = lambda i: CORES if i % CORES == 0 else -CORES
-    return lax.ppermute(block, "inst", [(i, (i + step(i)) % size) for i in range(size)])
+    step = lambda i: CORES if (i + crossing) % CORES == 0 else -CORES
+    return lax.ppermute(block, "inst", [(i, ((i ^ 1 if crossing else i) + step(i)) % size) for i in range(size)])
 
 
 def body(
@@ -246,48 +264,44 @@
     got = swapped(heads, "sp")
     short_own = got[:, :cut].reshape(short_rows, 2 * DH)
     own = got[:, cut:].reshape(rows, 2 * DH)
+    ints = lambda *shape: jax.ShapeDtypeStruct(shape, jnp.int32)
+    seen, slot, ends = pl.pallas_call(
+        plan_kernel,
+        out_shape=(ints(CORES, chips + 1), ints(CORES), ints(short_lengths.shape[1])),
+        in_specs=[SMEM_SPEC] * 4,
+        out_specs=(SMEM_SPEC,) * 3,
+        name="plan",
+    )(me[None], span_of, pair_partner, short_lengths)
     own, short_own, other_queries = lax.optimization_barrier((own, short_own, across(queries)))
     load = call(
         load_kernel,
         jax.ShapeDtypeStruct((rows + short_rows // 2, 2 * DH), jnp.bfloat16),
-        (short_lengths[me], short_queries[0], short_own, own),
+        (ends, short_queries[0], short_own, own),
         "load",
     )
-    ring = [(load, across(load))]
-    for step in range(1, chips // 2):
-        ring.append(tuple(ahead(block) for block in ring[-1]))
-    end = ahead(ring[-1][0])
-    core = me % CORES
-    chip = me // CORES + jnp.asarray(range(chips // 2 + 1), jnp.int32) * (2 * core - 1)
-    held = (chip % chips * CORES)[:, None] + jnp.stack([core, 1 - core])[None, :]
-    held = held.reshape(-1)
-    ids = jnp.arange(groups, dtype=jnp.int32)
-    spans = jnp.sum(jnp.where(held[:, None] == ids[None, :], span_of[None, :], 0), axis=1)
-    mine = jnp.stack([span_of[me], span_of[me ^ 1]])
-    seen = (spans[None, :] < mine[:, None]).astype(jnp.int32)
-
-    riders = [block for pair in ring for block in pair] + [end]
-    wanted = jnp.stack([pair_partner[me], pair_partner[me ^ 1]])
-    found = held[None, : len(riders)] == wanted[:, None]
-    slots = jnp.arange(len(riders), dtype=jnp.int32)
-    slot = jnp.min(jnp.where(found, slots[None, :], len(riders)), axis=1)
-
     keys_t = pltpu.VMEM((DH, rows), jnp.bfloat16)
     both = (state_of(rows), state_of(rows))
 
-    def ring_step(step, state, other):
+    def ring_step(step, states):
         return call(
             functools.partial(ring_kernel, indices=(2 * step, 2 * step + 1)),
             both,
-            (seen, queries, other_queries, *ring[step], state, other),
+            (seen, queries, other_queries, *ring[step], *states),
             "ring",
             [keys_t],
         )
 
-    state, other = call(own_kernel, both, (seen, queries, other_queries, load), "own", [keys_t])
+    states = call(own_kernel, both, (seen, queries, other_queries, load), "own", [keys_t])
+    ring = [(load,), (ahead(load), ahead(load, crossing=True))]
+    ring.append(tuple(ahead(block) for block in ring[1]))
+    even, states = lax.optimization_barrier((ring[2][0], states))
+    ring.append((ahead(even), ahead(ring[2][1])))
+    end = ahead(ring[3][0])
     for step in range(1, chips // 2):
-        state, other = ring_step(step, state, other)
-
+        states = ring_step(step, states)
+    state, other = states
+
+    riders = [block for pair in ring for block in pair] + [end]
     rider_space = [pltpu.VMEM((short_rows // 2, 2 * DH), jnp.bfloat16), pltpu.SemaphoreType.DMA]
     end_space = [pltpu.VMEM((rows, 3 * DH), jnp.float32), keys_t] + rider_space
 

time: 112 us -> 104 us (0.929)
  starting transfers between devices: 60.4 us -> 54.7 us
  Pallas kernels: 21 us -> 26.5 us
  other arithmetic: 4.64 us -> 0 us
  local copies, waits for them, and re-layouts: 4.36 us -> 0.74 us
  waiting for transfers between devices: 18.6 us -> 20.2 us
    pallas_call x8, Pallas kernels: 19.3 us -> 23.3 us  [call(): pl.pallas_call(kernel, out_shape=out_shape, in_specs=specs[:len(specs) -...]
    ppermute x7, waiting for transfers between devices: 4.86 us -> 8.42 us  [ahead(): lax.ppermute(block, 'inst', [(i, ((i ^ 1 if crossing else i) + step(i)) %...]
    ppermute x3 -> x2, starting transfers between devices: 14.1 us -> 11.1 us  [across(): lax.ppermute(block, 'inst', [(i, i ^ 1) for i in range(lax.axis_size('ins...]
    another operation x3 -> x0, other arithmetic: 2.81 us -> none  [the longest x1 1.41 us: body(): mine = jnp.stack([span_of[me], span_of[me ^ 1]])]
    ppermute x7, starting transfers between devices: 35.7 us -> 33 us  [ahead(): lax.ppermute(block, 'inst', [(i, ((i ^ 1 if crossing else i) + step(i)) %...]
    unnamed x18 -> x13, local copies, waits for them, and re-layouts: 2.87 us -> 0.7 us
    all_to_all x1, waiting for transfers between devices: 13.3 us -> 11.4 us  [swapped(): return lax.all_to_all(blocks, axis, split_axis=0, concat_axis=0, tiled=True)]
    pallas_call x0 -> x1, Pallas kernels: none -> 1.44 us  [body(): pl.pallas_call(plan_kernel, out_shape=(ints(CORES, chips + 1), ints(CORES...]
  transfers between devices with their start and end apart: 11 -> 10, of which waited for: 6 -> 5; matrix products, arithmetic and copies ran while one was open for 6% -> 1% of each run, Pallas kernels for 11% -> 18%
where the time goes in v3:
time: 104 us; the launch traced here: 103 us
  starting transfers between devices  54.7 us (53%)
  Pallas kernels  26.5 us (25%)
  waiting for transfers between devices  20.2 us (19%)
  between operations  1.07 us (1%)
    ppermute x7, starting transfers between devices, ahead(): lax.ppermute(block, 'inst', [(i, ((i ^ 1 if crossing else i) + step(i)) %...  33 us
    pallas_call x8, Pallas kernels, call(): pl.pallas_call(kernel, out_shape=out_shape, in_specs=specs[:len(specs) -...  23.3 us
    all_to_all x1, waiting for transfers between devices, swapped(): return lax.all_to_all(blocks, axis, split_axis=0, concat_axis=0, tiled=True)  11.4 us
    ppermute x2, starting transfers between devices, across(): lax.ppermute(block, 'inst', [(i, i ^ 1) for i in range(lax.axis_size('ins...  11.1 us
    all_to_all x1, starting transfers between devices, swapped(): return lax.all_to_all(blocks, axis, split_axis=0, concat_axis=0, tiled=True)  10.6 us
    ppermute x7, waiting for transfers between devices, ahead(): lax.ppermute(block, 'inst', [(i, ((i ^ 1 if crossing else i) + step(i)) %...  8.42 us
  transfers between devices with their start and end apart: 10, of which 5 were waited for; matrix products, arithmetic and copies ran while one was open for 1% of the time, Pallas kernels for 18%

profile of v3, /device:TPU:1, one launch (start us, length us, event | category | flops | bytes accessed | tf_op | source)
XLA Modules:
  0.0 103.2 jit_solution(14102649117539710512)
XLA Ops:
  0.7 1.7 %heads.1 = bf16[32,40,256]{2,1,0:T(8,128)(2,1)} custom-call(bf16[16,512]{1,0:T(8,128)(2,1)} %bitcast.22, bf16[16,512]{1,0:T(8,128)(2,1)} %bitcast.23, bf16[24,512]{1,0:T(8,128)(2,1)} %bitcast.20, bf16[24,512]{1,0:T(8,128)(2,1)} %bitcast.21), custom_call_target="tpu_custom_call" | custom-call | tf_op jit(solution)/shard_map/heads/pallas_call | solution.py:257
  2.4 10.6 %all-to-all-start = ((bf16[32,40,256]{2,1,0:T(8,128)(2,1)}), bf16[32,40,256]{2,1,0:T(8,128)(2,1)S(1)}, u32[]{:S(2)}, u32[]{:S(2)}) async-start(bf16[32,40,256]{2,1,0:T(8,128)(2,1)} %heads.1), calls=%async_computation | async-start | bytes 1310720 | tf_op jit(solution)/shard_map/all_to_all | solution.py:225
  13.0 2.9 %collective-permute-start = (bf16[768,128]{1,0:T(8,128)(2,1)S(1)}, bf16[768,128]{1,0:T(8,128)(2,1)S(1)}, u32[]{:S(2)}, u32[]{:S(2)}) collective-permute-start(bf16[768,128]{1,0:T(8,128)(2,1)S(1)} %bitcast.13), channel_id=1, source_target_pairs={{0,32},{32,0},{64,96},{96,64},{128,160},{160,128},{192,224},{224,1... | collective-permute-start | bytes 589832 | tf_op jit(solution)/shard_map/ppermute | solution.py:229
  15.9 0.7 copy.11.lengths_ref
  16.6 1.4 %plan.1 = (s32[2,9]{1,0:T(2,128)}, s32[2]{0:T(128)}, s32[8]{0:T(128)}) custom-call(s32[1]{0:T(128)} %bitcast.me_ref, s32[16]{0:T(128)} %span_ref.1, s32[16]{0:T(128)} %partner_ref.1, s32[16,8]{1,0:T(8,128)} %copy.11.lengths_ref), custom_call_target="tpu_custom_call" | custom-call | tf_op jit(solution)/shard_map/plan/pallas_call | solution.py:268
  18.1 11.4 %all-to-all-done = bf16[32,40,256]{2,1,0:T(8,128)(2,1)S(1)} async-done(((bf16[32,40,256]{2,1,0:T(8,128)(2,1)}), bf16[32,40,256]{2,1,0:T(8,128)(2,1)S(1)}, u32[]{:S(2)}, u32[]{:S(2)}) %all-to-all-start) | async-done | bytes 655392 | tf_op jit(solution)/shard_map/all_to_all | solution.py:225
  29.5 0.0 collective-permute-done.other_q_ref.q_ref
  29.5 0.0 copy-start.1
  29.5 1.4 %load.1.kv_ref.refs_0_ = bf16[1024,256]{1,0:T(8,128)(2,1)S(1)} custom-call(s32[8]{0:T(128)S(1)} %copy-done.4, bf16[512,128]{1,0:T(8,128)(2,1)S(1)} %bitcast.19, bf16[512,256]{1,0:T(8,128)(2,1)S(1)} %bitcast.12, bf16[768,256]{1,0:T(8,128)(2,1)S(1)} %bitcast.11), custom_call_target="tpu_custom_call" | custom-call | flops 1000000000 | bytes 1 | tf_op jit(solution)/shard_map/load/pallas_call | solution.py:170
  30.9 10.7 %collective-permute-start.1 = (bf16[1024,256]{1,0:T(8,128)(2,1)S(1)}, bf16[1024,256]{1,0:T(8,128)(2,1)S(1)}, u32[]{:S(2)}, u32[]{:S(2)}) collective-permute-start(bf16[1024,256]{1,0:T(8,128)(2,1)S(1)} %load.1.kv_ref.refs_0_), channel_id=1, source_target_pairs={{0,64},{32,480},{64,128},{96,32},{128,192},{160,96},{192,256},{224... | collective-permute-start | bytes 1572872 | tf_op jit(solution)/shard_map/ppermute | solution.py:235
  41.6 2.5 %collective-permute-start.5 = (bf16[1024,256]{1,0:T(8,128)(2,1)S(1)}, bf16[1024,256]{1,0:T(8,128)(2,1)S(1)}, u32[]{:S(2)}, u32[]{:S(2)}) collective-permute-start(bf16[1024,256]{1,0:T(8,128)(2,1)S(1)} %load.1.kv_ref.refs_0_), channel_id=1, source_target_pairs={{0,480},{32,64},{64,32},{96,128},{128,96},{160,192},{192,160},{224... | collective-permute-start | bytes 1572872 | tf_op jit(solution)/shard_map/ppermute | solution.py:235
  44.1 6.4 %collective-permute-done.1.refs_0_.refs_1_ = bf16[1024,256]{1,0:T(8,128)(2,1)S(1)} collective-permute-done((bf16[1024,256]{1,0:T(8,128)(2,1)S(1)}, bf16[1024,256]{1,0:T(8,128)(2,1)S(1)}, u32[]{:S(2)}, u32[]{:S(2)}) %collective-permute-start.1) | collective-permute-done | bytes 524320 | tf_op jit(solution)/shard_map/ppermute | solution.py:235
  50.5 5.0 %collective-permute-start.2 = (bf16[1024,256]{1,0:T(8,128)(2,1)S(1)}, bf16[1024,256]{1,0:T(8,128)(2,1)S(1)}, u32[]{:S(2)}, u32[]{:S(2)}) collective-permute-start(bf16[1024,256]{1,0:T(8,128)(2,1)S(1)} %collective-permute-done.1.refs_0_.refs_1_), channel_id=1, source_target_pairs={{0,64},{32,480},{64,128},{96,32},{128,192},{160,96},{192,256},{224... | collective-permute-start | bytes 1572872 | tf_op jit(solution)/shard_map/ppermute | solution.py:235
  55.5 0.0 collective-permute-done.5.refs_1_.refs_2_
  55.5 2.8 %collective-permute-start.6 = (bf16[1024,256]{1,0:T(8,128)(2,1)S(1)}, bf16[1024,256]{1,0:T(8,128)(2,1)S(1)}, u32[]{:S(2)}, u32[]{:S(2)}) collective-permute-start(bf16[1024,256]{1,0:T(8,128)(2,1)S(1)} %collective-permute-done.5.refs_1_.refs_2_), channel_id=1, source_target_pairs={{0,64},{32,480},{64,128},{96,32},{128,192},{160,96},{192,256},{224... | collective-permute-start | bytes 1572872 | tf_op jit(solution)/shard_map/ppermute | solution.py:235
  58.3 1.8 %own.1 = (f32[768,384]{1,0:T(8,128)S(1)}, f32[768,384]{1,0:T(8,128)S(1)}) custom-call(s32[2,9]{1,0:T(2,128)S(1)} %copy-done.1, bf16[768,128]{1,0:T(8,128)(2,1)S(1)} %bitcast.14, bf16[768,128]{1,0:T(8,128)(2,1)S(1)} %collective-permute-done.other_q_ref.q_ref, bf16[1024,256]{1,0:T(8,128)(2,1)S(1)} %load.1.kv_ref.refs_0_), custom_call_target="tpu_custom_call" | custom-call | flops 2000000000 | bytes 1 | tf_op jit(solution)/shard_map/own/pallas_call | solution.py:170
  60.2 1.4 %collective-permute-done.2.refs_0_.refs_3_ = bf16[1024,256]{1,0:T(8,128)(2,1)S(1)} collective-permute-done((bf16[1024,256]{1,0:T(8,128)(2,1)S(1)}, bf16[1024,256]{1,0:T(8,128)(2,1)S(1)}, u32[]{:S(2)}, u32[]{:S(2)}) %collective-permute-start.2) | collective-permute-done | bytes 524320 | tf_op jit(solution)/shard_map/ppermute | solution.py:235
  61.6 5.0 %collective-permute-start.3 = (bf16[1024,256]{1,0:T(8,128)(2,1)S(1)}, bf16[1024,256]{1,0:T(8,128)(2,1)S(1)}, u32[]{:S(2)}, u32[]{:S(2)}) collective-permute-start(bf16[1024,256]{1,0:T(8,128)(2,1)S(1)} %collective-permute-done.2.refs_0_.refs_3_), channel_id=1, source_target_pairs={{0,64},{32,480},{64,128},{96,32},{128,192},{160,96},{192,256},{224... | collective-permute-start | bytes 1572872 | tf_op jit(solution)/shard_map/ppermute | solution.py:235
  66.6 0.6 collective-permute-done.6.refs_1_.refs_4_
  67.2 5.0 %collective-permute-start.7 = (bf16[1024,256]{1,0:T(8,128)(2,1)S(1)}, bf16[1024,256]{1,0:T(8,128)(2,1)S(1)}, u32[]{:S(2)}, u32[]{:S(2)}) collective-permute-start(bf16[1024,256]{1,0:T(8,128)(2,1)S(1)} %collective-permute-done.6.refs_1_.refs_4_), channel_id=1, source_target_pairs={{0,64},{32,480},{64,128},{96,32},{128,192},{160,96},{192,256},{224... | collective-permute-start | bytes 1572872 | tf_op jit(solution)/shard_map/ppermute | solution.py:235
  72.2 4.1 %ring.3 = (f32[768,384]{1,0:T(8,128)S(1)}, f32[768,384]{1,0:T(8,128)S(1)}) custom-call(s32[2,9]{1,0:T(2,128)S(1)} %copy-done.1, bf16[768,128]{1,0:T(8,128)(2,1)S(1)} %bitcast.15, bf16[768,128]{1,0:T(8,128)(2,1)S(1)} %collective-permute-done.other_q_ref.q_ref, bf16[1024,256]{1,0:T(8,128)(2,1)S(1)} %collective-permute-done.1.refs_0_.refs_1_, ...), custom_call_target="tpu_custom_call" | custom-call | flops 4000000000 | bytes 1 | tf_op jit(solution)/shard_map/ring/pallas_call | solution.py:170
  76.4 0.0 collective-permute-done.3.refs_0_.refs_5_
  76.4 1.9 %collective-permute-start.4 = (bf16[1024,256]{1,0:T(8,128)(2,1)S(1)}, bf16[1024,256]{1,0:T(8,128)(2,1)S(1)}, u32[]{:S(2)}, u32[]{:S(2)}) collective-permute-start(bf16[1024,256]{1,0:T(8,128)(2,1)S(1)} %collective-permute-done.3.refs_0_.refs_5_), channel_id=1, source_target_pairs={{0,64},{32,480},{64,128},{96,32},{128,192},{160,96},{192,256},{224... | collective-permute-start | bytes 1572872 | tf_op jit(solution)/shard_map/ppermute | solution.py:235
  78.3 5.5 %ring.4 = (f32[768,384]{1,0:T(8,128)S(1)}, f32[768,384]{1,0:T(8,128)S(1)}) custom-call(s32[2,9]{1,0:T(2,128)S(1)} %copy-done.1, bf16[768,128]{1,0:T(8,128)(2,1)S(1)} %bitcast.16, bf16[768,128]{1,0:T(8,128)(2,1)S(1)} %collective-permute-done.other_q_ref.q_ref, bf16[1024,256]{1,0:T(8,128)(2,1)S(1)} %collective-permute-done.2.refs_0_.refs_3_, ...), custom_call_target="tpu_custom_call" | custom-call | flops 4000000000 | bytes 1 | tf_op jit(solution)/shard_map/ring/pallas_call | solution.py:170
  83.8 0.0 collective-permute-done.7.refs_1_.refs_6_
  83.8 4.2 %ring.5 = (f32[768,384]{1,0:T(8,128)S(1)}, f32[768,384]{1,0:T(8,128)S(1)}) custom-call(s32[2,9]{1,0:T(2,128)S(1)} %copy-done.1, bf16[768,128]{1,0:T(8,128)(2,1)S(1)} %bitcast.17, bf16[768,128]{1,0:T(8,128)(2,1)S(1)} %collective-permute-done.other_q_ref.q_ref, bf16[1024,256]{1,0:T(8,128)(2,1)S(1)} %collective-permute-done.3.refs_0_.refs_5_, ...), custom_call_target="tpu_custom_call" | custom-call | flops 4000000000 | bytes 1 | tf_op jit(solution)/shard_map/ring/pallas_call | solution.py:170
  88.0 0.0 collective-permute-done.4.kv_ref.refs_7_
  88.0 2.1 %end.3 = f32[1024,256]{1,0:T(8,128)S(1)} custom-call(s32[2,9]{1,0:T(2,128)S(1)} %copy-done.1, s32[2]{0:T(128)S(1)} %copy-done, bf16[768,128]{1,0:T(8,128)(2,1)S(1)} %collective-permute-done.other_q_ref.q_ref, bf16[1024,256]{1,0:T(8,128)(2,1)S(1)} %collective-permute-done.4.kv_ref.refs_7_, f32[768,384]{1,0:T(8,128)S(1)} %get-tuple-element.37.before, ...), custom_call_target="tpu_custom_call" | custom-call | flops 1000000000 | bytes 1 | tf_op jit(solution)/shard_map/end/pallas_call | solution.py:170
  90.1 8.3 %collective-permute-start.8 = (f32[1024,256]{1,0:T(8,128)S(1)}, f32[1024,256]{1,0:T(8,128)S(1)}, u32[]{:S(2)}, u32[]{:S(2)}) collective-permute-start(f32[1024,256]{1,0:T(8,128)S(1)} %end.3), channel_id=1, source_target_pairs={{0,32},{32,0},{64,96},{96,64},{128,160},{160,128},{192,224},{224,1... | collective-permute-start | bytes 3145736 | tf_op jit(solution)/shard_map/ppermute | solution.py:229
  98.3 1.8 %end.2.mine_ref = f32[768,256]{1,0:T(8,128)S(1)} custom-call(s32[2,9]{1,0:T(2,128)S(1)} %copy-done.1, s32[2]{0:T(128)S(1)} %copy-done, bf16[768,128]{1,0:T(8,128)(2,1)S(1)} %bitcast.18, bf16[1024,256]{1,0:T(8,128)(2,1)S(1)} %collective-permute-done.4.kv_ref.refs_7_, f32[768,384]{1,0:T(8,128)S(1)} %get-tuple-element.36.before), custom_call_target="tpu_custom_call" | custom-call | flops 1000000000 | bytes 1 | tf_op jit(solution)/shard_map/end/pallas_call | solution.py:170
  100.2 0.4 collective-permute-done.8.other_ref
  100.6 2.4 %merge.1 = (bf16[768,128]{1,0:T(8,128)(2,1)}, bf16[512,128]{1,0:T(8,128)(2,1)}) custom-call(s32[2]{0:T(128)S(1)} %copy-done, f32[768,256]{1,0:T(8,128)S(1)} %end.2.mine_ref, f32[1024,256]{1,0:T(8,128)S(1)} %collective-permute-done.8.other_ref, bf16[1024,256]{1,0:T(8,128)(2,1)S(1)} %load.1.kv_ref.refs_0_, ...), custom_call_target="tpu_custom_call" | custom-call | flops 1000000000 | bytes 1 | tf_op jit(solution)/shard_map/merge/pallas_call | solution.py:170
  (13 shorter events, 0.1 us)
Async XLA Ops:
  0.6 12.4 %copy-start.2 = (bf16[1,768,128]{2,1,0:T(8,128)(2,1)S(1)}, bf16[1,768,128]{2,1,0:T(8,128)(2,1)}, u32[]{:S(2)}) copy-start(bf16[1,768,128]{2,1,0:T(8,128)(2,1)} %param.9) | copy-start | bytes 589828
  0.6 15.3 %copy-start.5 = (s32[16,8]{0,1:T(8,128)S(1)}, s32[16,8]{0,1:T(8,128)}, u32[]{:S(2)}) copy-start(s32[16,8]{0,1:T(8,128)} %param.16) | copy-start | bytes 1540
  2.4 27.1 %copy-start.3 = (bf16[1,512,128]{2,1,0:T(8,128)(2,1)S(1)}, bf16[1,512,128]{2,1,0:T(8,128)(2,1)}, u32[]{:S(2)}) copy-start(bf16[1,512,128]{2,1,0:T(8,128)(2,1)} %param.13) | copy-start | bytes 393220
  2.4 27.0 %all-to-all-start = ((bf16[32,40,256]{2,1,0:T(8,128)(2,1)}), bf16[32,40,256]{2,1,0:T(8,128)(2,1)S(1)}, u32[]{:S(2)}, u32[]{:S(2)}) async-start(bf16[32,40,256]{2,1,0:T(8,128)(2,1)} %heads.1), calls=%async_computation | async-start | bytes 1310720 | tf_op jit(solution)/shard_map/all_to_all | solution.py:225
  13.0 16.4 %collective-permute-start = (bf16[768,128]{1,0:T(8,128)(2,1)S(1)}, bf16[768,128]{1,0:T(8,128)(2,1)S(1)}, u32[]{:S(2)}, u32[]{:S(2)}) collective-permute-start(bf16[768,128]{1,0:T(8,128)(2,1)S(1)} %bitcast.13), channel_id=1, source_target_pairs={{0,32},{32,0},{64,96},{96,64},{128,160},{160,128},{192,224},{224,1... | collective-permute-start | bytes 589832 | tf_op jit(solution)/shard_map/ppermute | solution.py:229
  18.1 11.4 %copy-start.4 = (s32[8]{0:T(128)S(1)}, s32[8]{0:T(128)}, u32[]{:S(2)}) copy-start(s32[8]{0:T(128)} %get-tuple-element.23.ends_ref) | copy-start | bytes 100
  29.5 28.8 %copy-start.1 = (s32[2,9]{1,0:T(2,128)S(1)}, s32[2,9]{1,0:T(2,128)}, u32[]{:S(2)}) copy-start(s32[2,9]{1,0:T(2,128)} %get-tuple-element.22.seen_ref) | copy-start | bytes 220
  30.9 19.6 %collective-permute-start.1 = (bf16[1024,256]{1,0:T(8,128)(2,1)S(1)}, bf16[1024,256]{1,0:T(8,128)(2,1)S(1)}, u32[]{:S(2)}, u32[]{:S(2)}) collective-permute-start(bf16[1024,256]{1,0:T(8,128)(2,1)S(1)} %load.1.kv_ref.refs_0_), channel_id=1, source_target_pairs={{0,64},{32,480},{64,128},{96,32},{128,192},{160,96},{192,256},{224... | collective-permute-start | bytes 1572872 | tf_op jit(solution)/shard_map/ppermute | solution.py:235
  41.6 13.9 %collective-permute-start.5 = (bf16[1024,256]{1,0:T(8,128)(2,1)S(1)}, bf16[1024,256]{1,0:T(8,128)(2,1)S(1)}, u32[]{:S(2)}, u32[]{:S(2)}) collective-permute-start(bf16[1024,256]{1,0:T(8,128)(2,1)S(1)} %load.1.kv_ref.refs_0_), channel_id=1, source_target_pairs={{0,480},{32,64},{64,32},{96,128},{128,96},{160,192},{192,160},{224... | collective-permute-start | bytes 1572872 | tf_op jit(solution)/shard_map/ppermute | solution.py:235
  50.5 11.1 %collective-permute-start.2 = (bf16[1024,256]{1,0:T(8,128)(2,1)S(1)}, bf16[1024,256]{1,0:T(8,128)(2,1)S(1)}, u32[]{:S(2)}, u32[]{:S(2)}) collective-permute-start(bf16[1024,256]{1,0:T(8,128)(2,1)S(1)} %collective-permute-done.1.refs_0_.refs_1_), channel_id=1, source_target_pairs={{0,64},{32,480},{64,128},{96,32},{128,192},{160,96},{192,256},{224... | collective-permute-start | bytes 1572872 | tf_op jit(solution)/shard_map/ppermute | solution.py:235
  55.5 11.7 %collective-permute-start.6 = (bf16[1024,256]{1,0:T(8,128)(2,1)S(1)}, bf16[1024,256]{1,0:T(8,128)(2,1)S(1)}, u32[]{:S(2)}, u32[]{:S(2)}) collective-permute-start(bf16[1024,256]{1,0:T(8,128)(2,1)S(1)} %collective-permute-done.5.refs_1_.refs_2_), channel_id=1, source_target_pairs={{0,64},{32,480},{64,128},{96,32},{128,192},{160,96},{192,256},{224... | collective-permute-start | bytes 1572872 | tf_op jit(solution)/shard_map/ppermute | solution.py:235
  61.6 14.8 %collective-permute-start.3 = (bf16[1024,256]{1,0:T(8,128)(2,1)S(1)}, bf16[1024,256]{1,0:T(8,128)(2,1)S(1)}, u32[]{:S(2)}, u32[]{:S(2)}) collective-permute-start(bf16[1024,256]{1,0:T(8,128)(2,1)S(1)} %collective-permute-done.2.refs_0_.refs_3_), channel_id=1, source_target_pairs={{0,64},{32,480},{64,128},{96,32},{128,192},{160,96},{192,256},{224... | collective-permute-start | bytes 1572872 | tf_op jit(solution)/shard_map/ppermute | solution.py:235
  67.2 16.6 %collective-permute-start.7 = (bf16[1024,256]{1,0:T(8,128)(2,1)S(1)}, bf16[1024,256]{1,0:T(8,128)(2,1)S(1)}, u32[]{:S(2)}, u32[]{:S(2)}) collective-permute-start(bf16[1024,256]{1,0:T(8,128)(2,1)S(1)} %collective-permute-done.6.refs_1_.refs_4_), channel_id=1, source_target_pairs={{0,64},{32,480},{64,128},{96,32},{128,192},{160,96},{192,256},{224... | collective-permute-start | bytes 1572872 | tf_op jit(solution)/shard_map/ppermute | solution.py:235
  76.4 11.6 %collective-permute-start.4 = (bf16[1024,256]{1,0:T(8,128)(2,1)S(1)}, bf16[1024,256]{1,0:T(8,128)(2,1)S(1)}, u32[]{:S(2)}, u32[]{:S(2)}) collective-permute-start(bf16[1024,256]{1,0:T(8,128)(2,1)S(1)} %collective-permute-done.3.refs_0_.refs_5_), channel_id=1, source_target_pairs={{0,64},{32,480},{64,128},{96,32},{128,192},{160,96},{192,256},{224... | collective-permute-start | bytes 1572872 | tf_op jit(solution)/shard_map/ppermute | solution.py:235
  83.8 4.2 %copy-start = (s32[2]{0:T(128)S(1)}, s32[2]{0:T(128)}, u32[]{:S(2)}) copy-start(s32[2]{0:T(128)} %get-tuple-element.21.slot_ref) | copy-start | bytes 28
  90.1 10.5 %collective-permute-start.8 = (f32[1024,256]{1,0:T(8,128)S(1)}, f32[1024,256]{1,0:T(8,128)S(1)}, u32[]{:S(2)}, u32[]{:S(2)}) collective-permute-start(f32[1024,256]{1,0:T(8,128)S(1)} %end.3), channel_id=1, source_target_pairs={{0,32},{32,0},{64,96},{96,64},{128,160},{160,128},{192,224},{224,1... | collective-permute-start | bytes 3145736 | tf_op jit(solution)/shard_map/ppermute | solution.py:229

commit v4 on v3

--- a/solution.py
+++ b/solution.py
@@ -65,7 +65,7 @@
         state[rows, 2 * DH :] = jnp.broadcast_to(top, (TILE, DH))
 
 
-def own_kernel(seen_ref, q_ref, other_q_ref, kv_ref, state, other, keys_t):
+def own_kernel(seen_ref, q_ref, other_q_ref, kv_ref, far_ref, state, other, keys_t):
     keys_t[...] = kv_ref[: q_ref.shape[0], :DH].T
     diagonal(q_ref, keys_t, kv_ref, state)
     other[:, : 2 * DH] = jnp.zeros((other.shape[0], 2 * DH), jnp.float32)
@@ -74,6 +74,24 @@
     @pl.when(seen_ref[1, 0] > 0)
     def _():
         add_block(other_q_ref, keys_t[...], kv_ref[: q_ref.shape[0], DH:], other)
+
+    both_sides(seen_ref, seen_ref.shape[1] - 1, q_ref, other_q_ref, far_ref, state, other, keys_t)
+
+
+def both_sides(seen_ref, index, q_ref, other_q_ref, kv_ref, state, other, keys_t):
+    rows = q_ref.shape[0]
+
+    @pl.when((seen_ref[0, index] > 0) | (seen_ref[1, index] > 0))
+    def _():
+        keys_t[...] = kv_ref[:rows, :DH].T
+
+    @pl.when(seen_ref[0, index] > 0)
+    def _():
+        add_block(q_ref, keys_t[...], kv_ref[:rows, DH:], state)
+
+    @pl.when(seen_ref[1, index] > 0)
+    def _():
+        add_block(other_q_ref, keys_t[...], kv_ref[:rows, DH:], other)
 
 
 def ring_kernel(seen_ref, q_ref, other_q_ref, *refs, indices):
@@ -81,18 +99,7 @@
     state[...] = before[...]
     other[...] = other_before[...]
     for index, kv_ref in zip(indices, kv_refs):
-
-        @pl.when((seen_ref[0, index] > 0) | (seen_ref[1, index] > 0))
-        def _():
-            keys_t[...] = kv_ref[: q_ref.shape[0], :DH].T
-
-        @pl.when(seen_ref[0, index] > 0)
-        def _():
-            add_block(q_ref, keys_t[...], kv_ref[: q_ref.shape[0], DH:], state)
-
-        @pl.when(seen_ref[1, index] > 0)
-        def _():
-            add_block(other_q_ref, keys_t[...], kv_ref[: q_ref.shape[0], DH:], other)
+        both_sides(seen_ref, index, q_ref, other_q_ref, kv_ref, state, other, keys_t)
 
 
 def fetch(slot, riders, target, sem):
@@ -221,6 +228,17 @@
             out[head * copies + copy] = block
 
 
+def far_heads_kernel(both, out):
+    copies = out.shape[0] // KVH
+    half = both.shape[1] // 2
+    for head in range(KVH):
+        keys = both[:, head * DH : (head + 1) * DH]
+        values = both[:, half + head * DH : half + (head + 1) * DH]
+        block = jnp.concatenate([keys, values], axis=1)
+        for copy in range(copies):
+            out[head * copies + copy] = block
+
+
 def swapped(blocks, axis):
     return lax.all_to_all(blocks, axis, split_axis=0, concat_axis=0, tiled=True)
 
@@ -229,9 +247,14 @@
     return lax.ppermute(block, "inst", [(i, i ^ 1) for i in range(lax.axis_size("inst"))])
 
 
-def ahead(block, crossing=False):
+def opposite(block):
     size = lax.axis_size("inst")
-    step = lambda i: CORES if (i + crossing) % CORES == 0 else -CORES
+    return lax.ppermute(block, "inst", [(i, (i + size // 2) % size) for i in range(size)])
+
+
+def ahead(block, crossing=False, chips=1):
+    size = lax.axis_size("inst")
+    step = lambda i: chips * (CORES if (i + crossing) % CORES == 0 else -CORES)
     return lax.ppermute(block, "inst", [(i, ((i ^ 1 if crossing else i) + step(i)) % size) for i in range(size)])
 
 
@@ -272,7 +295,14 @@
         out_specs=(SMEM_SPEC,) * 3,
         name="plan",
     )(me[None], span_of, pair_partner, short_lengths)
-    own, short_own, other_queries = lax.optimization_barrier((own, short_own, across(queries)))
+    far = opposite(jnp.concatenate([prompt_keys[0], prompt_values[0]], axis=1))
+    own, short_own, other_queries, far = lax.optimization_barrier((own, short_own, across(queries), far))
+    far = pl.pallas_call(
+        far_heads_kernel,
+        out_shape=jax.ShapeDtypeStruct((lax.axis_size("sp"), prompt_keys.shape[1], 2 * DH), jnp.bfloat16),
+        name="far_heads",
+    )(far)
+    far = swapped(far, "sp").reshape(rows, 2 * DH)
     load = call(
         load_kernel,
         jax.ShapeDtypeStruct((rows + short_rows // 2, 2 * DH), jnp.bfloat16),
@@ -282,32 +312,34 @@
     keys_t = pltpu.VMEM((DH, rows), jnp.bfloat16)
     both = (state_of(rows), state_of(rows))
 
-    def ring_step(step, states):
+    def ring_step(step, blocks, states):
         return call(
-            functools.partial(ring_kernel, indices=(2 * step, 2 * step + 1)),
+            functools.partial(ring_kernel, indices=(2 * step, 2 * step + 1)[: len(blocks)]),
             both,
-            (seen, queries, other_queries, *ring[step], *states),
+            (seen, queries, other_queries, *blocks, *states),
             "ring",
             [keys_t],
         )
 
-    states = call(own_kernel, both, (seen, queries, other_queries, load), "own", [keys_t])
+    states = call(own_kernel, both, (seen, queries, other_queries, load, far), "own", [keys_t])
     ring = [(load,), (ahead(load), ahead(load, crossing=True))]
     ring.append(tuple(ahead(block) for block in ring[1]))
     even, states = lax.optimization_barrier((ring[2][0], states))
-    ring.append((ahead(even), ahead(ring[2][1])))
-    end = ahead(ring[3][0])
-    for step in range(1, chips // 2):
-        states = ring_step(step, states)
-    state, other = states
-
-    riders = [block for pair in ring for block in pair] + [end]
+    last_rider, odd = lax.optimization_barrier((even[rows:], ring[2][1]))
+    ring.append((ahead(even), ahead(odd)))
+    last_rider = ahead(last_rider, chips=2)
+    states = ring_step(1, ring[1], states)
+    states = ring_step(2, ring[2], states)
+    state, other = ring_step(3, ring[3][:1], states)
+    end = ring[3][1]
+
+    riders = [block for pair in ring for block in pair] + [last_rider]
     rider_space = [pltpu.VMEM((short_rows // 2, 2 * DH), jnp.bfloat16), pltpu.SemaphoreType.DMA]
     end_space = [pltpu.VMEM((rows, 3 * DH), jnp.float32), keys_t] + rider_space
 
     def ending(which, q, before, riders):
         return call(
-            functools.partial(end_kernel, which=which, index=chips),
+            functools.partial(end_kernel, which=which, index=chips - 1),
             state_of(rows + (short_rows // 2 if riders else 0), 2 * DH),
             (seen, slot, q, end, before, *riders),
             "end",

time: 104 us -> 99.9 us (0.961)
  starting transfers between devices: 54.7 us -> 67.5 us
  waiting for transfers between devices: 20.2 us -> 7.51 us
  Pallas kernels: 26.5 us -> 22.1 us
    ppermute x0 -> x1, starting transfers between devices: none -> 10.6 us  [opposite(): lax.ppermute(block, 'inst', [(i, (i + size // 2) % size) for i in range(s...]
    ppermute x7, waiting for transfers between devices: 8.42 us -> 0.02 us  [ahead(): lax.ppermute(block, 'inst', [(i, ((i ^ 1 if crossing else i) + step(i)) %...]
    all_to_all x1 -> x2, starting transfers between devices: 10.6 us -> 18.4 us  [swapped(): return lax.all_to_all(blocks, axis, split_axis=0, concat_axis=0, tiled=True)]
    pallas_call x8, Pallas kernels: 23.3 us -> 17.4 us  [call(): pl.pallas_call(kernel, out_shape=out_shape, in_specs=specs[:len(specs) -...]
    ppermute x2, starting transfers between devices: 11.1 us -> 5.34 us  [across(): lax.ppermute(block, 'inst', [(i, i ^ 1) for i in range(lax.axis_size('ins...]
    all_to_all x1 -> x2, waiting for transfers between devices: 11.4 us -> 5.94 us  [swapped(): return lax.all_to_all(blocks, axis, split_axis=0, concat_axis=0, tiled=True)]
    pallas_call x0 -> x1, Pallas kernels: none -> 1.58 us  [body(): pl.pallas_call(far_heads_kernel, out_shape=jax.ShapeDtypeStruct((lax.axis...]
    ppermute x2, waiting for transfers between devices: 0.43 us -> 1.55 us  [across(): lax.ppermute(block, 'inst', [(i, i ^ 1) for i in range(lax.axis_size('ins...]
  transfers between devices with their start and end apart: 10 -> 12, of which waited for: 5 -> 3; matrix products, arithmetic and copies ran while one was open for 1% -> 1% of each run, Pallas kernels for 18% -> 15%
where the time goes in v4:
time: 99.9 us; the launch traced here: 99.1 us
  starting transfers between devices  67.5 us (68%)
  Pallas kernels  22.1 us (22%)
  waiting for transfers between devices  7.51 us (8%)
  between operations  1.18 us (1%)
    ppermute x7, starting transfers between devices, ahead(): lax.ppermute(block, 'inst', [(i, ((i ^ 1 if crossing else i) + step(i)) %...  33.1 us
    all_to_all x2, starting transfers between devices, swapped(): return lax.all_to_all(blocks, axis, split_axis=0, concat_axis=0, tiled=True)  18.4 us
    pallas_call x8, Pallas kernels, call(): pl.pallas_call(kernel, out_shape=out_shape, in_specs=specs[:len(specs) -...  17.4 us
    ppermute x1, starting transfers between devices, opposite(): lax.ppermute(block, 'inst', [(i, (i + size // 2) % size) for i in range(s...  10.6 us
    all_to_all x2, waiting for transfers between devices, swapped(): return lax.all_to_all(blocks, axis, split_axis=0, concat_axis=0, tiled=True)  5.94 us
    ppermute x2, starting transfers between devices, across(): lax.ppermute(block, 'inst', [(i, i ^ 1) for i in range(lax.axis_size('ins...  5.34 us
  transfers between devices with their start and end apart: 12, of which 3 were waited for; matrix products, arithmetic and copies ran while one was open for 1% of the time, Pallas kernels for 15%

profile of v4, /device:TPU:1, one launch (start us, length us, event | category | flops | bytes accessed | tf_op | source)
XLA Modules:
  0.0 99.1 jit_solution(13280595186002417122)
XLA Ops:
  0.7 1.7 %heads.1 = bf16[32,40,256]{2,1,0:T(8,128)(2,1)} custom-call(bf16[16,512]{1,0:T(8,128)(2,1)} %bitcast.26, bf16[16,512]{1,0:T(8,128)(2,1)} %bitcast.27, bf16[24,512]{1,0:T(8,128)(2,1)} %bitcast.22, bf16[24,512]{1,0:T(8,128)(2,1)} %bitcast.24), custom_call_target="tpu_custom_call" | custom-call | tf_op jit(solution)/shard_map/heads/pallas_call | solution.py:280
  2.4 10.6 %all-to-all-start = ((bf16[32,40,256]{2,1,0:T(8,128)(2,1)}), bf16[32,40,256]{2,1,0:T(8,128)(2,1)S(1)}, u32[]{:S(2)}, u32[]{:S(2)}) async-start(bf16[32,40,256]{2,1,0:T(8,128)(2,1)} %heads.1), calls=%async_computation | async-start | bytes 1310720 | tf_op jit(solution)/shard_map/all_to_all | solution.py:243
  13.0 2.9 %collective-permute-start = (bf16[768,128]{1,0:T(8,128)(2,1)S(1)}, bf16[768,128]{1,0:T(8,128)(2,1)S(1)}, u32[]{:S(2)}, u32[]{:S(2)}) collective-permute-start(bf16[768,128]{1,0:T(8,128)(2,1)S(1)} %bitcast.15), channel_id=1, source_target_pairs={{0,32},{32,0},{64,96},{96,64},{128,160},{160,128},{192,224},{224,1... | collective-permute-start | bytes 589832 | tf_op jit(solution)/shard_map/ppermute | solution.py:247
  15.9 10.6 %collective-permute-start.1 = (bf16[24,1024]{1,0:T(8,128)(2,1)S(1)}, bf16[24,1024]{1,0:T(8,128)(2,1)S(1)}, u32[]{:S(2)}, u32[]{:S(2)}) collective-permute-start(bf16[24,1024]{1,0:T(8,128)(2,1)S(1)} %pad_maximum_fusion), channel_id=1, source_target_pairs={{0,256},{32,288},{64,320},{96,352},{128,384},{160,416},{192,448},{... | collective-permute-start | bytes 147464 | tf_op jit(solution)/shard_map/ppermute | solution.py:252
  26.6 0.7 copy.11.lengths_ref
  27.3 1.4 %plan.1 = (s32[2,9]{1,0:T(2,128)}, s32[2]{0:T(128)}, s32[8]{0:T(128)}) custom-call(s32[1]{0:T(128)} %bitcast.me_ref, s32[16]{0:T(128)} %span_ref.1, s32[16]{0:T(128)} %partner_ref.1, s32[16,8]{1,0:T(8,128)} %copy.11.lengths_ref), custom_call_target="tpu_custom_call" | custom-call | tf_op jit(solution)/shard_map/plan/pallas_call | solution.py:291
  28.7 0.7 all-to-all-done
  29.5 0.0 copy-start.7
  29.5 0.0 collective-permute-done.other_q_ref.q_ref
  29.5 1.4 %load.1.kv_ref.refs_0_ = bf16[1024,256]{1,0:T(8,128)(2,1)S(1)} custom-call(s32[8]{0:T(128)S(1)} %copy-done.4, bf16[512,128]{1,0:T(8,128)(2,1)S(1)} %bitcast.21, bf16[512,256]{1,0:T(8,128)(2,1)S(1)} %bitcast.14, bf16[768,256]{1,0:T(8,128)(2,1)S(1)} %bitcast.13), custom_call_target="tpu_custom_call" | custom-call | flops 1000000000 | bytes 1 | tf_op jit(solution)/shard_map/load/pallas_call | solution.py:177
  30.9 0.0 copy-start.1
  30.9 10.7 %collective-permute-start.2 = (bf16[1024,256]{1,0:T(8,128)(2,1)S(1)}, bf16[1024,256]{1,0:T(8,128)(2,1)S(1)}, u32[]{:S(2)}, u32[]{:S(2)}) collective-permute-start(bf16[1024,256]{1,0:T(8,128)(2,1)S(1)} %load.1.kv_ref.refs_0_), channel_id=1, source_target_pairs={{0,64},{32,480},{64,128},{96,32},{128,192},{160,96},{192,256},{224... | collective-permute-start | bytes 1572872 | tf_op jit(solution)/shard_map/ppermute | solution.py:258
  41.6 2.5 %collective-permute-start.4 = (bf16[1024,256]{1,0:T(8,128)(2,1)S(1)}, bf16[1024,256]{1,0:T(8,128)(2,1)S(1)}, u32[]{:S(2)}, u32[]{:S(2)}) collective-permute-start(bf16[1024,256]{1,0:T(8,128)(2,1)S(1)} %load.1.kv_ref.refs_0_), channel_id=1, source_target_pairs={{0,480},{32,64},{64,32},{96,128},{128,96},{160,192},{192,160},{224... | collective-permute-start | bytes 1572872 | tf_op jit(solution)/shard_map/ppermute | solution.py:258
  44.1 1.6 %far_heads.1 = bf16[32,24,256]{2,1,0:T(8,128)(2,1)} custom-call(bf16[24,1024]{1,0:T(8,128)(2,1)} %copy-done.7), custom_call_target="tpu_custom_call" | custom-call | tf_op jit(solution)/shard_map/far_heads/pallas_call | solution.py:300
  45.7 7.8 %all-to-all-start.1 = ((bf16[32,24,256]{2,1,0:T(8,128)(2,1)}), bf16[32,24,256]{2,1,0:T(8,128)(2,1)S(1)}, u32[]{:S(2)}, u32[]{:S(2)}) async-start(bf16[32,24,256]{2,1,0:T(8,128)(2,1)} %far_heads.1), calls=%async_computation.1 | async-start | bytes 786432 | tf_op jit(solution)/shard_map/all_to_all | solution.py:243
  53.5 0.0 collective-permute-done.2.refs_0_.refs_1_
  53.5 2.2 %collective-permute-start.3 = (bf16[1024,256]{1,0:T(8,128)(2,1)S(1)}, bf16[1024,256]{1,0:T(8,128)(2,1)S(1)}, u32[]{:S(2)}, u32[]{:S(2)}) collective-permute-start(bf16[1024,256]{1,0:T(8,128)(2,1)S(1)} %collective-permute-done.2.refs_0_.refs_1_), channel_id=1, source_target_pairs={{0,64},{32,480},{64,128},{96,32},{128,192},{160,96},{192,256},{224... | collective-permute-start | bytes 1572872 | tf_op jit(solution)/shard_map/ppermute | solution.py:258
  55.7 0.0 collective-permute-done.4.refs_1_.refs_2_
  55.7 4.2 %collective-permute-start.5 = (bf16[1024,256]{1,0:T(8,128)(2,1)S(1)}, bf16[1024,256]{1,0:T(8,128)(2,1)S(1)}, u32[]{:S(2)}, u32[]{:S(2)}) collective-permute-start(bf16[1024,256]{1,0:T(8,128)(2,1)S(1)} %collective-permute-done.4.refs_1_.refs_2_), channel_id=1, source_target_pairs={{0,64},{32,480},{64,128},{96,32},{128,192},{160,96},{192,256},{224... | collective-permute-start | bytes 1572872 | tf_op jit(solution)/shard_map/ppermute | solution.py:258
  59.9 5.3 %all-to-all-done.1 = bf16[32,24,256]{2,1,0:T(8,128)(2,1)S(1)} async-done(((bf16[32,24,256]{2,1,0:T(8,128)(2,1)}), bf16[32,24,256]{2,1,0:T(8,128)(2,1)S(1)}, u32[]{:S(2)}, u32[]{:S(2)}) %all-to-all-start.1) | async-done | bytes 393248 | tf_op jit(solution)/shard_map/all_to_all | solution.py:243
  65.2 4.0 %own.1 = (f32[768,384]{1,0:T(8,128)S(1)}, f32[768,384]{1,0:T(8,128)S(1)}) custom-call(s32[2,9]{1,0:T(2,128)S(1)} %copy-done.1, bf16[768,128]{1,0:T(8,128)(2,1)S(1)} %bitcast.16, bf16[768,128]{1,0:T(8,128)(2,1)S(1)} %collective-permute-done.other_q_ref.q_ref, bf16[1024,256]{1,0:T(8,128)(2,1)S(1)} %load.1.kv_ref.refs_0_, bf16[768,256]{1,0:T(8,128)(2,1)S(1)} %bitcast.12), custom_call_target="tpu_custom_call" | custom-call | flops 2000000000 | bytes 1 | tf_op jit(solution)/shard_map/own/pallas_call | solution.py:177
  69.2 1.9 %collective-permute-start.7 = (bf16[1024,256]{1,0:T(8,128)(2,1)S(1)}, bf16[1024,256]{1,0:T(8,128)(2,1)S(1)}, u32[]{:S(2)}, u32[]{:S(2)}) collective-permute-start(bf16[1024,256]{1,0:T(8,128)(2,1)S(1)} %collective-permute-done.3.refs_0_.refs_3_), channel_id=1, source_target_pairs={{0,64},{32,480},{64,128},{96,32},{128,192},{160,96},{192,256},{224... | collective-permute-start | bytes 1572872 | tf_op jit(solution)/shard_map/ppermute | solution.py:258
  71.2 3.4 %collective-permute-start.6 = (bf16[1024,256]{1,0:T(8,128)(2,1)S(1)}, bf16[1024,256]{1,0:T(8,128)(2,1)S(1)}, u32[]{:S(2)}, u32[]{:S(2)}) collective-permute-start(bf16[1024,256]{1,0:T(8,128)(2,1)S(1)} %collective-permute-done.5.refs_1_.refs_4_), channel_id=1, source_target_pairs={{0,64},{32,480},{64,128},{96,32},{128,192},{160,96},{192,256},{224... | collective-permute-start | bytes 1572872 | tf_op jit(solution)/shard_map/ppermute | solution.py:258
  74.6 8.3 %collective-permute-start.8 = (bf16[256,256]{1,0:T(8,128)(2,1)S(1)}, bf16[256,256]{1,0:T(8,128)(2,1)S(1)}, u32[]{:S(2)}, u32[]{:S(2)}) collective-permute-start(bf16[256,256]{1,0:T(8,128)(2,1)S(1)} %slice.11), channel_id=1, source_target_pairs={{0,128},{32,416},{64,192},{96,480},{128,256},{160,32},{192,320},{2... | collective-permute-start | bytes 393224 | tf_op jit(solution)/shard_map/ppermute | solution.py:258
  82.8 3.0 %ring.3 = (f32[768,384]{1,0:T(8,128)S(1)}, f32[768,384]{1,0:T(8,128)S(1)}) custom-call(s32[2,9]{1,0:T(2,128)S(1)} %copy-done.1, bf16[768,128]{1,0:T(8,128)(2,1)S(1)} %bitcast.17, bf16[768,128]{1,0:T(8,128)(2,1)S(1)} %collective-permute-done.other_q_ref.q_ref, bf16[1024,256]{1,0:T(8,128)(2,1)S(1)} %collective-permute-done.2.refs_0_.refs_1_, ...), custom_call_target="tpu_custom_call" | custom-call | flops 4000000000 | bytes 1 | tf_op jit(solution)/shard_map/ring/pallas_call | solution.py:177
  85.8 3.2 %ring.4 = (f32[768,384]{1,0:T(8,128)S(1)}, f32[768,384]{1,0:T(8,128)S(1)}) custom-call(s32[2,9]{1,0:T(2,128)S(1)} %copy-done.1, bf16[768,128]{1,0:T(8,128)(2,1)S(1)} %bitcast.18, bf16[768,128]{1,0:T(8,128)(2,1)S(1)} %collective-permute-done.other_q_ref.q_ref, bf16[1024,256]{1,0:T(8,128)(2,1)S(1)} %collective-permute-done.3.refs_0_.refs_3_, ...), custom_call_target="tpu_custom_call" | custom-call | flops 4000000000 | bytes 1 | tf_op jit(solution)/shard_map/ring/pallas_call | solution.py:177
  89.0 0.7 ring.5
  89.8 2.0 %end.3 = f32[1024,256]{1,0:T(8,128)S(1)} custom-call(s32[2,9]{1,0:T(2,128)S(1)} %copy-done.1, s32[2]{0:T(128)S(1)} %copy-done, bf16[768,128]{1,0:T(8,128)(2,1)S(1)} %collective-permute-done.other_q_ref.q_ref, bf16[1024,256]{1,0:T(8,128)(2,1)S(1)} %collective-permute-done.6.kv_ref.refs_6_, f32[768,384]{1,0:T(8,128)S(1)} %get-tuple-element.42.before, ...), custom_call_target="tpu_custom_call" | custom-call | flops 1000000000 | bytes 1 | tf_op jit(solution)/shard_map/end/pallas_call | solution.py:177
  91.8 2.5 %collective-permute-start.9 = (f32[1024,256]{1,0:T(8,128)S(1)}, f32[1024,256]{1,0:T(8,128)S(1)}, u32[]{:S(2)}, u32[]{:S(2)}) collective-permute-start(f32[1024,256]{1,0:T(8,128)S(1)} %end.3), channel_id=1, source_target_pairs={{0,32},{32,0},{64,96},{96,64},{128,160},{160,128},{192,224},{224,1... | collective-permute-start | bytes 3145736 | tf_op jit(solution)/shard_map/ppermute | solution.py:247
  94.3 0.7 end.2.mine_ref
  95.0 1.6 %collective-permute-done.9.other_ref = f32[1024,256]{1,0:T(8,128)S(1)} collective-permute-done((f32[1024,256]{1,0:T(8,128)S(1)}, f32[1024,256]{1,0:T(8,128)S(1)}, u32[]{:S(2)}, u32[]{:S(2)}) %collective-permute-start.9) | collective-permute-done | bytes 1048608 | tf_op jit(solution)/shard_map/ppermute | solution.py:247
  96.6 2.4 %merge.1 = (bf16[768,128]{1,0:T(8,128)(2,1)}, bf16[512,128]{1,0:T(8,128)(2,1)}) custom-call(s32[2]{0:T(128)S(1)} %copy-done, f32[768,256]{1,0:T(8,128)S(1)} %end.2.mine_ref, f32[1024,256]{1,0:T(8,128)S(1)} %collective-permute-done.9.other_ref, bf16[1024,256]{1,0:T(8,128)(2,1)S(1)} %load.1.kv_ref.refs_0_, ...), custom_call_target="tpu_custom_call" | custom-call | flops 1000000000 | bytes 1 | tf_op jit(solution)/shard_map/merge/pallas_call | solution.py:177
  (26 shorter events, 0.1 us)
Async XLA Ops:
  0.6 15.3 %copy-start.5 = (bf16[1,24,512]{2,1,0:T(8,128)(2,1)S(1)}, bf16[1,24,512]{2,1,0:T(8,128)(2,1)}, u32[]{:S(2)}) copy-start(bf16[1,24,512]{2,1,0:T(8,128)(2,1)} %param.10) | copy-start | bytes 73732
  0.6 15.3 %copy-start.6 = (bf16[1,24,512]{2,1,0:T(8,128)(2,1)S(1)}, bf16[1,24,512]{2,1,0:T(8,128)(2,1)}, u32[]{:S(2)}) copy-start(bf16[1,24,512]{2,1,0:T(8,128)(2,1)} %param.11) | copy-start | bytes 73732
  0.7 12.4 %copy-start.2 = (bf16[1,768,128]{2,1,0:T(8,128)(2,1)S(1)}, bf16[1,768,128]{2,1,0:T(8,128)(2,1)}, u32[]{:S(2)}) copy-start(bf16[1,768,128]{2,1,0:T(8,128)(2,1)} %param.9) | copy-start | bytes 589828
  0.7 25.9 %copy-start.8 = (s32[16,8]{0,1:T(8,128)S(1)}, s32[16,8]{0,1:T(8,128)}, u32[]{:S(2)}) copy-start(s32[16,8]{0,1:T(8,128)} %param.16) | copy-start | bytes 1540
  2.4 27.1 %copy-start.3 = (bf16[1,512,128]{2,1,0:T(8,128)(2,1)S(1)}, bf16[1,512,128]{2,1,0:T(8,128)(2,1)}, u32[]{:S(2)}) copy-start(bf16[1,512,128]{2,1,0:T(8,128)(2,1)} %param.13) | copy-start | bytes 393220
  2.4 27.0 %all-to-all-start = ((bf16[32,40,256]{2,1,0:T(8,128)(2,1)}), bf16[32,40,256]{2,1,0:T(8,128)(2,1)S(1)}, u32[]{:S(2)}, u32[]{:S(2)}) async-start(bf16[32,40,256]{2,1,0:T(8,128)(2,1)} %heads.1), calls=%async_computation | async-start | bytes 1310720 | tf_op jit(solution)/shard_map/all_to_all | solution.py:243
  13.0 16.5 %collective-permute-start = (bf16[768,128]{1,0:T(8,128)(2,1)S(1)}, bf16[768,128]{1,0:T(8,128)(2,1)S(1)}, u32[]{:S(2)}, u32[]{:S(2)}) collective-permute-start(bf16[768,128]{1,0:T(8,128)(2,1)S(1)} %bitcast.15), channel_id=1, source_target_pairs={{0,32},{32,0},{64,96},{96,64},{128,160},{160,128},{192,224},{224,1... | collective-permute-start | bytes 589832 | tf_op jit(solution)/shard_map/ppermute | solution.py:247
  15.9 13.5 %collective-permute-start.1 = (bf16[24,1024]{1,0:T(8,128)(2,1)S(1)}, bf16[24,1024]{1,0:T(8,128)(2,1)S(1)}, u32[]{:S(2)}, u32[]{:S(2)}) collective-permute-start(bf16[24,1024]{1,0:T(8,128)(2,1)S(1)} %pad_maximum_fusion), channel_id=1, source_target_pairs={{0,256},{32,288},{64,320},{96,352},{128,384},{160,416},{192,448},{... | collective-permute-start | bytes 147464 | tf_op jit(solution)/shard_map/ppermute | solution.py:252
  28.7 0.8 copy-start.4
  29.5 1.4 %copy-start.7 = (bf16[24,1024]{1,0:T(8,128)(2,1)}, bf16[24,1024]{1,0:T(8,128)(2,1)S(1)}, u32[]{:S(2)}) copy-start(bf16[24,1024]{1,0:T(8,128)(2,1)S(1)} %collective-permute-done.1.both) | copy-start | bytes 147460
  30.9 34.3 %copy-start.1 = (s32[2,9]{1,0:T(2,128)S(1)}, s32[2,9]{1,0:T(2,128)}, u32[]{:S(2)}) copy-start(s32[2,9]{1,0:T(2,128)} %get-tuple-element.25.seen_ref) | copy-start | bytes 220
  30.9 22.6 %collective-permute-start.2 = (bf16[1024,256]{1,0:T(8,128)(2,1)S(1)}, bf16[1024,256]{1,0:T(8,128)(2,1)S(1)}, u32[]{:S(2)}, u32[]{:S(2)}) collective-permute-start(bf16[1024,256]{1,0:T(8,128)(2,1)S(1)} %load.1.kv_ref.refs_0_), channel_id=1, source_target_pairs={{0,64},{32,480},{64,128},{96,32},{128,192},{160,96},{192,256},{224... | collective-permute-start | bytes 1572872 | tf_op jit(solution)/shard_map/ppermute | solution.py:258
  41.6 14.1 %collective-permute-start.4 = (bf16[1024,256]{1,0:T(8,128)(2,1)S(1)}, bf16[1024,256]{1,0:T(8,128)(2,1)S(1)}, u32[]{:S(2)}, u32[]{:S(2)}) collective-permute-start(bf16[1024,256]{1,0:T(8,128)(2,1)S(1)} %load.1.kv_ref.refs_0_), channel_id=1, source_target_pairs={{0,480},{32,64},{64,32},{96,128},{128,96},{160,192},{192,160},{224... | collective-permute-start | bytes 1572872 | tf_op jit(solution)/shard_map/ppermute | solution.py:258
  45.7 19.5 %all-to-all-start.1 = ((bf16[32,24,256]{2,1,0:T(8,128)(2,1)}), bf16[32,24,256]{2,1,0:T(8,128)(2,1)S(1)}, u32[]{:S(2)}, u32[]{:S(2)}) async-start(bf16[32,24,256]{2,1,0:T(8,128)(2,1)} %far_heads.1), calls=%async_computation.1 | async-start | bytes 786432 | tf_op jit(solution)/shard_map/all_to_all | solution.py:243
  53.5 15.7 %collective-permute-start.3 = (bf16[1024,256]{1,0:T(8,128)(2,1)S(1)}, bf16[1024,256]{1,0:T(8,128)(2,1)S(1)}, u32[]{:S(2)}, u32[]{:S(2)}) collective-permute-start(bf16[1024,256]{1,0:T(8,128)(2,1)S(1)} %collective-permute-done.2.refs_0_.refs_1_), channel_id=1, source_target_pairs={{0,64},{32,480},{64,128},{96,32},{128,192},{160,96},{192,256},{224... | collective-permute-start | bytes 1572872 | tf_op jit(solution)/shard_map/ppermute | solution.py:258
  55.7 15.4 %collective-permute-start.5 = (bf16[1024,256]{1,0:T(8,128)(2,1)S(1)}, bf16[1024,256]{1,0:T(8,128)(2,1)S(1)}, u32[]{:S(2)}, u32[]{:S(2)}) collective-permute-start(bf16[1024,256]{1,0:T(8,128)(2,1)S(1)} %collective-permute-done.4.refs_1_.refs_2_), channel_id=1, source_target_pairs={{0,64},{32,480},{64,128},{96,32},{128,192},{160,96},{192,256},{224... | collective-permute-start | bytes 1572872 | tf_op jit(solution)/shard_map/ppermute | solution.py:258
  69.2 19.8 %collective-permute-start.7 = (bf16[1024,256]{1,0:T(8,128)(2,1)S(1)}, bf16[1024,256]{1,0:T(8,128)(2,1)S(1)}, u32[]{:S(2)}, u32[]{:S(2)}) collective-permute-start(bf16[1024,256]{1,0:T(8,128)(2,1)S(1)} %collective-permute-done.3.refs_0_.refs_3_), channel_id=1, source_target_pairs={{0,64},{32,480},{64,128},{96,32},{128,192},{160,96},{192,256},{224... | collective-permute-start | bytes 1572872 | tf_op jit(solution)/shard_map/ppermute | solution.py:258
  71.2 18.6 %collective-permute-start.6 = (bf16[1024,256]{1,0:T(8,128)(2,1)S(1)}, bf16[1024,256]{1,0:T(8,128)(2,1)S(1)}, u32[]{:S(2)}, u32[]{:S(2)}) collective-permute-start(bf16[1024,256]{1,0:T(8,128)(2,1)S(1)} %collective-permute-done.5.refs_1_.refs_4_), channel_id=1, source_target_pairs={{0,64},{32,480},{64,128},{96,32},{128,192},{160,96},{192,256},{224... | collective-permute-start | bytes 1572872 | tf_op jit(solution)/shard_map/ppermute | solution.py:258
  74.6 15.2 %collective-permute-start.8 = (bf16[256,256]{1,0:T(8,128)(2,1)S(1)}, bf16[256,256]{1,0:T(8,128)(2,1)S(1)}, u32[]{:S(2)}, u32[]{:S(2)}) collective-permute-start(bf16[256,256]{1,0:T(8,128)(2,1)S(1)} %slice.11), channel_id=1, source_target_pairs={{0,128},{32,416},{64,192},{96,480},{128,256},{160,32},{192,320},{2... | collective-permute-start | bytes 393224 | tf_op jit(solution)/shard_map/ppermute | solution.py:258
  89.0 0.8 copy-start
  91.8 4.7 %collective-permute-start.9 = (f32[1024,256]{1,0:T(8,128)S(1)}, f32[1024,256]{1,0:T(8,128)S(1)}, u32[]{:S(2)}, u32[]{:S(2)}) collective-permute-start(f32[1024,256]{1,0:T(8,128)S(1)} %end.3), channel_id=1, source_target_pairs={{0,32},{32,0},{64,96},{96,64},{128,160},{160,128},{192,224},{224,1... | collective-permute-start | bytes 3145736 | tf_op jit(solution)/shard_map/ppermute | solution.py:247

commit v5 on v4

--- a/solution.py
+++ b/solution.py
@@ -102,19 +102,22 @@
         both_sides(seen_ref, index, q_ref, other_q_ref, kv_ref, state, other, keys_t)
 
 
-def fetch(slot, riders, target, sem):
+def fetch(slot, riders, target, sem, act):
     for k, ref in enumerate(riders):
 
         @pl.when(slot == k)
         def _():
-            load = pltpu.make_async_copy(ref.at[pl.ds(ref.shape[0] - target.shape[0], target.shape[0]), :], target, sem)
-            load.start()
-            load.wait()
+            rows = target.shape[0]
+            load = pltpu.make_async_copy(ref.at[pl.ds(ref.shape[0] - rows, rows), :], target, sem)
+            getattr(load, act)()
 
 
 def end_kernel(seen_ref, slot_ref, q_ref, kv_ref, before, *refs, which, index):
     riders, (packed, state, keys_t, rider, sem) = refs[:-5], refs[-5:]
     rows = q_ref.shape[0]
+    if riders:
+        rider[...] = jnp.zeros(rider.shape, rider.dtype)
+        fetch(slot_ref[which], riders, rider, sem, "start")
     state[...] = before[...]
 
     @pl.when(seen_ref[which, index] > 0)
@@ -126,8 +129,7 @@
     lane = lax.broadcasted_iota(jnp.int32, (rows, DH), 1)
     packed[:rows, DH:] = jnp.where(lane < DH // 2, state[:, DH : 2 * DH], state[:, 2 * DH :])
     if riders:
-        rider[...] = jnp.zeros(rider.shape, rider.dtype)
-        fetch(slot_ref[which], riders, rider, sem)
+        fetch(slot_ref[which], riders, rider, sem, "wait")
         packed[rows:, :] = rider[...].astype(jnp.float32)
 
 
@@ -135,10 +137,7 @@
     riders, (out, short_out, rider, sem) = refs[:-4], refs[-4:]
     total = out.shape[0]
     rider[...] = other_ref[total:, :].astype(jnp.bfloat16)
-    fetch(slot_ref[0], riders, rider, sem)
-    half = rider.shape[0]
-    short_out[:half, :] = rider[:, :DH]
-    short_out[half:, :] = rider[:, DH:]
+    fetch(slot_ref[0], riders, rider, sem, "start")
     for start in range(0, total, TILE):
         rows = pl.ds(start, TILE)
         mine = mine_ref[rows, 2 * DH - 1 :]
@@ -149,6 +148,10 @@
         sums = mine_ref[rows, :DH] * mine + other_ref[rows, :DH] * other
         weight = mine_ref[rows, DH : DH + 1] * mine + other_ref[rows, DH : DH + 1] * other
         out[rows, :] = (sums / weight).astype(jnp.bfloat16)
+    fetch(slot_ref[0], riders, rider, sem, "wait")
+    half = rider.shape[0]
+    short_out[:half, :] = rider[:, :DH]
+    short_out[half:, :] = rider[:, DH:]
 
 
 def load_kernel(ends_ref, q_ref, kv_ref, own_ref, out_ref):
@@ -322,13 +325,13 @@
         )
 
     states = call(own_kernel, both, (seen, queries, other_queries, load, far), "own", [keys_t])
-    ring = [(load,), (ahead(load), ahead(load, crossing=True))]
+    ring = [(load,), lax.optimization_barrier((ahead(load), ahead(load, crossing=True)))]
     ring.append(tuple(ahead(block) for block in ring[1]))
     even, states = lax.optimization_barrier((ring[2][0], states))
-    last_rider, odd = lax.optimization_barrier((even[rows:], ring[2][1]))
+    states = ring_step(1, ring[1], states)
+    last_rider, odd, states = lax.optimization_barrier((even[rows:], ring[2][1], states))
     ring.append((ahead(even), ahead(odd)))
     last_rider = ahead(last_rider, chips=2)
-    states = ring_step(1, ring[1], states)
     states = ring_step(2, ring[2], states)
     state, other = ring_step(3, ring[3][:1], states)
     end = ring[3][1]

time: 99.9 us -> 104 us (1.041)
  starting transfers between devices: 67.5 us -> 76.7 us
  waiting for transfers between devices: 7.51 us -> 3.41 us
    ppermute x2, starting transfers between devices: 5.34 us -> 11.4 us  [across(): lax.ppermute(block, 'inst', [(i, i ^ 1) for i in range(lax.axis_size('ins...]
    all_to_all x2, waiting for transfers between devices: 5.94 us -> 1.75 us  [swapped(): return lax.all_to_all(blocks, axis, split_axis=0, concat_axis=0, tiled=True)]
    ppermute x7, starting transfers between devices: 33.1 us -> 36.3 us  [ahead(): lax.ppermute(block, 'inst', [(i, ((i ^ 1 if crossing else i) + step(i)) %...]
  transfers between devices with their start and end apart: 12 -> 12, of which waited for: 3 -> 4; matrix products, arithmetic and copies ran while one was open for 1% -> 1% of each run, Pallas kernels for 15% -> 14%
where the time goes in v5:
time: 104 us; the launch traced here: 103 us
  starting transfers between devices  76.7 us (74%)
  Pallas kernels  21.1 us (20%)
  waiting for transfers between devices  3.41 us (3%)
  between operations  1.16 us (1%)
    ppermute x7, starting transfers between devices, ahead(): lax.ppermute(block, 'inst', [(i, ((i ^ 1 if crossing else i) + step(i)) %...  36.3 us
    all_to_all x2, starting transfers between devices, swapped(): return lax.all_to_all(blocks, axis, split_axis=0, concat_axis=0, tiled=True)  18.4 us
    pallas_call x8, Pallas kernels, call(): pl.pallas_call(kernel, out_shape=out_shape, in_specs=specs[:len(specs) -...  16.4 us
    ppermute x2, starting transfers between devices, across(): lax.ppermute(block, 'inst', [(i, i ^ 1) for i in range(lax.axis_size('ins...  11.4 us
    ppermute x1, starting transfers between devices, opposite(): lax.ppermute(block, 'inst', [(i, (i + size // 2) % size) for i in range(s...  10.6 us
  transfers between devices with their start and end apart: 12, of which 4 were waited for; matrix products, arithmetic and copies ran while one was open for 1% of the time, Pallas kernels for 14%

profile of v5, /device:TPU:1, one launch (start us, length us, event | category | flops | bytes accessed | tf_op | source)
XLA Modules:
  0.0 103.2 jit_solution(11884825793206556706)
XLA Ops:
  0.7 1.7 %heads.1 = bf16[32,40,256]{2,1,0:T(8,128)(2,1)} custom-call(bf16[16,512]{1,0:T(8,128)(2,1)} %bitcast.26, bf16[16,512]{1,0:T(8,128)(2,1)} %bitcast.27, bf16[24,512]{1,0:T(8,128)(2,1)} %bitcast.22, bf16[24,512]{1,0:T(8,128)(2,1)} %bitcast.24), custom_call_target="tpu_custom_call" | custom-call | tf_op jit(solution)/shard_map/heads/pallas_call | solution.py:283
  2.4 10.6 %all-to-all-start = ((bf16[32,40,256]{2,1,0:T(8,128)(2,1)}), bf16[32,40,256]{2,1,0:T(8,128)(2,1)S(1)}, u32[]{:S(2)}, u32[]{:S(2)}) async-start(bf16[32,40,256]{2,1,0:T(8,128)(2,1)} %heads.1), calls=%async_computation | async-start | bytes 1310720 | tf_op jit(solution)/shard_map/all_to_all | solution.py:246
  13.0 2.9 %collective-permute-start = (bf16[768,128]{1,0:T(8,128)(2,1)S(1)}, bf16[768,128]{1,0:T(8,128)(2,1)S(1)}, u32[]{:S(2)}, u32[]{:S(2)}) collective-permute-start(bf16[768,128]{1,0:T(8,128)(2,1)S(1)} %bitcast.15), channel_id=1, source_target_pairs={{0,32},{32,0},{64,96},{96,64},{128,160},{160,128},{192,224},{224,1... | collective-permute-start | bytes 589832 | tf_op jit(solution)/shard_map/ppermute | solution.py:250
  15.9 10.6 %collective-permute-start.1 = (bf16[24,1024]{1,0:T(8,128)(2,1)S(1)}, bf16[24,1024]{1,0:T(8,128)(2,1)S(1)}, u32[]{:S(2)}, u32[]{:S(2)}) collective-permute-start(bf16[24,1024]{1,0:T(8,128)(2,1)S(1)} %pad_maximum_fusion), channel_id=1, source_target_pairs={{0,256},{32,288},{64,320},{96,352},{128,384},{160,416},{192,448},{... | collective-permute-start | bytes 147464 | tf_op jit(solution)/shard_map/ppermute | solution.py:255
  26.6 0.7 copy.11.lengths_ref
  27.3 1.4 %plan.1 = (s32[2,9]{1,0:T(2,128)}, s32[2]{0:T(128)}, s32[8]{0:T(128)}) custom-call(s32[1]{0:T(128)} %bitcast.me_ref, s32[16]{0:T(128)} %span_ref.1, s32[16]{0:T(128)} %partner_ref.1, s32[16,8]{1,0:T(8,128)} %copy.11.lengths_ref), custom_call_target="tpu_custom_call" | custom-call | tf_op jit(solution)/shard_map/plan/pallas_call | solution.py:294
  28.7 0.7 all-to-all-done
  29.5 0.0 copy-start.7
  29.5 0.0 collective-permute-done.other_q_ref.q_ref
  29.5 1.4 %load.1.kv_ref.refs_0_ = bf16[1024,256]{1,0:T(8,128)(2,1)S(1)} custom-call(s32[8]{0:T(128)S(1)} %copy-done.4, bf16[512,128]{1,0:T(8,128)(2,1)S(1)} %bitcast.21, bf16[512,256]{1,0:T(8,128)(2,1)S(1)} %bitcast.14, bf16[768,256]{1,0:T(8,128)(2,1)S(1)} %bitcast.13), custom_call_target="tpu_custom_call" | custom-call | flops 1000000000 | bytes 1 | tf_op jit(solution)/shard_map/load/pallas_call | solution.py:180
  30.9 0.0 copy-start.1
  30.9 10.7 %collective-permute-start.2 = (bf16[1024,256]{1,0:T(8,128)(2,1)S(1)}, bf16[1024,256]{1,0:T(8,128)(2,1)S(1)}, u32[]{:S(2)}, u32[]{:S(2)}) collective-permute-start(bf16[1024,256]{1,0:T(8,128)(2,1)S(1)} %load.1.kv_ref.refs_0_), channel_id=1, source_target_pairs={{0,64},{32,480},{64,128},{96,32},{128,192},{160,96},{192,256},{224... | collective-permute-start | bytes 1572872 | tf_op jit(solution)/shard_map/ppermute | solution.py:261
  41.6 2.5 %collective-permute-start.3 = (bf16[1024,256]{1,0:T(8,128)(2,1)S(1)}, bf16[1024,256]{1,0:T(8,128)(2,1)S(1)}, u32[]{:S(2)}, u32[]{:S(2)}) collective-permute-start(bf16[1024,256]{1,0:T(8,128)(2,1)S(1)} %load.1.kv_ref.refs_0_), channel_id=1, source_target_pairs={{0,480},{32,64},{64,32},{96,128},{128,96},{160,192},{192,160},{224... | collective-permute-start | bytes 1572872 | tf_op jit(solution)/shard_map/ppermute | solution.py:261
  44.1 1.6 %far_heads.1 = bf16[32,24,256]{2,1,0:T(8,128)(2,1)} custom-call(bf16[24,1024]{1,0:T(8,128)(2,1)} %copy-done.7), custom_call_target="tpu_custom_call" | custom-call | tf_op jit(solution)/shard_map/far_heads/pallas_call | solution.py:303
  45.7 7.8 %all-to-all-start.1 = ((bf16[32,24,256]{2,1,0:T(8,128)(2,1)}), bf16[32,24,256]{2,1,0:T(8,128)(2,1)S(1)}, u32[]{:S(2)}, u32[]{:S(2)}) async-start(bf16[32,24,256]{2,1,0:T(8,128)(2,1)} %far_heads.1), calls=%async_computation.1 | async-start | bytes 786432 | tf_op jit(solution)/shard_map/all_to_all | solution.py:246
  53.5 0.0 collective-permute-done.2.refs_0_.refs_1_
  53.5 4.8 %collective-permute-start.4 = (bf16[1024,256]{1,0:T(8,128)(2,1)S(1)}, bf16[1024,256]{1,0:T(8,128)(2,1)S(1)}, u32[]{:S(2)}, u32[]{:S(2)}) collective-permute-start(bf16[1024,256]{1,0:T(8,128)(2,1)S(1)} %collective-permute-done.2.refs_0_.refs_1_), channel_id=1, source_target_pairs={{0,64},{32,480},{64,128},{96,32},{128,192},{160,96},{192,256},{224... | collective-permute-start | bytes 1572872 | tf_op jit(solution)/shard_map/ppermute | solution.py:261
  58.4 5.7 %collective-permute-start.5 = (bf16[1024,256]{1,0:T(8,128)(2,1)S(1)}, bf16[1024,256]{1,0:T(8,128)(2,1)S(1)}, u32[]{:S(2)}, u32[]{:S(2)}) collective-permute-start(bf16[1024,256]{1,0:T(8,128)(2,1)S(1)} %collective-permute-done.3.refs_1_.refs_2_), channel_id=1, source_target_pairs={{0,64},{32,480},{64,128},{96,32},{128,192},{160,96},{192,256},{224... | collective-permute-start | bytes 1572872 | tf_op jit(solution)/shard_map/ppermute | solution.py:261
  64.1 1.1 %all-to-all-done.1 = bf16[32,24,256]{2,1,0:T(8,128)(2,1)S(1)} async-done(((bf16[32,24,256]{2,1,0:T(8,128)(2,1)}), bf16[32,24,256]{2,1,0:T(8,128)(2,1)S(1)}, u32[]{:S(2)}, u32[]{:S(2)}) %all-to-all-start.1) | async-done | bytes 393248 | tf_op jit(solution)/shard_map/all_to_all | solution.py:246
  65.2 5.1 %own.1 = (f32[768,384]{1,0:T(8,128)S(1)}, f32[768,384]{1,0:T(8,128)S(1)}) custom-call(s32[2,9]{1,0:T(2,128)S(1)} %copy-done.1, bf16[768,128]{1,0:T(8,128)(2,1)S(1)} %bitcast.16, bf16[768,128]{1,0:T(8,128)(2,1)S(1)} %collective-permute-done.other_q_ref.q_ref, bf16[1024,256]{1,0:T(8,128)(2,1)S(1)} %load.1.kv_ref.refs_0_, bf16[768,256]{1,0:T(8,128)(2,1)S(1)} %bitcast.12), custom_call_target="tpu_custom_call" | custom-call | flops 2000000000 | bytes 1 | tf_op jit(solution)/shard_map/own/pallas_call | solution.py:180
  70.3 1.9 %collective-permute-start.7 = (bf16[1024,256]{1,0:T(8,128)(2,1)S(1)}, bf16[1024,256]{1,0:T(8,128)(2,1)S(1)}, u32[]{:S(2)}, u32[]{:S(2)}) collective-permute-start(bf16[1024,256]{1,0:T(8,128)(2,1)S(1)} %collective-permute-done.4.refs_0_.refs_3_), channel_id=1, source_target_pairs={{0,64},{32,480},{64,128},{96,32},{128,192},{160,96},{192,256},{224... | collective-permute-start | bytes 1572872 | tf_op jit(solution)/shard_map/ppermute | solution.py:261
  72.2 1.9 %ring.3 = (f32[768,384]{1,0:T(8,128)S(1)}, f32[768,384]{1,0:T(8,128)S(1)}) custom-call(s32[2,9]{1,0:T(2,128)S(1)} %copy-done.1, bf16[768,128]{1,0:T(8,128)(2,1)S(1)} %bitcast.17, bf16[768,128]{1,0:T(8,128)(2,1)S(1)} %collective-permute-done.other_q_ref.q_ref, bf16[1024,256]{1,0:T(8,128)(2,1)S(1)} %collective-permute-done.2.refs_0_.refs_1_, ...), custom_call_target="tpu_custom_call" | custom-call | flops 4000000000 | bytes 1 | tf_op jit(solution)/shard_map/ring/pallas_call | solution.py:180
  74.1 3.1 %collective-permute-start.6 = (bf16[1024,256]{1,0:T(8,128)(2,1)S(1)}, bf16[1024,256]{1,0:T(8,128)(2,1)S(1)}, u32[]{:S(2)}, u32[]{:S(2)}) collective-permute-start(bf16[1024,256]{1,0:T(8,128)(2,1)S(1)} %collective-permute-done.5.refs_1_.refs_4_), channel_id=1, source_target_pairs={{0,64},{32,480},{64,128},{96,32},{128,192},{160,96},{192,256},{224... | collective-permute-start | bytes 1572872 | tf_op jit(solution)/shard_map/ppermute | solution.py:261
  77.2 7.5 %collective-permute-start.8 = (bf16[256,256]{1,0:T(8,128)(2,1)S(1)}, bf16[256,256]{1,0:T(8,128)(2,1)S(1)}, u32[]{:S(2)}, u32[]{:S(2)}) collective-permute-start(bf16[256,256]{1,0:T(8,128)(2,1)S(1)} %slice.11), channel_id=1, source_target_pairs={{0,128},{32,416},{64,192},{96,480},{128,256},{160,32},{192,320},{2... | collective-permute-start | bytes 393224 | tf_op jit(solution)/shard_map/ppermute | solution.py:261
  84.8 2.1 %ring.4 = (f32[768,384]{1,0:T(8,128)S(1)}, f32[768,384]{1,0:T(8,128)S(1)}) custom-call(s32[2,9]{1,0:T(2,128)S(1)} %copy-done.1, bf16[768,128]{1,0:T(8,128)(2,1)S(1)} %bitcast.18, bf16[768,128]{1,0:T(8,128)(2,1)S(1)} %collective-permute-done.other_q_ref.q_ref, bf16[1024,256]{1,0:T(8,128)(2,1)S(1)} %collective-permute-done.4.refs_0_.refs_3_, ...), custom_call_target="tpu_custom_call" | custom-call | flops 4000000000 | bytes 1 | tf_op jit(solution)/shard_map/ring/pallas_call | solution.py:180
  86.9 1.9 %ring.5 = (f32[768,384]{1,0:T(8,128)S(1)}, f32[768,384]{1,0:T(8,128)S(1)}) custom-call(s32[2,9]{1,0:T(2,128)S(1)} %copy-done.1, bf16[768,128]{1,0:T(8,128)(2,1)S(1)} %bitcast.19, bf16[768,128]{1,0:T(8,128)(2,1)S(1)} %collective-permute-done.other_q_ref.q_ref, bf16[1024,256]{1,0:T(8,128)(2,1)S(1)} %collective-permute-done.7.refs_0_.refs_5_, ...), custom_call_target="tpu_custom_call" | custom-call | flops 4000000000 | bytes 1 | tf_op jit(solution)/shard_map/ring/pallas_call | solution.py:180
  88.8 0.1 collective-permute-done.8.refs_7_
  88.9 0.9 end.3
  89.8 8.5 %collective-permute-start.9 = (f32[1024,256]{1,0:T(8,128)S(1)}, f32[1024,256]{1,0:T(8,128)S(1)}, u32[]{:S(2)}, u32[]{:S(2)}) collective-permute-start(f32[1024,256]{1,0:T(8,128)S(1)} %end.3), channel_id=1, source_target_pairs={{0,32},{32,0},{64,96},{96,64},{128,160},{160,128},{192,224},{224,1... | collective-permute-start | bytes 3145736 | tf_op jit(solution)/shard_map/ppermute | solution.py:250
  98.3 0.7 end.2.mine_ref
  99.1 1.6 %collective-permute-done.9.other_ref = f32[1024,256]{1,0:T(8,128)S(1)} collective-permute-done((f32[1024,256]{1,0:T(8,128)S(1)}, f32[1024,256]{1,0:T(8,128)S(1)}, u32[]{:S(2)}, u32[]{:S(2)}) %collective-permute-start.9) | collective-permute-done | bytes 1048608 | tf_op jit(solution)/shard_map/ppermute | solution.py:250
  100.6 2.4 %merge.1 = (bf16[768,128]{1,0:T(8,128)(2,1)}, bf16[512,128]{1,0:T(8,128)(2,1)}) custom-call(s32[2]{0:T(128)S(1)} %copy-done, f32[768,256]{1,0:T(8,128)S(1)} %end.2.mine_ref, f32[1024,256]{1,0:T(8,128)S(1)} %collective-permute-done.9.other_ref, bf16[1024,256]{1,0:T(8,128)(2,1)S(1)} %load.1.kv_ref.refs_0_, ...), custom_call_target="tpu_custom_call" | custom-call | flops 1000000000 | bytes 1 | tf_op jit(solution)/shard_map/merge/pallas_call | solution.py:180
  (26 shorter events, 0.1 us)
Async XLA Ops:
  0.6 15.3 %copy-start.5 = (bf16[1,24,512]{2,1,0:T(8,128)(2,1)S(1)}, bf16[1,24,512]{2,1,0:T(8,128)(2,1)}, u32[]{:S(2)}) copy-start(bf16[1,24,512]{2,1,0:T(8,128)(2,1)} %param.10) | copy-start | bytes 73732
  0.6 15.3 %copy-start.6 = (bf16[1,24,512]{2,1,0:T(8,128)(2,1)S(1)}, bf16[1,24,512]{2,1,0:T(8,128)(2,1)}, u32[]{:S(2)}) copy-start(bf16[1,24,512]{2,1,0:T(8,128)(2,1)} %param.11) | copy-start | bytes 73732
  0.7 12.4 %copy-start.2 = (bf16[1,768,128]{2,1,0:T(8,128)(2,1)S(1)}, bf16[1,768,128]{2,1,0:T(8,128)(2,1)}, u32[]{:S(2)}) copy-start(bf16[1,768,128]{2,1,0:T(8,128)(2,1)} %param.9) | copy-start | bytes 589828
  0.7 25.9 %copy-start.8 = (s32[16,8]{0,1:T(8,128)S(1)}, s32[16,8]{0,1:T(8,128)}, u32[]{:S(2)}) copy-start(s32[16,8]{0,1:T(8,128)} %param.16) | copy-start | bytes 1540
  2.4 27.1 %copy-start.3 = (bf16[1,512,128]{2,1,0:T(8,128)(2,1)S(1)}, bf16[1,512,128]{2,1,0:T(8,128)(2,1)}, u32[]{:S(2)}) copy-start(bf16[1,512,128]{2,1,0:T(8,128)(2,1)} %param.13) | copy-start | bytes 393220
  2.4 27.0 %all-to-all-start = ((bf16[32,40,256]{2,1,0:T(8,128)(2,1)}), bf16[32,40,256]{2,1,0:T(8,128)(2,1)S(1)}, u32[]{:S(2)}, u32[]{:S(2)}) async-start(bf16[32,40,256]{2,1,0:T(8,128)(2,1)} %heads.1), calls=%async_computation | async-start | bytes 1310720 | tf_op jit(solution)/shard_map/all_to_all | solution.py:246
  13.0 16.5 %collective-permute-start = (bf16[768,128]{1,0:T(8,128)(2,1)S(1)}, bf16[768,128]{1,0:T(8,128)(2,1)S(1)}, u32[]{:S(2)}, u32[]{:S(2)}) collective-permute-start(bf16[768,128]{1,0:T(8,128)(2,1)S(1)} %bitcast.15), channel_id=1, source_target_pairs={{0,32},{32,0},{64,96},{96,64},{128,160},{160,128},{192,224},{224,1... | collective-permute-start | bytes 589832 | tf_op jit(solution)/shard_map/ppermute | solution.py:250
  15.9 13.5 %collective-permute-start.1 = (bf16[24,1024]{1,0:T(8,128)(2,1)S(1)}, bf16[24,1024]{1,0:T(8,128)(2,1)S(1)}, u32[]{:S(2)}, u32[]{:S(2)}) collective-permute-start(bf16[24,1024]{1,0:T(8,128)(2,1)S(1)} %pad_maximum_fusion), channel_id=1, source_target_pairs={{0,256},{32,288},{64,320},{96,352},{128,384},{160,416},{192,448},{... | collective-permute-start | bytes 147464 | tf_op jit(solution)/shard_map/ppermute | solution.py:255
  28.7 0.8 copy-start.4
  29.5 1.4 %copy-start.7 = (bf16[24,1024]{1,0:T(8,128)(2,1)}, bf16[24,1024]{1,0:T(8,128)(2,1)S(1)}, u32[]{:S(2)}) copy-start(bf16[24,1024]{1,0:T(8,128)(2,1)S(1)} %collective-permute-done.1.both) | copy-start | bytes 147460
  30.9 34.3 %copy-start.1 = (s32[2,9]{1,0:T(2,128)S(1)}, s32[2,9]{1,0:T(2,128)}, u32[]{:S(2)}) copy-start(s32[2,9]{1,0:T(2,128)} %get-tuple-element.29.seen_ref) | copy-start | bytes 220
  30.9 22.6 %collective-permute-start.2 = (bf16[1024,256]{1,0:T(8,128)(2,1)S(1)}, bf16[1024,256]{1,0:T(8,128)(2,1)S(1)}, u32[]{:S(2)}, u32[]{:S(2)}) collective-permute-start(bf16[1024,256]{1,0:T(8,128)(2,1)S(1)} %load.1.kv_ref.refs_0_), channel_id=1, source_target_pairs={{0,64},{32,480},{64,128},{96,32},{128,192},{160,96},{192,256},{224... | collective-permute-start | bytes 1572872 | tf_op jit(solution)/shard_map/ppermute | solution.py:261
  41.6 11.9 %collective-permute-start.3 = (bf16[1024,256]{1,0:T(8,128)(2,1)S(1)}, bf16[1024,256]{1,0:T(8,128)(2,1)S(1)}, u32[]{:S(2)}, u32[]{:S(2)}) collective-permute-start(bf16[1024,256]{1,0:T(8,128)(2,1)S(1)} %load.1.kv_ref.refs_0_), channel_id=1, source_target_pairs={{0,480},{32,64},{64,32},{96,128},{128,96},{160,192},{192,160},{224... | collective-permute-start | bytes 1572872 | tf_op jit(solution)/shard_map/ppermute | solution.py:261
  45.7 19.5 %all-to-all-start.1 = ((bf16[32,24,256]{2,1,0:T(8,128)(2,1)}), bf16[32,24,256]{2,1,0:T(8,128)(2,1)S(1)}, u32[]{:S(2)}, u32[]{:S(2)}) async-start(bf16[32,24,256]{2,1,0:T(8,128)(2,1)} %far_heads.1), calls=%async_computation.1 | async-start | bytes 786432 | tf_op jit(solution)/shard_map/all_to_all | solution.py:246
  53.5 16.7 %collective-permute-start.4 = (bf16[1024,256]{1,0:T(8,128)(2,1)S(1)}, bf16[1024,256]{1,0:T(8,128)(2,1)S(1)}, u32[]{:S(2)}, u32[]{:S(2)}) collective-permute-start(bf16[1024,256]{1,0:T(8,128)(2,1)S(1)} %collective-permute-done.2.refs_0_.refs_1_), channel_id=1, source_target_pairs={{0,64},{32,480},{64,128},{96,32},{128,192},{160,96},{192,256},{224... | collective-permute-start | bytes 1572872 | tf_op jit(solution)/shard_map/ppermute | solution.py:261
  58.4 15.7 %collective-permute-start.5 = (bf16[1024,256]{1,0:T(8,128)(2,1)S(1)}, bf16[1024,256]{1,0:T(8,128)(2,1)S(1)}, u32[]{:S(2)}, u32[]{:S(2)}) collective-permute-start(bf16[1024,256]{1,0:T(8,128)(2,1)S(1)} %collective-permute-done.3.refs_1_.refs_2_), channel_id=1, source_target_pairs={{0,64},{32,480},{64,128},{96,32},{128,192},{160,96},{192,256},{224... | collective-permute-start | bytes 1572872 | tf_op jit(solution)/shard_map/ppermute | solution.py:261
  70.3 16.6 %collective-permute-start.7 = (bf16[1024,256]{1,0:T(8,128)(2,1)S(1)}, bf16[1024,256]{1,0:T(8,128)(2,1)S(1)}, u32[]{:S(2)}, u32[]{:S(2)}) collective-permute-start(bf16[1024,256]{1,0:T(8,128)(2,1)S(1)} %collective-permute-done.4.refs_0_.refs_3_), channel_id=1, source_target_pairs={{0,64},{32,480},{64,128},{96,32},{128,192},{160,96},{192,256},{224... | collective-permute-start | bytes 1572872 | tf_op jit(solution)/shard_map/ppermute | solution.py:261
  74.1 14.8 %collective-permute-start.6 = (bf16[1024,256]{1,0:T(8,128)(2,1)S(1)}, bf16[1024,256]{1,0:T(8,128)(2,1)S(1)}, u32[]{:S(2)}, u32[]{:S(2)}) collective-permute-start(bf16[1024,256]{1,0:T(8,128)(2,1)S(1)} %collective-permute-done.5.refs_1_.refs_4_), channel_id=1, source_target_pairs={{0,64},{32,480},{64,128},{96,32},{128,192},{160,96},{192,256},{224... | collective-permute-start | bytes 1572872 | tf_op jit(solution)/shard_map/ppermute | solution.py:261
  77.2 11.6 %collective-permute-start.8 = (bf16[256,256]{1,0:T(8,128)(2,1)S(1)}, bf16[256,256]{1,0:T(8,128)(2,1)S(1)}, u32[]{:S(2)}, u32[]{:S(2)}) collective-permute-start(bf16[256,256]{1,0:T(8,128)(2,1)S(1)} %slice.11), channel_id=1, source_target_pairs={{0,128},{32,416},{64,192},{96,480},{128,256},{160,32},{192,320},{2... | collective-permute-start | bytes 393224 | tf_op jit(solution)/shard_map/ppermute | solution.py:261
  86.9 2.0 %copy-start = (s32[2]{0:T(128)S(1)}, s32[2]{0:T(128)}, u32[]{:S(2)}) copy-start(s32[2]{0:T(128)} %get-tuple-element.28.slot_ref) | copy-start | bytes 28
  89.8 10.8 %collective-permute-start.9 = (f32[1024,256]{1,0:T(8,128)S(1)}, f32[1024,256]{1,0:T(8,128)S(1)}, u32[]{:S(2)}, u32[]{:S(2)}) collective-permute-start(f32[1024,256]{1,0:T(8,128)S(1)} %end.3), channel_id=1, source_target_pairs={{0,32},{32,0},{64,96},{96,64},{128,160},{160,128},{192,224},{224,1... | collective-permute-start | bytes 3145736 | tf_op jit(solution)/shard_map/ppermute | solution.py:250

commit v6 on v5

--- a/solution.py
+++ b/solution.py
@@ -112,7 +112,19 @@
             getattr(load, act)()
 
 
-def end_kernel(seen_ref, slot_ref, q_ref, kv_ref, before, *refs, which, index):
+def side_kernel(seen_ref, q_ref, kv_ref, before, state, keys_t, *, which, index):
+    rows = q_ref.shape[0]
+    state[...] = before[...]
+
+    @pl.when(seen_ref[which, index] > 0)
+    def _():
+        keys_t[...] = kv_ref[:rows, :DH].T
+        add_block(q_ref, keys_t[...], kv_ref[:rows, DH:], state)
+
+
+def end_kernel(seen_ref, slot_ref, q_ref, *refs, which, indices):
+    count = len(indices)
+    kv_refs, before, refs = refs[:count], refs[count], refs[count + 1 :]
     riders, (packed, state, keys_t, rider, sem) = refs[:-5], refs[-5:]
     rows = q_ref.shape[0]
     if riders:
@@ -120,10 +132,12 @@
         fetch(slot_ref[which], riders, rider, sem, "start")
     state[...] = before[...]
 
-    @pl.when(seen_ref[which, index] > 0)
-    def _():
-        keys_t[...] = kv_ref[:rows, :DH].T
-        add_block(q_ref, keys_t[...], kv_ref[:rows, DH:], state)
+    for index, kv_ref in zip(indices, kv_refs):
+
+        @pl.when(seen_ref[which, index] > 0)
+        def _():
+            keys_t[...] = kv_ref[:rows, :DH].T
+            add_block(q_ref, keys_t[...], kv_ref[:rows, DH:], state)
 
     packed[:rows, :DH] = state[:, :DH]
     lane = lax.broadcasted_iota(jnp.int32, (rows, DH), 1)
@@ -325,33 +339,40 @@
         )
 
     states = call(own_kernel, both, (seen, queries, other_queries, load, far), "own", [keys_t])
-    ring = [(load,), lax.optimization_barrier((ahead(load), ahead(load, crossing=True)))]
+    ring = [(load,), (ahead(load), ahead(load, crossing=True))]
     ring.append(tuple(ahead(block) for block in ring[1]))
     even, states = lax.optimization_barrier((ring[2][0], states))
-    states = ring_step(1, ring[1], states)
-    last_rider, odd, states = lax.optimization_barrier((even[rows:], ring[2][1], states))
+    last_rider, odd = lax.optimization_barrier((even[rows:], ring[2][1]))
     ring.append((ahead(even), ahead(odd)))
     last_rider = ahead(last_rider, chips=2)
+    states = ring_step(1, ring[1], states)
     states = ring_step(2, ring[2], states)
-    state, other = ring_step(3, ring[3][:1], states)
+    state, other = states
+    other = call(
+        functools.partial(side_kernel, which=1, index=chips - 2),
+        state_of(rows),
+        (seen, other_queries, ring[3][0], other),
+        "end",
+        [keys_t],
+    )
     end = ring[3][1]
 
     riders = [block for pair in ring for block in pair] + [last_rider]
     rider_space = [pltpu.VMEM((short_rows // 2, 2 * DH), jnp.bfloat16), pltpu.SemaphoreType.DMA]
     end_space = [pltpu.VMEM((rows, 3 * DH), jnp.float32), keys_t] + rider_space
 
-    def ending(which, q, before, riders):
+    def ending(which, q, blocks, indices, before, riders):
         return call(
-            functools.partial(end_kernel, which=which, index=chips - 1),
+            functools.partial(end_kernel, which=which, indices=indices),
             state_of(rows + (short_rows // 2 if riders else 0), 2 * DH),
-            (seen, slot, q, end, before, *riders),
+            (seen, slot, q, *blocks, before, *riders),
             "end",
             end_space,
             len(riders),
         )
 
-    other = across(ending(1, other_queries, other, riders))
-    state = ending(0, queries, state, [])
+    other = across(ending(1, other_queries, (end,), (chips - 1,), other, riders))
+    state = ending(0, queries, (ring[3][0], end), (chips - 2, chips - 1), state, [])
     prompt_out, short_out = call(
         merge_kernel,
         (jax.ShapeDtypeStruct((rows, DH), jnp.bfloat16), jax.ShapeDtypeStruct((short_rows, DH), jnp.bfloat16)),

time: 104 us -> 103 us (level)
  starting transfers between devices: 76.7 us -> 69.8 us
  Pallas kernels: 21.1 us -> 24.4 us
  waiting for transfers between devices: 3.41 us -> 6.41 us
    ppermute x7, starting transfers between devices: 36.3 us -> 31.8 us  [ahead(): lax.ppermute(block, 'inst', [(i, ((i ^ 1 if crossing else i) + step(i)) %...]
    all_to_all x2, waiting for transfers between devices: 1.75 us -> 5.94 us  [swapped(): return lax.all_to_all(blocks, axis, split_axis=0, concat_axis=0, tiled=True)]
    pallas_call x8, Pallas kernels: 16.4 us -> 19.7 us  [call(): pl.pallas_call(kernel, out_shape=out_shape, in_specs=specs[:len(specs) -...]
    ppermute x2, starting transfers between devices: 11.4 us -> 8.93 us  [across(): lax.ppermute(block, 'inst', [(i, i ^ 1) for i in range(lax.axis_size('ins...]
    ppermute x2, waiting for transfers between devices: 1.55 us -> 0.46 us  [across(): lax.ppermute(block, 'inst', [(i, i ^ 1) for i in range(lax.axis_size('ins...]
  transfers between devices with their start and end apart: 12 -> 12, of which waited for: 4 -> 3; matrix products, arithmetic and copies ran while one was open for 1% -> 1% of each run, Pallas kernels for 14% -> 17%
where the time goes in v6:
time: 103 us
  starting transfers between devices  69.8 us (68%)
  Pallas kernels  24.4 us (24%)
  waiting for transfers between devices  6.41 us (6%)
  between operations  1.18 us (1%)
    ppermute x7, starting transfers between devices, ahead(): lax.ppermute(block, 'inst', [(i, ((i ^ 1 if crossing else i) + step(i)) %...  31.8 us
    pallas_call x8, Pallas kernels, call(): pl.pallas_call(kernel, out_shape=out_shape, in_specs=specs[:len(specs) -...  19.7 us
    all_to_all x2, starting transfers between devices, swapped(): return lax.all_to_all(blocks, axis, split_axis=0, concat_axis=0, tiled=True)  18.4 us
    ppermute x1, starting transfers between devices, opposite(): lax.ppermute(block, 'inst', [(i, (i + size // 2) % size) for i in range(s...  10.6 us
    ppermute x2, starting transfers between devices, across(): lax.ppermute(block, 'inst', [(i, i ^ 1) for i in range(lax.axis_size('ins...  8.93 us
    all_to_all x2, waiting for transfers between devices, swapped(): return lax.all_to_all(blocks, axis, split_axis=0, concat_axis=0, tiled=True)  5.94 us
  transfers between devices with their start and end apart: 12, of which 3 were waited for; matrix products, arithmetic and copies ran while one was open for 1% of the time, Pallas kernels for 17%

profile of v6, /device:TPU:1, one launch (start us, length us, event | category | flops | bytes accessed | tf_op | source)
XLA Modules:
  0.0 102.5 jit_solution(13087516012697995527)
XLA Ops:
  0.7 1.7 %heads.1 = bf16[32,40,256]{2,1,0:T(8,128)(2,1)} custom-call(bf16[16,512]{1,0:T(8,128)(2,1)} %bitcast.25, bf16[16,512]{1,0:T(8,128)(2,1)} %bitcast.26, bf16[24,512]{1,0:T(8,128)(2,1)} %bitcast.21, bf16[24,512]{1,0:T(8,128)(2,1)} %bitcast.23), custom_call_target="tpu_custom_call" | custom-call | tf_op jit(solution)/shard_map/heads/pallas_call | solution.py:297
  2.4 10.6 %all-to-all-start = ((bf16[32,40,256]{2,1,0:T(8,128)(2,1)}), bf16[32,40,256]{2,1,0:T(8,128)(2,1)S(1)}, u32[]{:S(2)}, u32[]{:S(2)}) async-start(bf16[32,40,256]{2,1,0:T(8,128)(2,1)} %heads.1), calls=%async_computation | async-start | bytes 1310720 | tf_op jit(solution)/shard_map/all_to_all | solution.py:260
  13.0 2.9 %collective-permute-start = (bf16[768,128]{1,0:T(8,128)(2,1)S(1)}, bf16[768,128]{1,0:T(8,128)(2,1)S(1)}, u32[]{:S(2)}, u32[]{:S(2)}) collective-permute-start(bf16[768,128]{1,0:T(8,128)(2,1)S(1)} %bitcast.15), channel_id=1, source_target_pairs={{0,32},{32,0},{64,96},{96,64},{128,160},{160,128},{192,224},{224,1... | collective-permute-start | bytes 589832 | tf_op jit(solution)/shard_map/ppermute | solution.py:264
  16.0 10.6 %collective-permute-start.1 = (bf16[24,1024]{1,0:T(8,128)(2,1)S(1)}, bf16[24,1024]{1,0:T(8,128)(2,1)S(1)}, u32[]{:S(2)}, u32[]{:S(2)}) collective-permute-start(bf16[24,1024]{1,0:T(8,128)(2,1)S(1)} %pad_maximum_fusion), channel_id=1, source_target_pairs={{0,256},{32,288},{64,320},{96,352},{128,384},{160,416},{192,448},{... | collective-permute-start | bytes 147464 | tf_op jit(solution)/shard_map/ppermute | solution.py:269
  26.6 0.7 copy.11.lengths_ref
  27.3 1.4 %plan.1 = (s32[2,9]{1,0:T(2,128)}, s32[2]{0:T(128)}, s32[8]{0:T(128)}) custom-call(s32[1]{0:T(128)} %bitcast.me_ref, s32[16]{0:T(128)} %span_ref.1, s32[16]{0:T(128)} %partner_ref.1, s32[16,8]{1,0:T(8,128)} %copy.11.lengths_ref), custom_call_target="tpu_custom_call" | custom-call | tf_op jit(solution)/shard_map/plan/pallas_call | solution.py:308
  28.7 0.7 all-to-all-done
  29.5 0.0 collective-permute-done.1.both
  29.5 0.0 copy-start.7
  29.5 0.0 collective-permute-done.other_q_ref.q_ref
  29.5 1.4 %load.1.kv_ref.refs_2_.refs_0_ = bf16[1024,256]{1,0:T(8,128)(2,1)S(1)} custom-call(s32[8]{0:T(128)S(1)} %copy-done.4, bf16[512,128]{1,0:T(8,128)(2,1)S(1)} %bitcast.20, bf16[512,256]{1,0:T(8,128)(2,1)S(1)} %bitcast.14, bf16[768,256]{1,0:T(8,128)(2,1)S(1)} %bitcast.13), custom_call_target="tpu_custom_call" | custom-call | flops 1000000000 | bytes 1 | tf_op jit(solution)/shard_map/load/pallas_call | solution.py:194
  30.9 0.0 copy-start.1
  30.9 10.7 %collective-permute-start.2 = (bf16[1024,256]{1,0:T(8,128)(2,1)S(1)}, bf16[1024,256]{1,0:T(8,128)(2,1)S(1)}, u32[]{:S(2)}, u32[]{:S(2)}) collective-permute-start(bf16[1024,256]{1,0:T(8,128)(2,1)S(1)} %load.1.kv_ref.refs_2_.refs_0_), channel_id=1, source_target_pairs={{0,64},{32,480},{64,128},{96,32},{128,192},{160,96},{192,256},{224... | collective-permute-start | bytes 1572872 | tf_op jit(solution)/shard_map/ppermute | solution.py:275
  41.6 2.5 %collective-permute-start.5 = (bf16[1024,256]{1,0:T(8,128)(2,1)S(1)}, bf16[1024,256]{1,0:T(8,128)(2,1)S(1)}, u32[]{:S(2)}, u32[]{:S(2)}) collective-permute-start(bf16[1024,256]{1,0:T(8,128)(2,1)S(1)} %load.1.kv_ref.refs_2_.refs_0_), channel_id=1, source_target_pairs={{0,480},{32,64},{64,32},{96,128},{128,96},{160,192},{192,160},{224... | collective-permute-start | bytes 1572872 | tf_op jit(solution)/shard_map/ppermute | solution.py:275
  44.1 1.6 %far_heads.1 = bf16[32,24,256]{2,1,0:T(8,128)(2,1)} custom-call(bf16[24,1024]{1,0:T(8,128)(2,1)} %copy-done.7), custom_call_target="tpu_custom_call" | custom-call | tf_op jit(solution)/shard_map/far_heads/pallas_call | solution.py:317
  45.7 7.8 %all-to-all-start.1 = ((bf16[32,24,256]{2,1,0:T(8,128)(2,1)}), bf16[32,24,256]{2,1,0:T(8,128)(2,1)S(1)}, u32[]{:S(2)}, u32[]{:S(2)}) async-start(bf16[32,24,256]{2,1,0:T(8,128)(2,1)} %far_heads.1), calls=%async_computation.1 | async-start | bytes 786432 | tf_op jit(solution)/shard_map/all_to_all | solution.py:260
  53.5 0.0 collective-permute-done.2.refs_0_.refs_3_.refs_1_
  53.5 2.2 %collective-permute-start.3 = (bf16[1024,256]{1,0:T(8,128)(2,1)S(1)}, bf16[1024,256]{1,0:T(8,128)(2,1)S(1)}, u32[]{:S(2)}, u32[]{:S(2)}) collective-permute-start(bf16[1024,256]{1,0:T(8,128)(2,1)S(1)} %collective-permute-done.2.refs_0_.refs_3_.refs_1_), channel_id=1, source_target_pairs={{0,64},{32,480},{64,128},{96,32},{128,192},{160,96},{192,256},{224... | collective-permute-start | bytes 1572872 | tf_op jit(solution)/shard_map/ppermute | solution.py:275
  55.7 4.2 %collective-permute-start.6 = (bf16[1024,256]{1,0:T(8,128)(2,1)S(1)}, bf16[1024,256]{1,0:T(8,128)(2,1)S(1)}, u32[]{:S(2)}, u32[]{:S(2)}) collective-permute-start(bf16[1024,256]{1,0:T(8,128)(2,1)S(1)} %collective-permute-done.5.refs_1_.refs_4_.refs_2_), channel_id=1, source_target_pairs={{0,64},{32,480},{64,128},{96,32},{128,192},{160,96},{192,256},{224... | collective-permute-start | bytes 1572872 | tf_op jit(solution)/shard_map/ppermute | solution.py:275
  59.9 5.3 %all-to-all-done.1 = bf16[32,24,256]{2,1,0:T(8,128)(2,1)S(1)} async-done(((bf16[32,24,256]{2,1,0:T(8,128)(2,1)}), bf16[32,24,256]{2,1,0:T(8,128)(2,1)S(1)}, u32[]{:S(2)}, u32[]{:S(2)}) %all-to-all-start.1) | async-done | bytes 393248 | tf_op jit(solution)/shard_map/all_to_all | solution.py:260
  65.2 4.0 %own.1 = (f32[768,384]{1,0:T(8,128)S(1)}, f32[768,384]{1,0:T(8,128)S(1)}) custom-call(s32[2,9]{1,0:T(2,128)S(1)} %copy-done.1, bf16[768,128]{1,0:T(8,128)(2,1)S(1)} %bitcast.16, bf16[768,128]{1,0:T(8,128)(2,1)S(1)} %collective-permute-done.other_q_ref.q_ref, bf16[1024,256]{1,0:T(8,128)(2,1)S(1)} %load.1.kv_ref.refs_2_.refs_0_, bf16[768,256]{1,0:T(8,128)(2,1)S(1)} %bitcast.12), custom_call_target="tpu_custom_call" | custom-call | flops 2000000000 | bytes 1 | tf_op jit(solution)/shard_map/own/pallas_call | solution.py:194
  69.3 1.9 %collective-permute-start.4 = (bf16[1024,256]{1,0:T(8,128)(2,1)S(1)}, bf16[1024,256]{1,0:T(8,128)(2,1)S(1)}, u32[]{:S(2)}, u32[]{:S(2)}) collective-permute-start(bf16[1024,256]{1,0:T(8,128)(2,1)S(1)} %collective-permute-done.3.refs_0_.refs_5_.refs_3_), channel_id=1, source_target_pairs={{0,64},{32,480},{64,128},{96,32},{128,192},{160,96},{192,256},{224... | collective-permute-start | bytes 1572872 | tf_op jit(solution)/shard_map/ppermute | solution.py:275
  71.2 8.4 %collective-permute-start.8 = (bf16[256,256]{1,0:T(8,128)(2,1)S(1)}, bf16[256,256]{1,0:T(8,128)(2,1)S(1)}, u32[]{:S(2)}, u32[]{:S(2)}) collective-permute-start(bf16[256,256]{1,0:T(8,128)(2,1)S(1)} %slice.11), channel_id=1, source_target_pairs={{0,128},{32,416},{64,192},{96,480},{128,256},{160,32},{192,320},{2... | collective-permute-start | bytes 393224 | tf_op jit(solution)/shard_map/ppermute | solution.py:275
  79.6 1.9 %collective-permute-start.7 = (bf16[1024,256]{1,0:T(8,128)(2,1)S(1)}, bf16[1024,256]{1,0:T(8,128)(2,1)S(1)}, u32[]{:S(2)}, u32[]{:S(2)}) collective-permute-start(bf16[1024,256]{1,0:T(8,128)(2,1)S(1)} %collective-permute-done.6.refs_1_.refs_6_.refs_4_), channel_id=1, source_target_pairs={{0,64},{32,480},{64,128},{96,32},{128,192},{160,96},{192,256},{224... | collective-permute-start | bytes 1572872 | tf_op jit(solution)/shard_map/ppermute | solution.py:275
  81.5 4.1 %ring.2 = (f32[768,384]{1,0:T(8,128)S(1)}, f32[768,384]{1,0:T(8,128)S(1)}) custom-call(s32[2,9]{1,0:T(2,128)S(1)} %copy-done.1, bf16[768,128]{1,0:T(8,128)(2,1)S(1)} %bitcast.17, bf16[768,128]{1,0:T(8,128)(2,1)S(1)} %collective-permute-done.other_q_ref.q_ref, bf16[1024,256]{1,0:T(8,128)(2,1)S(1)} %collective-permute-done.2.refs_0_.refs_3_.refs_1_, ...), custom_call_target="tpu_custom_call" | custom-call | flops 4000000000 | bytes 1 | tf_op jit(solution)/shard_map/ring/pallas_call | solution.py:194
  85.7 4.3 %ring.3 = (f32[768,384]{1,0:T(8,128)S(1)}, f32[768,384]{1,0:T(8,128)S(1)}) custom-call(s32[2,9]{1,0:T(2,128)S(1)} %copy-done.1, bf16[768,128]{1,0:T(8,128)(2,1)S(1)} %bitcast.18, bf16[768,128]{1,0:T(8,128)(2,1)S(1)} %collective-permute-done.other_q_ref.q_ref, bf16[1024,256]{1,0:T(8,128)(2,1)S(1)} %collective-permute-done.3.refs_0_.refs_5_.refs_3_, ...), custom_call_target="tpu_custom_call" | custom-call | flops 4000000000 | bytes 1 | tf_op jit(solution)/shard_map/ring/pallas_call | solution.py:194
  90.0 0.6 end.4.refs_1_
  90.7 0.9 end.5
  91.6 6.1 %collective-permute-start.9 = (f32[1024,256]{1,0:T(8,128)S(1)}, f32[1024,256]{1,0:T(8,128)S(1)}, u32[]{:S(2)}, u32[]{:S(2)}) collective-permute-start(f32[1024,256]{1,0:T(8,128)S(1)} %end.5), channel_id=1, source_target_pairs={{0,32},{32,0},{64,96},{96,64},{128,160},{160,128},{192,224},{224,1... | collective-permute-start | bytes 3145736 | tf_op jit(solution)/shard_map/ppermute | solution.py:264
  97.7 1.8 %end.3.mine_ref = f32[768,256]{1,0:T(8,128)S(1)} custom-call(s32[2,9]{1,0:T(2,128)S(1)} %copy-done.1, s32[2]{0:T(128)S(1)} %copy-done, bf16[768,128]{1,0:T(8,128)(2,1)S(1)} %bitcast.19, bf16[1024,256]{1,0:T(8,128)(2,1)S(1)} %collective-permute-done.4.refs_0_.kv_ref.refs_7_.refs_5_, ...), custom_call_target="tpu_custom_call" | custom-call | flops 1000000000 | bytes 1 | tf_op jit(solution)/shard_map/end/pallas_call | solution.py:194
  99.5 0.5 collective-permute-done.9.other_ref
  99.9 2.4 %merge.1 = (bf16[768,128]{1,0:T(8,128)(2,1)}, bf16[512,128]{1,0:T(8,128)(2,1)}) custom-call(s32[2]{0:T(128)S(1)} %copy-done, f32[768,256]{1,0:T(8,128)S(1)} %end.3.mine_ref, f32[1024,256]{1,0:T(8,128)S(1)} %collective-permute-done.9.other_ref, bf16[1024,256]{1,0:T(8,128)(2,1)S(1)} %load.1.kv_ref.refs_2_.refs_0_, ...), custom_call_target="tpu_custom_call" | custom-call | flops 1000000000 | bytes 1 | tf_op jit(solution)/shard_map/merge/pallas_call | solution.py:194
  (26 shorter events, 0.1 us)
Async XLA Ops:
  0.6 15.3 %copy-start.6 = (bf16[1,24,512]{2,1,0:T(8,128)(2,1)S(1)}, bf16[1,24,512]{2,1,0:T(8,128)(2,1)}, u32[]{:S(2)}) copy-start(bf16[1,24,512]{2,1,0:T(8,128)(2,1)} %param.11) | copy-start | bytes 73732
  0.6 15.3 %copy-start.5 = (bf16[1,24,512]{2,1,0:T(8,128)(2,1)S(1)}, bf16[1,24,512]{2,1,0:T(8,128)(2,1)}, u32[]{:S(2)}) copy-start(bf16[1,24,512]{2,1,0:T(8,128)(2,1)} %param.10) | copy-start | bytes 73732
  0.7 12.4 %copy-start.2 = (bf16[1,768,128]{2,1,0:T(8,128)(2,1)S(1)}, bf16[1,768,128]{2,1,0:T(8,128)(2,1)}, u32[]{:S(2)}) copy-start(bf16[1,768,128]{2,1,0:T(8,128)(2,1)} %param.9) | copy-start | bytes 589828
  0.7 25.9 %copy-start.8 = (s32[16,8]{0,1:T(8,128)S(1)}, s32[16,8]{0,1:T(8,128)}, u32[]{:S(2)}) copy-start(s32[16,8]{0,1:T(8,128)} %param.16) | copy-start | bytes 1540
  2.4 27.1 %copy-start.3 = (bf16[1,512,128]{2,1,0:T(8,128)(2,1)S(1)}, bf16[1,512,128]{2,1,0:T(8,128)(2,1)}, u32[]{:S(2)}) copy-start(bf16[1,512,128]{2,1,0:T(8,128)(2,1)} %param.13) | copy-start | bytes 393220
  2.4 27.0 %all-to-all-start = ((bf16[32,40,256]{2,1,0:T(8,128)(2,1)}), bf16[32,40,256]{2,1,0:T(8,128)(2,1)S(1)}, u32[]{:S(2)}, u32[]{:S(2)}) async-start(bf16[32,40,256]{2,1,0:T(8,128)(2,1)} %heads.1), calls=%async_computation | async-start | bytes 1310720 | tf_op jit(solution)/shard_map/all_to_all | solution.py:260
  13.0 16.5 %collective-permute-start = (bf16[768,128]{1,0:T(8,128)(2,1)S(1)}, bf16[768,128]{1,0:T(8,128)(2,1)S(1)}, u32[]{:S(2)}, u32[]{:S(2)}) collective-permute-start(bf16[768,128]{1,0:T(8,128)(2,1)S(1)} %bitcast.15), channel_id=1, source_target_pairs={{0,32},{32,0},{64,96},{96,64},{128,160},{160,128},{192,224},{224,1... | collective-permute-start | bytes 589832 | tf_op jit(solution)/shard_map/ppermute | solution.py:264
  16.0 13.5 %collective-permute-start.1 = (bf16[24,1024]{1,0:T(8,128)(2,1)S(1)}, bf16[24,1024]{1,0:T(8,128)(2,1)S(1)}, u32[]{:S(2)}, u32[]{:S(2)}) collective-permute-start(bf16[24,1024]{1,0:T(8,128)(2,1)S(1)} %pad_maximum_fusion), channel_id=1, source_target_pairs={{0,256},{32,288},{64,320},{96,352},{128,384},{160,416},{192,448},{... | collective-permute-start | bytes 147464 | tf_op jit(solution)/shard_map/ppermute | solution.py:269
  28.7 0.8 copy-start.4
  29.5 1.4 %copy-start.7 = (bf16[24,1024]{1,0:T(8,128)(2,1)}, bf16[24,1024]{1,0:T(8,128)(2,1)S(1)}, u32[]{:S(2)}) copy-start(bf16[24,1024]{1,0:T(8,128)(2,1)S(1)} %collective-permute-done.1.both) | copy-start | bytes 147460
  30.9 34.2 %copy-start.1 = (s32[2,9]{1,0:T(2,128)S(1)}, s32[2,9]{1,0:T(2,128)}, u32[]{:S(2)}) copy-start(s32[2,9]{1,0:T(2,128)} %get-tuple-element.23.seen_ref) | copy-start | bytes 220
  30.9 22.6 %collective-permute-start.2 = (bf16[1024,256]{1,0:T(8,128)(2,1)S(1)}, bf16[1024,256]{1,0:T(8,128)(2,1)S(1)}, u32[]{:S(2)}, u32[]{:S(2)}) collective-permute-start(bf16[1024,256]{1,0:T(8,128)(2,1)S(1)} %load.1.kv_ref.refs_2_.refs_0_), channel_id=1, source_target_pairs={{0,64},{32,480},{64,128},{96,32},{128,192},{160,96},{192,256},{224... | collective-permute-start | bytes 1572872 | tf_op jit(solution)/shard_map/ppermute | solution.py:275
  41.6 14.1 %collective-permute-start.5 = (bf16[1024,256]{1,0:T(8,128)(2,1)S(1)}, bf16[1024,256]{1,0:T(8,128)(2,1)S(1)}, u32[]{:S(2)}, u32[]{:S(2)}) collective-permute-start(bf16[1024,256]{1,0:T(8,128)(2,1)S(1)} %load.1.kv_ref.refs_2_.refs_0_), channel_id=1, source_target_pairs={{0,480},{32,64},{64,32},{96,128},{128,96},{160,192},{192,160},{224... | collective-permute-start | bytes 1572872 | tf_op jit(solution)/shard_map/ppermute | solution.py:275
  45.7 19.5 %all-to-all-start.1 = ((bf16[32,24,256]{2,1,0:T(8,128)(2,1)}), bf16[32,24,256]{2,1,0:T(8,128)(2,1)S(1)}, u32[]{:S(2)}, u32[]{:S(2)}) async-start(bf16[32,24,256]{2,1,0:T(8,128)(2,1)} %far_heads.1), calls=%async_computation.1 | async-start | bytes 786432 | tf_op jit(solution)/shard_map/all_to_all | solution.py:260
  53.5 15.7 %collective-permute-start.3 = (bf16[1024,256]{1,0:T(8,128)(2,1)S(1)}, bf16[1024,256]{1,0:T(8,128)(2,1)S(1)}, u32[]{:S(2)}, u32[]{:S(2)}) collective-permute-start(bf16[1024,256]{1,0:T(8,128)(2,1)S(1)} %collective-permute-done.2.refs_0_.refs_3_.refs_1_), channel_id=1, source_target_pairs={{0,64},{32,480},{64,128},{96,32},{128,192},{160,96},{192,256},{224... | collective-permute-start | bytes 1572872 | tf_op jit(solution)/shard_map/ppermute | solution.py:275
  55.7 15.5 %collective-permute-start.6 = (bf16[1024,256]{1,0:T(8,128)(2,1)S(1)}, bf16[1024,256]{1,0:T(8,128)(2,1)S(1)}, u32[]{:S(2)}, u32[]{:S(2)}) collective-permute-start(bf16[1024,256]{1,0:T(8,128)(2,1)S(1)} %collective-permute-done.5.refs_1_.refs_4_.refs_2_), channel_id=1, source_target_pairs={{0,64},{32,480},{64,128},{96,32},{128,192},{160,96},{192,256},{224... | collective-permute-start | bytes 1572872 | tf_op jit(solution)/shard_map/ppermute | solution.py:275
  69.3 20.7 %collective-permute-start.4 = (bf16[1024,256]{1,0:T(8,128)(2,1)S(1)}, bf16[1024,256]{1,0:T(8,128)(2,1)S(1)}, u32[]{:S(2)}, u32[]{:S(2)}) collective-permute-start(bf16[1024,256]{1,0:T(8,128)(2,1)S(1)} %collective-permute-done.3.refs_0_.refs_5_.refs_3_), channel_id=1, source_target_pairs={{0,64},{32,480},{64,128},{96,32},{128,192},{160,96},{192,256},{224... | collective-permute-start | bytes 1572872 | tf_op jit(solution)/shard_map/ppermute | solution.py:275
  71.2 19.4 %collective-permute-start.8 = (bf16[256,256]{1,0:T(8,128)(2,1)S(1)}, bf16[256,256]{1,0:T(8,128)(2,1)S(1)}, u32[]{:S(2)}, u32[]{:S(2)}) collective-permute-start(bf16[256,256]{1,0:T(8,128)(2,1)S(1)} %slice.11), channel_id=1, source_target_pairs={{0,128},{32,416},{64,192},{96,480},{128,256},{160,32},{192,320},{2... | collective-permute-start | bytes 393224 | tf_op jit(solution)/shard_map/ppermute | solution.py:275
  79.6 11.0 %collective-permute-start.7 = (bf16[1024,256]{1,0:T(8,128)(2,1)S(1)}, bf16[1024,256]{1,0:T(8,128)(2,1)S(1)}, u32[]{:S(2)}, u32[]{:S(2)}) collective-permute-start(bf16[1024,256]{1,0:T(8,128)(2,1)S(1)} %collective-permute-done.6.refs_1_.refs_6_.refs_4_), channel_id=1, source_target_pairs={{0,64},{32,480},{64,128},{96,32},{128,192},{160,96},{192,256},{224... | collective-permute-start | bytes 1572872 | tf_op jit(solution)/shard_map/ppermute | solution.py:275
  90.0 0.7 copy-start
  91.6 8.3 %collective-permute-start.9 = (f32[1024,256]{1,0:T(8,128)S(1)}, f32[1024,256]{1,0:T(8,128)S(1)}, u32[]{:S(2)}, u32[]{:S(2)}) collective-permute-start(f32[1024,256]{1,0:T(8,128)S(1)} %end.5), channel_id=1, source_target_pairs={{0,32},{32,0},{64,96},{96,64},{128,160},{160,128},{192,224},{224,1... | collective-permute-start | bytes 3145736 | tf_op jit(solution)/shard_map/ppermute | solution.py:264
